TPU v7x, 512 devices: a whole 4x8x8 slice. The times are simulated.
512 devices in a mesh: grp: 8 (over z_lo, core), blk: 8 (over y), set: 8 (over z_hi, x).
Axes of the slice: x: 4, y: 8, z: 8 (z_hi: 2, z_lo: 4; z = z_hi * 4 + z_lo), core: 2. Of those that a mesh axis runs over, the one named last changes fastest.
Arguments:
- queries: bfloat16 [65536, 384], P(('grp', 'blk', 'set')), may hold values from -8 to 8
- keys: bfloat16 [65536, 384], P(('grp', 'blk', 'set')), may hold values from -8 to 8
- values: bfloat16 [65536, 384], P(('grp', 'blk', 'set')), may hold values from -6 to 6
- valid: int32 [65536], P(('grp', 'blk', 'set')), may hold values 0 or 1
- offsets: int32 [2, 6], replicated, may hold values from 0 to 63, as said below
- w_out: bfloat16 [384, 768], replicated, may hold values from -0.3125 to 0.3125
Outputs:
- projected: bfloat16 [65536, 768], P(('grp', 'blk', 'set'))
Inputs may be any that keep to these rules, and one draw needn't show every extreme that they name: offsets[0, h] lies in 0 to 7 and offsets[1, h] - offsets[0, h] is a multiple of 8 for every head h.
All inputs are finite; a program needn't handle non-finite values. No bound on the sum of `valid` on one device may be relied on, other than what follows from the above.
Results may differ from a plain program's by a relative error of at most 0.0015.
The roundings to bfloat16 on the way count: a program that leaves them out, or rounds other values in their place, can miss the bound.
Values may be sent and summed in bfloat16 or wider, within the bound.
No kernel may reach another device: no remote copies, remote signals or barrier semaphores. Data moves between devices by JAX's collectives and lax.ppermute only.
A program may use at most 64 MiB of HBM per device.

v0:
```python
import math

import jax
import jax.numpy as jnp
from jax import lax
from jax.sharding import PartitionSpec as P

HEAD_COUNT = 6
HD = 64


def in_one_piece(arrays, axis, dim, along):
    columns = [a.reshape(*a.shape[:along], -1) for a in arrays]
    both = jnp.concatenate(columns, axis=along)
    whole, at, done = (lax.all_gather(both, axis, axis=dim, tiled=True), 0, [])
    for a, column in zip(arrays, columns):
        piece = whole[..., at : at + column.shape[along]]
        done.append(piece.reshape(*piece.shape[:along], *a.shape[along:]))
        at += column.shape[along]
    return tuple(done)


def side_by_side(arrays, axis, dim, along):
    ends, at = ([], 0)
    for a in arrays[:-1]:
        at += a.shape[along]
        ends.append(at)
    both = jnp.concatenate(arrays, axis=along)
    return tuple(jnp.split(lax.all_gather(both, axis, axis=dim, tiled=True), ends, axis=along))


def head_attend(query_head, key_head, value_head, key_allowed, self_slot, scaling):
    scores = (
        lax.dot_general(
            query_head, key_head, (((1,), (1,)), ((), ())), preferred_element_type=jnp.float32
        )
        * scaling
    )
    columns = jnp.arange(key_head.shape[0], dtype=jnp.int32)
    allowed = key_allowed[None, :] | (columns[None, :] == self_slot[:, None])
    scores = jnp.where(allowed, scores, jnp.float32(-1e30))
    highest = jnp.max(scores, axis=1, keepdims=True)
    weights = jnp.exp(scores - highest)
    totals = jnp.sum(weights, axis=1)
    mixture = (
        jnp.dot(weights.astype(jnp.bfloat16), value_head, preferred_element_type=jnp.float32)
        / totals[:, None]
    )
    return (mixture, highest[:, 0] + jnp.log(totals))


def attend(queries, keys, values, key_allowed, self_slot):
    row_count = queries.shape[0]
    length = keys.shape[0]
    heads_query = queries.reshape(row_count, HEAD_COUNT, HD).transpose(1, 0, 2)
    heads_key = keys.reshape(length, HEAD_COUNT, HD).transpose(1, 0, 2)
    heads_value = values.reshape(length, HEAD_COUNT, HD).transpose(1, 0, 2)
    scaling = 1.0 / math.sqrt(HD)
    mixture, log_totals = lax.map(
        lambda packed: head_attend(packed[0], packed[1], packed[2], packed[3], self_slot, scaling),
        (heads_query, heads_key, heads_value, key_allowed.T),
    )
    return (mixture.transpose(1, 0, 2).reshape(row_count, HEAD_COUNT * HD), log_totals.T)


def selector_table(shift_amount, cycle_length):
    return jnp.arange(cycle_length, dtype=jnp.int32)[:, None] == shift_amount[None, :]


def pick_rows(matrix, shift_amount, cycle_length):
    row_total = matrix.shape[0]
    selector = selector_table(shift_amount, cycle_length)
    blocks = matrix.reshape(row_total // cycle_length, cycle_length, HEAD_COUNT, HD)
    chosen = jnp.sum(
        jnp.where(selector[None, :, :, None], blocks, jnp.zeros((), matrix.dtype)), axis=1
    )
    return chosen.reshape(row_total // cycle_length, HEAD_COUNT * HD)


def pick_flags(key_flags, shift_amount, cycle_length):
    row_total = key_flags.shape[0]
    selector = selector_table(shift_amount, cycle_length)
    blocks = key_flags.reshape(row_total // cycle_length, cycle_length)
    return jnp.sum(
        jnp.where(selector[None, :, :], blocks[:, :, None], jnp.zeros((), key_flags.dtype)), axis=1
    )


def pick_head_flags(head_flags, shift_amount, cycle_length):
    row_total = head_flags.shape[0]
    selector = selector_table(shift_amount, cycle_length)
    blocks = head_flags.reshape(row_total // cycle_length, cycle_length, HEAD_COUNT)
    return jnp.sum(jnp.where(selector[None, :, :], blocks, jnp.zeros((), head_flags.dtype)), axis=1)


def spread_back(mixture, log_totals, shift_amount, cycle_length):
    row_count = mixture.shape[0]
    selector = selector_table(shift_amount, cycle_length)
    wide = jnp.where(
        selector[None, :, :, None], mixture.reshape(row_count, 1, HEAD_COUNT, HD), jnp.float32(0.0)
    )
    spread_totals = jnp.where(selector[None, :, :], log_totals[:, None, :], jnp.float32(0.0))
    present = jnp.broadcast_to(selector[None, :, :], (row_count, cycle_length, HEAD_COUNT))
    return (
        wide.reshape(row_count * cycle_length, HEAD_COUNT * HD),
        spread_totals.reshape(row_count * cycle_length, HEAD_COUNT),
        present.reshape(row_count * cycle_length, HEAD_COUNT),
    )


def combine(levels):
    highest = levels[0][1]
    for entry in levels[1:]:
        highest = jnp.maximum(highest, jnp.where(entry[2], entry[1], highest))
    numerator = jnp.zeros(levels[0][0].shape, jnp.float32)
    denominator = jnp.zeros(levels[0][1].shape, jnp.float32)
    for entry in levels:
        scaled = jnp.where(entry[2], jnp.exp(entry[1] - highest), jnp.float32(0.0))
        expanded = jnp.broadcast_to(scaled[:, :, None], (scaled.shape[0], HEAD_COUNT, HD)).reshape(
            scaled.shape[0], HEAD_COUNT * HD
        )
        numerator = numerator + entry[0] * expanded
        denominator = denominator + scaled
    wide_denominator = jnp.broadcast_to(
        denominator[:, :, None], (denominator.shape[0], HEAD_COUNT, HD)
    ).reshape(denominator.shape[0], HEAD_COUNT * HD)
    return numerator / wide_denominator


def per_device(queries, keys, values, valid, offsets, w_out):
    row_count = queries.shape[0]
    inner_size = lax.axis_size("set")
    block_size = lax.axis_size("blk")
    group_size = lax.axis_size("grp")
    inner_index = lax.axis_index("set")
    block_index = lax.axis_index("blk")
    group_index = lax.axis_index("grp")
    outer_period = block_size * group_size
    key_flags = valid.astype(jnp.bfloat16)
    dense_keys, dense_values, dense_flags = in_one_piece((keys, values, key_flags), "set", 0, 1)
    segment_rows = dense_keys.shape[0]
    dense_allowed = jnp.broadcast_to((dense_flags > 0)[:, None], (segment_rows, HEAD_COUNT))
    own_slots = inner_index * row_count + jnp.arange(row_count, dtype=jnp.int32)
    dense_level = attend(queries, dense_keys, dense_values, dense_allowed, own_slots)
    middle_shift = offsets[0]
    outer_shift = offsets[1]
    middle_key_part = pick_rows(dense_keys, middle_shift, block_size)
    middle_value_part = pick_rows(dense_values, middle_shift, block_size)
    middle_flag_part = pick_flags(dense_flags, middle_shift, block_size)
    middle_keys, middle_values, middle_flags = side_by_side(
        (middle_key_part, middle_value_part, middle_flag_part), "blk", 0, 1
    )
    stride_offset = (outer_shift - middle_shift) // block_size
    outer_key_part = pick_rows(middle_keys, stride_offset, group_size)
    outer_value_part = pick_rows(middle_values, stride_offset, group_size)
    outer_flag_part = pick_head_flags(middle_flags, stride_offset, group_size)
    outer_keys, outer_values, outer_flags = side_by_side(
        (outer_key_part, outer_value_part, outer_flag_part), "grp", 0, 1
    )
    middle_count = row_count // block_size
    middle_slots = (block_index * inner_size + inner_index) * middle_count + jnp.arange(
        middle_count, dtype=jnp.int32
    )
    middle_level = attend(
        pick_rows(queries, middle_shift, block_size),
        middle_keys,
        middle_values,
        middle_flags > 0,
        middle_slots,
    )
    outer_count = row_count // outer_period
    outer_slots = (
        (group_index * block_size + block_index) * inner_size + inner_index
    ) * outer_count + jnp.arange(outer_count, dtype=jnp.int32)
    outer_level = attend(
        pick_rows(queries, outer_shift, outer_period),
        outer_keys,
        outer_values,
        outer_flags > 0,
        outer_slots,
    )
    levels = [
        (dense_level[0], dense_level[1], jnp.ones((row_count, HEAD_COUNT), jnp.bool_)),
        spread_back(middle_level[0], middle_level[1], middle_shift, block_size),
        spread_back(outer_level[0], outer_level[1], outer_shift, outer_period),
    ]
    attention = combine(levels).astype(jnp.bfloat16)
    return jnp.dot(attention, w_out, preferred_element_type=jnp.float32).astype(jnp.bfloat16)


def solution(mesh):
    in_specs = (
        P(("grp", "blk", "set"), None),
        P(("grp", "blk", "set"), None),
        P(("grp", "blk", "set"), None),
        P(("grp", "blk", "set")),
        P(),
        P(),
    )
    out_specs = P(("grp", "blk", "set"), None)
    return jax.shard_map(
        per_device, mesh=mesh, in_specs=in_specs, out_specs=out_specs, check_vma=False
    )
```

profile of v0, /device:TPU:1, one launch (start us, length us, event | category | flops | bytes accessed | tf_op | source)
XLA Modules:
  0.0 228.2 jit_solution(6456099407341516714)
XLA Ops:
  15.5 74.3 %all-gather.4.cloned.1.call-done = bf16[1024,769]{0,1:T(8,128)(2,1)} async-done(((bf16[128,769]{0,1:T(8,128)(2,1)}), bf16[1024,769]{0,1:T(8,128)(2,1)}) %all-gather.4.cloned.1.call-update) | async-done | bytes 1574928 | tf_op jit(solution)/shard_map/all_gather | solution.py:15
  91.4 1.5 fusion.64
  95.3 2.7 %reshape.300 = bf16[128,8,6,64]{3,2,1,0:T(8,128)(2,1)S(1)} reshape(bf16[1024,384]{1,0:T(8,128)(2,1)} %copy.98) | data formatting | bytes 1572864 | tf_op jit(solution)/shard_map/reshape | solution.py:73
  98.0 3.8 %reshape.302 = bf16[128,8,6,64]{3,2,1,0:T(8,128)(2,1)} reshape(bf16[1024,384]{1,0:T(8,128)(2,1)} %copy.100) | data formatting | bytes 1572864 | tf_op jit(solution)/shard_map/reshape | solution.py:73
  101.7 4.5 %select_reduce_fusion.3 = (bf16[128,6,64]{2,1,0:T(8,128)(2,1)}, bf16[128,6,64]{2,1,0:T(8,128)(2,1)}) fusion(bf16[128,8,6,64]{3,2,1,0:T(8,128)(2,1)S(1)} %reshape.300, pred[8,6]{1,0:T(8,128)(4,1)S(1)} %iota_compare_fusion.4, bf16[128,8,6,64]{3,2,1,0:T(8,128)(2,1)} %reshape.302), kind=kLoop, calls=%fused_computation.69 | loop fusion | flops 1474560 | bytes 1769520 | tf_op jit(solution)/shard_map/reduce_sum | solution.py:74
  108.4 1.4 pad_maximum_fusion.1
  110.8 22.4 %while.39 = (s32[]{:T(128)}, f32[6,128,64]{1,2,0:T(8,128)}, f32[6,128]{1,0:T(8,128)}, pred[6,1024]{1,0:T(8,128)(4,1)S(1)}, bf16[6,128,64]{1,2,0:T(8,128)(2,1)}, ...) while((s32[]{:T(128)}, f32[6,128,64]{1,2,0:T(8,128)}, ...), condition=%wide.region_3.4_spmd.clone, body=%wide.region_0.3_spmd.clone.sunk | while | flops 34742272 | bytes 1895545 | solution.py:59
  110.8 1.3 fusion.84
  113.3 1.3 dynamic_update_slice.40
  114.6 1.3 fusion.84
  117.0 1.3 dynamic_update_slice.40
  118.3 1.3 fusion.84
  120.7 1.3 dynamic_update_slice.40
  122.0 1.3 fusion.84
  124.4 1.3 dynamic_update_slice.40
  125.7 1.3 fusion.84
  128.2 1.3 dynamic_update_slice.40
  129.5 1.3 fusion.84
  131.9 1.3 dynamic_update_slice.40
  133.2 16.5 %all-gather.6.cloned.1.call-done = bf16[1024,774]{0,1:T(8,128)(2,1)} async-done(((bf16[128,774]{0,1:T(8,128)(2,1)}), bf16[1024,774]{0,1:T(8,128)(2,1)}) %all-gather.6.cloned.1.call-update) | async-done | bytes 1585168 | tf_op jit(solution)/shard_map/all_gather | solution.py:29
  151.3 1.5 fusion.63
  155.1 2.7 %reshape.308 = bf16[128,8,6,64]{3,2,1,0:T(8,128)(2,1)S(1)} reshape(bf16[1024,384]{1,0:T(8,128)(2,1)} %copy.106) | data formatting | bytes 1572864 | tf_op jit(solution)/shard_map/reshape | solution.py:73
  157.8 3.8 %reshape.310 = bf16[128,8,6,64]{3,2,1,0:T(8,128)(2,1)} reshape(bf16[1024,384]{1,0:T(8,128)(2,1)} %copy.108) | data formatting | bytes 1572864 | tf_op jit(solution)/shard_map/reshape | solution.py:73
  161.6 4.5 %select_reduce_fusion.1 = (bf16[128,6,64]{2,1,0:T(8,128)(2,1)}, bf16[128,6,64]{2,1,0:T(8,128)(2,1)}) fusion(bf16[128,8,6,64]{3,2,1,0:T(8,128)(2,1)S(1)} %reshape.308, pred[8,6]{1,0:T(8,128)(4,1)} %copy-done.9, bf16[128,8,6,64]{3,2,1,0:T(8,128)(2,1)} %reshape.310), kind=kLoop, calls=%fused_computation.67 | loop fusion | flops 1474560 | bytes 1769520 | tf_op jit(solution)/shard_map/reduce_sum | solution.py:74
  170.2 1.5 copy.103
  173.3 10.7 %while.40 = (s32[]{:T(128)}, f32[6,16,64]{2,1,0:T(8,128)S(1)}, f32[6,16]{1,0:T(8,128)S(1)}, pred[6,1024]{1,0:T(8,128)(4,1)S(1)}, bf16[6,16,64]{2,1,0:T(8,128)(2,...) while((s32[]{:T(128)}, f32[6,16,64]{2,1,0:T(8,128)S(1)}, ...), condition=%wide.region_11.12_spmd.clone, body=%wide.region_8.11_spmd.clone.sunk | while | flops 4342786 | bytes 740537 | solution.py:59
  175.2 1.3 fusion.89
  176.9 1.3 fusion.89
  178.7 1.3 fusion.89
  184.6 28.0 %all-gather.8.cloned.1.call-done = bf16[1024,774]{0,1:T(8,128)(2,1)} async-done(((bf16[128,774]{0,1:T(8,128)(2,1)}), bf16[1024,774]{0,1:T(8,128)(2,1)}) %all-gather.8.cloned.1.call-update) | async-done | bytes 1585168 | tf_op jit(solution)/shard_map/all_gather | solution.py:29
  213.3 1.5 fusion.62
  214.9 4.6 %while.41 = (s32[]{:T(128)}, f32[6,2,64]{2,1,0:T(2,128)S(1)}, f32[6,2]{1,0:T(8,128)S(1)}, pred[6,1024]{1,0:T(8,128)(4,1)S(1)}, bf16[6,2,64]{2,1,0:T(2,128)(2,1)S...) while((s32[]{:T(128)}, f32[6,2,64]{2,1,0:T(2,128)S(1)}, ...), condition=%wide.region_19.20_spmd.clone, body=%wide.region_16.19_spmd.clone.sunk | while | flops 542850 | bytes 295105 | solution.py:59
  (211 shorter events, 47.1 us)
Async XLA Ops:
  6.5 214.2 %copy-start = (bf16[384,768]{1,0:T(8,128)(2,1)S(1)}, bf16[384,768]{1,0:T(8,128)(2,1)}, u32[]{:S(2)}) copy-start(bf16[384,768]{1,0:T(8,128)(2,1)} %param.17) | copy-start | bytes 1769476
  6.5 5.8 %copy-start.15 = (s32[2,6]{1,0:T(2,128)S(1)}, s32[2,6]{1,0:T(2,128)}, u32[]{:S(2)}) copy-start(s32[2,6]{1,0:T(2,128)} %param.16) | copy-start | bytes 148
  6.5 83.3 %all-gather.4.cloned.1.call-start = ((), (), s32[]{:S(2)}) async-start(), calls=%async_computation | async-start | bytes 1787904 | tf_op jit(solution)/shard_map/all_gather | solution.py:15
  10.0 139.7 %all-gather.6.cloned.1.call-start = ((), (), s32[]{:S(2)}) async-start(), calls=%async_computation.1 | async-start | bytes 1787904 | tf_op jit(solution)/shard_map/all_gather | solution.py:29
  11.1 79.5 %copy-start.4 = (bf16[128,384]{0,1:T(8,128)(2,1)}, bf16[128,384]{0,1:T(8,128)(2,1)S(1)}, u32[]{:S(2)}) copy-start(bf16[128,384]{0,1:T(8,128)(2,1)S(1)} %copy.93) | copy-start | bytes 294916
  12.4 2.1 copy-start.9
  13.2 77.5 %copy-start.6 = (pred[64,6]{0,1:T(8,128)(4,1)}, pred[64,6]{0,1:T(8,128)(4,1)S(1)}, u32[]{:S(2)}) copy-start(pred[64,6]{0,1:T(8,128)(4,1)S(1)} %iota_compare_fusion.3) | copy-start | bytes 1156
  92.9 1.2 copy-start.3
  109.8 102.8 %all-gather.8.cloned.1.call-start = ((), (), s32[]{:S(2)}) async-start(), calls=%async_computation.2 | async-start | bytes 1787904 | tf_op jit(solution)/shard_map/all_gather | solution.py:29
  152.8 1.2 copy-start.1
  166.1 4.1 %copy-start.2 = (bf16[1024,384]{0,1:T(8,128)(2,1)S(1)}, bf16[1024,384]{0,1:T(8,128)(2,1)}, u32[]{:S(2)}) copy-start(bf16[1024,384]{0,1:T(8,128)(2,1)} %copy-done.1) | copy-start | bytes 2359300
  171.7 1.6 copy-start.14
  184.6 30.3 %copy-start.8 = (f32[6,2,64]{2,1,0:T(2,128)S(1)}, f32[6,2,64]{2,1,0:T(2,128)}, u32[]{:S(2)}) copy-start(f32[6,2,64]{2,1,0:T(2,128)} %custom-call.4) | copy-start | bytes 9220
  184.6 30.3 %copy-start.11 = (f32[6,2]{1,0:T(8,128)S(1)}, f32[6,2]{1,0:T(8,128)}, u32[]{:S(2)}) copy-start(f32[6,2]{1,0:T(8,128)} %custom-call.5) | copy-start | bytes 148
  214.8 5.0 %copy-start.7 = (pred[64,6]{0,1:T(8,128)(4,1)S(1)}, pred[64,6]{0,1:T(8,128)(4,1)}, u32[]{:S(2)}) copy-start(pred[64,6]{0,1:T(8,128)(4,1)} %copy-done.6) | copy-start | bytes 1156
  214.8 5.7 %copy-start.10 = (f32[6,128]{1,0:T(8,128)S(1)}, f32[6,128]{1,0:T(8,128)}, u32[]{:S(2)}) copy-start(f32[6,128]{1,0:T(8,128)} %get-tuple-element.135) | copy-start | bytes 9220
  214.9 5.7 %copy-start.12 = (pred[128,6]{0,1:T(8,128)(4,1)S(1)}, pred[128,6]{0,1:T(8,128)(4,1)}, u32[]{:S(2)}) copy-start(pred[128,6]{0,1:T(8,128)(4,1)} %reshape.307) | copy-start | bytes 2308
  214.9 5.7 %copy-start.13 = (pred[128,6]{0,1:T(8,128)(4,1)S(1)}, pred[128,6]{0,1:T(8,128)(4,1)}, u32[]{:S(2)}) copy-start(pred[128,6]{0,1:T(8,128)(4,1)} %reshape.299) | copy-start | bytes 2308
  214.9 5.7 %copy-start.5 = (f32[6,128,64]{1,2,0:T(8,128)S(1)}, f32[6,128,64]{1,2,0:T(8,128)}, u32[]{:S(2)}) copy-start(f32[6,128,64]{1,2,0:T(8,128)} %get-tuple-element.134) | copy-start | bytes 589828
Sparse Core Ops, SparseCore 0:
  10.4 79.3 all-gather.3
  109.9 39.7 all-gather.5
  170.3 42.2 all-gather.7
where the time goes:
time: 230 us; the launch traced here: 228 us
  waiting for transfers between devices  119 us (52%)
  local copies, waits for them, and re-layouts  47.5 us (21%)
  matrix products  25.7 us (11%)
  other arithmetic  22 us (10%)
  between operations  13.5 us (6%)
    all_gather x1, waiting for transfers between devices, in_one_piece(): whole, at, done = (lax.all_gather(both, axis, axis=dim, tiled=True), 0, [])  74.3 us
    all_gather x2, waiting for transfers between devices, side_by_side(): lax.all_gather(both, axis, axis=dim, tiled=True)  44.5 us
    dot_general x18, matrix products, head_attend(): lax.dot_general(query_head, key_head, (((1,), (1,)), ((), ())), preferred...  16.7 us
    reshape x6, local copies, waits for them, and re-layouts, pick_rows(): matrix.reshape(row_total // cycle_length, cycle_length, HEAD_COUNT, HD)  14.1 us
    reduce_sum x4, other arithmetic, pick_rows(): jnp.sum(jnp.where(selector[None, :, :, None], blocks, jnp.zeros((), matri...  9.69 us
    dynamic_update_slice x18, local copies, waits for them, and re-layouts, attend(): lax.map(lambda packed: head_attend(packed[0], packed[1], packed[2], packe...  8.03 us
    dot_general x18, matrix products, head_attend(): jnp.dot(weights.astype(jnp.bfloat16), value_head, preferred_element_type=...  8.01 us
    split x5, local copies, waits for them, and re-layouts, side_by_side(): jnp.split(lax.all_gather(both, axis, axis=dim, tiled=True), ends, axis=al...  6.01 us
  transfers between devices with their start and end apart: 3, of which 3 were waited for; matrix products, arithmetic and copies ran while one was open for 19% of the time, Pallas kernels for 0%

commit v1 on v0

v1 whole, which is shorter than its diff:
```python
import functools
import math

import jax
import jax.numpy as jnp
from jax import lax
from jax.experimental import pallas as pl
from jax.experimental.pallas import tpu as pltpu
from jax.sharding import PartitionSpec as P

HEADS = 6
HD = 64
PEERS = 8
ROWS = 128
FLAG_ROWS = 16
KEY_BLOCK = ROWS + FLAG_ROWS
FIRST_BLOCK = KEY_BLOCK + ROWS // 2
EXP_SCALE = math.log2(math.e) / math.sqrt(HD)
FAR = -1e30
F32 = jnp.float32
BF16 = jnp.bfloat16

VMEM = pl.BlockSpec(memory_space=pltpu.VMEM)
SMEM = pl.BlockSpec(memory_space=pltpu.SMEM)


def lanes(shape):
    return lax.broadcasted_iota(jnp.int32, shape, len(shape) - 1)


def rows(shape):
    return lax.broadcasted_iota(jnp.int32, shape, len(shape) - 2)


def my_head():
    return jnp.minimum(lax.axis_index("set"), HEADS - 1)


def shifts(offsets_ref):
    head = my_head()
    middle = offsets_ref[0, head]
    return middle, (offsets_ref[1, head] - middle) // 8


def scores(query, block_ref, index, self_mask):
    raw = lax.dot_general(
        query, block_ref[index, 0:ROWS, :], (((1,), (1,)), ((), ())), preferred_element_type=F32
    )
    flags = block_ref[index, ROWS:KEY_BLOCK, :].astype(F32)[0:1, :]
    bias = jnp.where(flags > 0.5, F32(0.0), F32(FAR))
    if self_mask is not None:
        bias = jnp.where(self_mask, F32(0.0), bias)
    return raw + bias


def level(query, block_ref, self_masks):
    parts = [scores(query, block_ref, c, self_masks[c]) for c in range(PEERS)]
    best = functools.reduce(jnp.maximum, parts)
    top = jnp.max(best, axis=1, keepdims=True)
    sums = None
    mixture = None
    for c in range(PEERS):
        weight = jnp.exp2((parts[c] - top) * F32(EXP_SCALE))
        sums = weight if sums is None else sums + weight
        add = jnp.dot(weight.astype(BF16), block_ref[c, 0:ROWS, :], preferred_element_type=F32)
        mixture = add if mixture is None else mixture + add
    total = jnp.sum(sums, axis=1, keepdims=True)
    lane = lanes(mixture.shape)
    return jnp.where(lane < 32, top, jnp.where(lane < 64, total, mixture))


def merge(one, two):
    top_one, top_two = one[:, 0:1], two[:, 0:1]
    top = jnp.maximum(top_one, top_two)
    scale_one = jnp.exp2((top_one - top) * F32(EXP_SCALE))
    scale_two = jnp.exp2((top_two - top) * F32(EXP_SCALE))
    both = one * scale_one + two * scale_two
    return jnp.where(lanes(both.shape) < 32, top, both)


def divided(state):
    return state / state[:, 32:33]


def pack_kernel(query_ref, key_ref, value_ref, valid_ref, out_ref):
    flags = jnp.broadcast_to(valid_ref[...].astype(F32), (FLAG_ROWS, ROWS)).astype(BF16)
    half = ROWS // 2
    for h in range(HEADS):
        at = slice(h * HD, (h + 1) * HD)
        out_ref[h, 0:ROWS, 0:HD] = key_ref[:, at]
        out_ref[h, 0:ROWS, HD : 2 * HD] = value_ref[:, at]
        out_ref[h, ROWS:KEY_BLOCK, :] = flags
        out_ref[h, KEY_BLOCK:FIRST_BLOCK, 0:HD] = query_ref[0:half, at]
        out_ref[h, KEY_BLOCK:FIRST_BLOCK, HD : 2 * HD] = query_ref[half:ROWS, at]
    for h in range(HEADS, PEERS):
        out_ref[h] = jnp.zeros((FIRST_BLOCK, 2 * HD), BF16)


def pick_kernel(which, offsets_ref, blocks_ref, out_ref, wide):
    shift = shifts(offsets_ref)[which]
    flag_rows = jnp.zeros((PEERS, ROWS), F32)
    for c in range(PEERS):
        wide[c * ROWS : (c + 1) * ROWS, :] = blocks_ref[c, 0:ROWS, :].astype(F32)
        flags = blocks_ref[c, ROWS:KEY_BLOCK, :].astype(F32)[0:PEERS, :]
        flag_rows = jnp.where(rows((PEERS, ROWS)) == c, flags, flag_rows)
    picked = wide[pl.ds(shift, ROWS, stride=8), :].astype(BF16)
    square = (ROWS, ROWS)
    selector = rows(square) == shift + 8 * (lanes(square) % 16)
    spread = jnp.dot(
        flag_rows.astype(BF16), selector.astype(F32).astype(BF16), preferred_element_type=F32
    )
    own = rows((PEERS, ROWS)) == lanes((PEERS, ROWS)) // 16
    flags = jnp.sum(jnp.where(own, spread, F32(0.0)), axis=0, keepdims=True)
    flags = jnp.broadcast_to(flags, (FLAG_ROWS, ROWS)).astype(BF16)
    for c in range(PEERS):
        out_ref[c, 0:ROWS, :] = picked
        out_ref[c, ROWS:KEY_BLOCK, :] = flags


def first_kernel(offsets_ref, blocks_ref, state_ref, middle_ref, outer_ref, wide, narrow):
    middle, stride = shifts(offsets_ref)
    half = ROWS // 2
    low = lanes((half, 2 * HD)) < HD
    diagonal = rows((ROWS, ROWS)) == lanes((ROWS, ROWS))
    for j in range(PEERS):
        pair = blocks_ref[j, KEY_BLOCK:FIRST_BLOCK, :].astype(F32)
        wide[j * ROWS : j * ROWS + half, :] = jnp.where(low, pair, F32(0.0))
        wide[j * ROWS + half : (j + 1) * ROWS, :] = jnp.where(
            low, pltpu.roll(pair, HD, 1), F32(0.0)
        )
        query = wide[j * ROWS : (j + 1) * ROWS, :].astype(BF16)
        masks = [diagonal if c == j else None for c in range(PEERS)]
        state_ref[j * ROWS : (j + 1) * ROWS, :] = level(query, blocks_ref, masks)
    picked = wide[pl.ds(middle, ROWS, stride=8), :]
    middle_ref[...] = picked.astype(BF16)
    narrow[...] = picked
    outer_ref[...] = narrow[pl.ds(stride, ROWS // 8, stride=8), :].astype(BF16)


def middle_kernel(offsets_ref, state_ref, query_ref, blocks_ref, out_ref, merged_ref, wide):
    middle, _ = shifts(offsets_ref)
    mine = lax.axis_index("blk")
    diagonal = rows((ROWS, ROWS)) == lanes((ROWS, ROWS))
    masks = [diagonal & (mine == c) for c in range(PEERS)]
    found = level(query_ref[...], blocks_ref, masks)
    both = merge(state_ref[pl.ds(middle, ROWS, stride=8), :], found)
    merged_ref[...] = both
    wide[...] = state_ref[...]
    wide[pl.ds(middle, ROWS, stride=8), :] = both
    half = ROWS // 2
    low = lanes((half, 2 * HD)) < HD
    for j in range(PEERS):
        one = divided(wide[j * ROWS : j * ROWS + half, :])
        two = divided(wide[j * ROWS + half : (j + 1) * ROWS, :])
        out_ref[j] = jnp.where(low, pltpu.roll(one, HD, 1), two).astype(BF16)


def outer_kernel(offsets_ref, merged_ref, query_ref, blocks_ref, before_ref, out_ref):
    middle, stride = shifts(offsets_ref)
    block, group = lax.axis_index("blk"), lax.axis_index("grp")
    count = ROWS // 8
    shape = (count, ROWS)
    diagonal = lanes(shape) == block * count + rows(shape)
    masks = [diagonal & (group == c) for c in range(PEERS)]
    found = level(query_ref[...], blocks_ref, masks)
    both = divided(merge(merged_ref[pl.ds(stride, count, stride=8), :], found))
    turned = pltpu.roll(both, HD, 1)
    half = ROWS // 2
    here = rows((half, 2 * HD)) == middle + 8 * stride
    low = lanes((1, 2 * HD)) < HD
    for j in range(PEERS):
        row = jnp.where(low, turned[2 * j : 2 * j + 1, :], both[2 * j + 1 : 2 * j + 2, :])
        out_ref[j] = jnp.where(here, row, before_ref[j].astype(F32)).astype(BF16)


def project_kernel(blocks_ref, weight_ref, out_ref):
    half = ROWS // 2
    for part in range(2):
        total = None
        for h in range(HEADS):
            add = jnp.dot(
                blocks_ref[h, :, part * HD : (part + 1) * HD],
                weight_ref[h * HD : (h + 1) * HD, :],
                preferred_element_type=F32,
            )
            total = add if total is None else total + add
        out_ref[part * half : (part + 1) * half, :] = total.astype(BF16)


def call(kernel, name, out_shape, in_specs, scratch=(), flops=0, moved=0):
    outs = jax.tree.map(lambda _: VMEM, out_shape)
    return pl.pallas_call(
        kernel,
        name=name,
        out_shape=out_shape,
        in_specs=in_specs,
        out_specs=outs,
        scratch_shapes=list(scratch),
        compiler_params=pltpu.CompilerParams(vmem_limit_bytes=40 * 2**20),
        cost_estimate=pl.CostEstimate(flops=flops, bytes_accessed=moved, transcendentals=0),
    )


def shaped(*shape, dtype=BF16):
    return jax.ShapeDtypeStruct(shape, dtype)


def per_device(queries, keys, values, valid, offsets, w_out):
    wide = pltpu.VMEM((PEERS * ROWS, 2 * HD), F32)
    narrow = pltpu.VMEM((ROWS, 2 * HD), F32)
    swap = functools.partial(lax.all_to_all, split_axis=0, concat_axis=0, tiled=True)

    packed = call(pack_kernel, "pack", shaped(PEERS, FIRST_BLOCK, 2 * HD), [VMEM] * 4)(
        queries, keys, values, valid.reshape(1, ROWS)
    )
    dense = swap(packed, "set")

    def pick(which, name, blocks):
        return call(
            functools.partial(pick_kernel, which),
            name,
            shaped(PEERS, KEY_BLOCK, 2 * HD),
            [SMEM, VMEM],
            [wide],
        )(offsets, blocks)

    middle_blocks = swap(pick(0, "pick_middle", dense), "blk")
    state, middle_query, outer_query = call(
        first_kernel,
        "first",
        (shaped(PEERS * ROWS, 2 * HD, dtype=F32), shaped(ROWS, 2 * HD), shaped(ROWS // 8, 2 * HD)),
        [SMEM, VMEM],
        [wide, narrow],
        flops=6_000_000_000,
        moved=2_000_000,
    )(offsets, dense)
    outer_blocks = swap(pick(1, "pick_outer", middle_blocks), "grp")
    before, merged = call(
        middle_kernel,
        "middle",
        (shaped(PEERS, ROWS // 2, 2 * HD), shaped(ROWS, 2 * HD, dtype=F32)),
        [SMEM, VMEM, VMEM, VMEM],
        [wide],
        flops=2_000_000_000,
        moved=2_000_000,
    )(offsets, state, middle_query, middle_blocks)
    combined = call(
        outer_kernel,
        "outer",
        shaped(PEERS, ROWS // 2, 2 * HD),
        [SMEM, VMEM, VMEM, VMEM, VMEM],
    )(offsets, merged, outer_query, outer_blocks, before)
    home = swap(combined, "set")
    return call(project_kernel, "project", shaped(ROWS, 768), [VMEM, VMEM])(home, w_out)


def solution(mesh):
    spread = P(("grp", "blk", "set"), None)
    return jax.shard_map(
        per_device,
        mesh=mesh,
        in_specs=(spread, spread, spread, P(("grp", "blk", "set")), P(), P()),
        out_specs=spread,
        check_vma=False,
    )
```

time: 230 us -> 84.2 us (0.37)
  waiting for transfers between devices: 119 us -> 3.35 us
  blocking collectives: 0 us -> 52.9 us
  local copies, waits for them, and re-layouts: 47.5 us -> 3.34 us
  matrix products: 25.7 us -> 0 us
  other arithmetic: 22 us -> 0 us
  between operations: 13.5 us -> 0.06 us
  starting transfers between devices: 0.27 us -> 13.2 us
  Pallas kernels: 0 us -> 11 us
    all_gather x3 -> x0, waiting for transfers between devices: 119 us -> none  [the longest x1 74.3 us: in_one_piece(): whole, at, done = (lax.all_gather(both, axis, axis=dim, tiled=True), 0, [])]
    all_to_all x0 -> x3, blocking collectives: none -> 52.9 us  [the longest x1 24.9 us: per_device(): dense = swap(packed, 'set')]
    dot_general x37 -> x0, matrix products: 25.7 us -> none  [the longest x18 16.7 us: head_attend(): lax.dot_general(query_head, key_head, (((1,), (1,)), ((), ())), preferred...]
    reshape x11 -> x0, local copies, waits for them, and re-layouts: 18.8 us -> none  [the longest x6 14.1 us: pick_rows(): matrix.reshape(row_total // cycle_length, cycle_length, HEAD_COUNT, HD)]
    reduce_sum x24 -> x0, other arithmetic: 15.3 us -> none  [the longest x4 9.69 us: pick_rows(): jnp.sum(jnp.where(selector[None, :, :, None], blocks, jnp.zeros((), matri...]
    all_to_all x0 -> x1, starting transfers between devices: none -> 13.2 us  [per_device(): outer_blocks = swap(pick(1, 'pick_outer', middle_blocks), 'grp')]
    pallas_call x0 -> x7, Pallas kernels: none -> 11 us  [the longest x1 4.35 us: per_device(): call(first_kernel, 'first', (shaped(PEERS * ROWS, 2 * HD, dtype=F32), sha...]
    dynamic_update_slice x18 -> x0, local copies, waits for them, and re-layouts: 8.03 us -> none  [attend(): lax.map(lambda packed: head_attend(packed[0], packed[1], packed[2], packe...]
  transfers between devices with their start and end apart: 3 -> 1, of which waited for: 3 -> 1; matrix products, arithmetic and copies ran while one was open for 19% -> 0% of each run, Pallas kernels for 0% -> 7%
where the time goes in v1:
time: 84.2 us; the launch traced here: 83.8 us
  blocking collectives  52.9 us (63%)
  starting transfers between devices  13.2 us (16%)
  Pallas kernels  11 us (13%)
  waiting for transfers between devices  3.35 us (4%)
  local copies, waits for them, and re-layouts  3.34 us (4%)
    all_to_all x1, blocking collectives, per_device(): dense = swap(packed, 'set')  24.9 us
    all_to_all x1, blocking collectives, per_device(): middle_blocks = swap(pick(0, 'pick_middle', dense), 'blk')  16.3 us
    all_to_all x1, starting transfers between devices, per_device(): outer_blocks = swap(pick(1, 'pick_outer', middle_blocks), 'grp')  13.2 us
    all_to_all x1, blocking collectives, per_device(): home = swap(combined, 'set')  11.7 us
    pallas_call x1, Pallas kernels, per_device(): call(first_kernel, 'first', (shaped(PEERS * ROWS, 2 * HD, dtype=F32), sha...  4.35 us
    all_to_all x1, waiting for transfers between devices, per_device(): outer_blocks = swap(pick(1, 'pick_outer', middle_blocks), 'grp')  3.35 us
    unnamed x12, local copies, waits for them, and re-layouts  3.34 us
    pallas_call x2, Pallas kernels, pick(): call(functools.partial(pick_kernel, which), name, shaped(PEERS, KEY_BLOCK...  2.16 us
  transfers between devices with their start and end apart: 1, of which 1 were waited for; matrix products, arithmetic and copies ran while one was open for 0% of the time, Pallas kernels for 7%

profile of v1, /device:TPU:1, one launch (start us, length us, event | category | flops | bytes accessed | tf_op | source)
XLA Modules:
  0.0 83.8 jit_solution(12165132165392378429)
XLA Ops:
  0.0 0.0 copy-start.5
  0.0 0.7 copy-done.5
  0.7 0.0 copy-start.1
  0.7 0.9 %copy-done.1 = bf16[128,384]{1,0:T(8,128)(2,1)S(1)} copy-done((bf16[128,384]{1,0:T(8,128)(2,1)S(1)}, bf16[128,384]{1,0:T(8,128)(2,1)}, u32[]{:S(2)}) %copy-start.1) | copy-done | bytes 98328
  1.5 0.0 copy-start.2
  1.6 0.9 %copy-done.2 = bf16[128,384]{1,0:T(8,128)(2,1)S(1)} copy-done((bf16[128,384]{1,0:T(8,128)(2,1)S(1)}, bf16[128,384]{1,0:T(8,128)(2,1)}, u32[]{:S(2)}) %copy-start.2) | copy-done | bytes 98328
  2.4 0.0 copy-start.3
  2.4 0.9 %copy-done.3 = bf16[128,384]{1,0:T(8,128)(2,1)S(1)} copy-done((bf16[128,384]{1,0:T(8,128)(2,1)S(1)}, bf16[128,384]{1,0:T(8,128)(2,1)}, u32[]{:S(2)}) %copy-start.3) | copy-done | bytes 98328
  3.3 0.2 pack.1
  3.6 0.0 copy-start.4
  3.6 24.9 %all_to_all.20.blocks_ref = bf16[8,208,128]{2,1,0:T(8,128)(2,1)S(1)} all-to-all(bf16[8,208,128]{2,1,0:T(8,128)(2,1)S(1)} %pack.1), channel_id=1, replica_groups=mesh['grp'=8,'blk'=8,'set'=8] {'set'}, dimensions={0} | all-to-all | bytes 851968 | tf_op jit(solution)/shard_map/all_to_all | solution.py:216
  28.4 0.0 copy-done.4
  28.4 0.7 pick_middle.1
  29.2 16.3 %all_to_all.21.blocks_ref = bf16[8,144,128]{2,1,0:T(8,128)(2,1)S(1)} all-to-all(bf16[8,144,128]{2,1,0:T(8,128)(2,1)S(1)} %pick_middle.1), channel_id=1, replica_groups=mesh['grp'=8,'blk'=8,'set'=8] {'blk'}, dimensions={0} | all-to-all | bytes 589824 | tf_op jit(solution)/shard_map/all_to_all | solution.py:227
  45.5 1.4 %pick_outer.1 = bf16[8,144,128]{2,1,0:T(8,128)(2,1)} custom-call(s32[2,6]{1,0:T(2,128)S(1)} %copy-done.4, bf16[8,144,128]{2,1,0:T(8,128)(2,1)S(1)} %all_to_all.21.blocks_ref), custom_call_target="tpu_custom_call" | custom-call | tf_op jit(solution)/shard_map/pick_outer/pallas_call | solution.py:219
  46.9 13.2 %all-to-all-start.2 = ((bf16[8,144,128]{2,1,0:T(8,128)(2,1)}), bf16[8,144,128]{2,1,0:T(8,128)(2,1)S(1)}, u32[]{:S(2)}, u32[]{:S(2)}) async-start(bf16[8,144,128]{2,1,0:T(8,128)(2,1)} %pick_outer.1), calls=%async_computation.2 | async-start | bytes 589824 | tf_op jit(solution)/shard_map/all_to_all | solution.py:237
  60.1 4.3 %first.1 = (f32[1024,128]{1,0:T(8,128)S(1)}, bf16[128,128]{1,0:T(8,128)(2,1)S(1)}, bf16[16,128]{1,0:T(8,128)(2,1)S(1)}) custom-call(s32[2,6]{1,0:T(2,128)S(1)} %copy-done.4, bf16[8,208,128]{2,1,0:T(8,128)(2,1)S(1)} %all_to_all.20.blocks_ref), custom_call_target="tpu_custom_call" | custom-call | flops 6000000000 | bytes 2000000 | tf_op jit(solution)/shard_map/first/pallas_call | solution.py:228
  64.5 1.6 %middle.1 = (bf16[8,64,128]{2,1,0:T(8,128)(2,1)S(1)}, f32[128,128]{1,0:T(8,128)S(1)}) custom-call(s32[2,6]{1,0:T(2,128)S(1)} %copy-done.4, f32[1024,128]{1,0:T(8,128)S(1)} %get-tuple-element.10.state_ref, bf16[128,128]{1,0:T(8,128)(2,1)S(1)} %get-tuple-element.11.query_ref, bf16[8,144,128]{2,1,0:T(8,128)(2,1)S(1)} %all_to_all.21.blocks_ref), custom_call_target="tpu_custom_call" | custom-call | flops 2000000000 | bytes 2000000 | tf_op jit(solution)/shard_map/middle/pallas_call | solution.py:238
  66.1 0.0 copy-start
  66.1 3.3 %all-to-all-done.2.blocks_ref = bf16[8,144,128]{2,1,0:T(8,128)(2,1)S(1)} async-done(((bf16[8,144,128]{2,1,0:T(8,128)(2,1)}), bf16[8,144,128]{2,1,0:T(8,128)(2,1)S(1)}, u32[]{:S(2)}, u32[]{:S(2)}) %all-to-all-start.2) | async-done | bytes 294944 | tf_op jit(solution)/shard_map/all_to_all | solution.py:237
  69.5 1.4 %outer.1 = bf16[8,64,128]{2,1,0:T(8,128)(2,1)S(1)} custom-call(s32[2,6]{1,0:T(2,128)S(1)} %copy-done.4, f32[128,128]{1,0:T(8,128)S(1)} %get-tuple-element.12.merged_ref, bf16[16,128]{1,0:T(8,128)(2,1)S(1)} %get-tuple-element.13.query_ref, bf16[8,144,128]{2,1,0:T(8,128)(2,1)S(1)} %all-to-all-done.2.blocks_ref, ...), custom_call_target="tpu_custom_call" | custom-call | tf_op jit(solution)/shard_map/outer/pallas_call | solution.py:247
  70.9 11.7 %all_to_all.22.blocks_ref = bf16[8,64,128]{2,1,0:T(8,128)(2,1)S(1)} all-to-all(bf16[8,64,128]{2,1,0:T(8,128)(2,1)S(1)} %outer.1), channel_id=1, replica_groups=mesh['grp'=8,'blk'=8,'set'=8] {'set'}, dimensions={0} | all-to-all | bytes 262144 | tf_op jit(solution)/shard_map/all_to_all | solution.py:253
  82.7 0.0 copy-done
  82.7 1.2 %project.1 = bf16[128,768]{1,0:T(8,128)(2,1)} custom-call(bf16[8,64,128]{2,1,0:T(8,128)(2,1)S(1)} %all_to_all.22.blocks_ref, bf16[384,768]{1,0:T(8,128)(2,1)S(1)} %copy-done), custom_call_target="tpu_custom_call" | custom-call | tf_op jit(solution)/shard_map/project/pallas_call | solution.py:254
Async XLA Ops:
  0.0 0.7 copy-start.5
  0.7 0.9 %copy-start.1 = (bf16[128,384]{1,0:T(8,128)(2,1)S(1)}, bf16[128,384]{1,0:T(8,128)(2,1)}, u32[]{:S(2)}) copy-start(bf16[128,384]{1,0:T(8,128)(2,1)} %query_ref.1) | copy-start | bytes 294916
  1.5 0.9 %copy-start.2 = (bf16[128,384]{1,0:T(8,128)(2,1)S(1)}, bf16[128,384]{1,0:T(8,128)(2,1)}, u32[]{:S(2)}) copy-start(bf16[128,384]{1,0:T(8,128)(2,1)} %key_ref.1) | copy-start | bytes 294916
  2.4 0.9 %copy-start.3 = (bf16[128,384]{1,0:T(8,128)(2,1)S(1)}, bf16[128,384]{1,0:T(8,128)(2,1)}, u32[]{:S(2)}) copy-start(bf16[128,384]{1,0:T(8,128)(2,1)} %value_ref.1) | copy-start | bytes 294916
  3.6 24.9 %copy-start.4 = (s32[2,6]{1,0:T(2,128)S(1)}, s32[2,6]{1,0:T(2,128)}, u32[]{:S(2)}) copy-start(s32[2,6]{1,0:T(2,128)} %offsets_ref.9) | copy-start | bytes 148
  46.9 22.6 %all-to-all-start.2 = ((bf16[8,144,128]{2,1,0:T(8,128)(2,1)}), bf16[8,144,128]{2,1,0:T(8,128)(2,1)S(1)}, u32[]{:S(2)}, u32[]{:S(2)}) async-start(bf16[8,144,128]{2,1,0:T(8,128)(2,1)} %pick_outer.1), calls=%async_computation.2 | async-start | bytes 589824 | tf_op jit(solution)/shard_map/all_to_all | solution.py:237
  66.1 16.5 %copy-start = (bf16[384,768]{1,0:T(8,128)(2,1)S(1)}, bf16[384,768]{1,0:T(8,128)(2,1)}, u32[]{:S(2)}) copy-start(bf16[384,768]{1,0:T(8,128)(2,1)} %weight_ref.1) | copy-start | bytes 1769476

commit v2 on v1

--- a/solution.py
+++ b/solution.py
@@ -17,11 +17,13 @@
 FIRST_BLOCK = KEY_BLOCK + ROWS // 2
 EXP_SCALE = math.log2(math.e) / math.sqrt(HD)
 FAR = -1e30
+ROOM = 60 * 2**20
 F32 = jnp.float32
 BF16 = jnp.bfloat16
 
 VMEM = pl.BlockSpec(memory_space=pltpu.VMEM)
 SMEM = pl.BlockSpec(memory_space=pltpu.SMEM)
+HBM = pl.BlockSpec(memory_space=pltpu.HBM)
 
 
 def lanes(shape):
@@ -82,7 +84,20 @@
     return state / state[:, 32:33]
 
 
-def pack_kernel(query_ref, key_ref, value_ref, valid_ref, out_ref):
+def pack_kernel(query_hbm, key_hbm, value_hbm, valid_hbm, out_ref, query_ref, key_ref, value_ref, valid_ref, sems):
+    pairs = (
+        (valid_hbm, valid_ref),
+        (key_hbm, key_ref),
+        (value_hbm, value_ref),
+        (query_hbm, query_ref),
+    )
+    copies = [pltpu.make_async_copy(a, b, sems.at[i]) for i, (a, b) in enumerate(pairs)]
+    for copy in copies:
+        copy.start()
+    for h in range(HEADS, PEERS):
+        out_ref[h] = jnp.zeros((FIRST_BLOCK, 2 * HD), BF16)
+    for copy in copies:
+        copy.wait()
     flags = jnp.broadcast_to(valid_ref[...].astype(F32), (FLAG_ROWS, ROWS)).astype(BF16)
     half = ROWS // 2
     for h in range(HEADS):
@@ -92,29 +107,30 @@
         out_ref[h, ROWS:KEY_BLOCK, :] = flags
         out_ref[h, KEY_BLOCK:FIRST_BLOCK, 0:HD] = query_ref[0:half, at]
         out_ref[h, KEY_BLOCK:FIRST_BLOCK, HD : 2 * HD] = query_ref[half:ROWS, at]
-    for h in range(HEADS, PEERS):
-        out_ref[h] = jnp.zeros((FIRST_BLOCK, 2 * HD), BF16)
-
-
-def pick_kernel(which, offsets_ref, blocks_ref, out_ref, wide):
+
+
+def pick_kernel(which, offsets_ref, blocks_ref, out_ref):
     shift = shifts(offsets_ref)[which]
+    count = ROWS // 8
+    shape = (count, ROWS)
+    selector = (lanes(shape) == shift + 8 * rows(shape)).astype(F32).astype(BF16)
     flag_rows = jnp.zeros((PEERS, ROWS), F32)
     for c in range(PEERS):
-        wide[c * ROWS : (c + 1) * ROWS, :] = blocks_ref[c, 0:ROWS, :].astype(F32)
+        picked = jnp.dot(selector, blocks_ref[c, 0:ROWS, :], preferred_element_type=F32).astype(BF16)
+        for d in range(PEERS):
+            out_ref[d, c * count : (c + 1) * count, :] = picked
         flags = blocks_ref[c, ROWS:KEY_BLOCK, :].astype(F32)[0:PEERS, :]
         flag_rows = jnp.where(rows((PEERS, ROWS)) == c, flags, flag_rows)
-    picked = wide[pl.ds(shift, ROWS, stride=8), :].astype(BF16)
     square = (ROWS, ROWS)
-    selector = rows(square) == shift + 8 * (lanes(square) % 16)
+    chosen = rows(square) == shift + 8 * (lanes(square) % count)
     spread = jnp.dot(
-        flag_rows.astype(BF16), selector.astype(F32).astype(BF16), preferred_element_type=F32
-    )
-    own = rows((PEERS, ROWS)) == lanes((PEERS, ROWS)) // 16
+        flag_rows.astype(BF16), chosen.astype(F32).astype(BF16), preferred_element_type=F32
+    )
+    own = rows((PEERS, ROWS)) == lanes((PEERS, ROWS)) // count
     flags = jnp.sum(jnp.where(own, spread, F32(0.0)), axis=0, keepdims=True)
     flags = jnp.broadcast_to(flags, (FLAG_ROWS, ROWS)).astype(BF16)
-    for c in range(PEERS):
-        out_ref[c, 0:ROWS, :] = picked
-        out_ref[c, ROWS:KEY_BLOCK, :] = flags
+    for d in range(PEERS):
+        out_ref[d, ROWS:KEY_BLOCK, :] = flags
 
 
 def first_kernel(offsets_ref, blocks_ref, state_ref, middle_ref, outer_ref, wide, narrow):
@@ -165,29 +181,32 @@
     found = level(query_ref[...], blocks_ref, masks)
     both = divided(merge(merged_ref[pl.ds(stride, count, stride=8), :], found))
     turned = pltpu.roll(both, HD, 1)
-    half = ROWS // 2
-    here = rows((half, 2 * HD)) == middle + 8 * stride
+    tile = 16
+    token = middle + 8 * stride
+    start = pl.multiple_of((token // tile) * tile, tile)
+    here = rows((tile, 2 * HD)) == token - start
     low = lanes((1, 2 * HD)) < HD
     for j in range(PEERS):
         row = jnp.where(low, turned[2 * j : 2 * j + 1, :], both[2 * j + 1 : 2 * j + 2, :])
-        out_ref[j] = jnp.where(here, row, before_ref[j].astype(F32)).astype(BF16)
+        kept = before_ref[j, pl.ds(start, tile), :].astype(F32)
+        out_ref[j, pl.ds(start, tile), :] = jnp.where(here, row, kept).astype(BF16)
 
 
 def project_kernel(blocks_ref, weight_ref, out_ref):
     half = ROWS // 2
-    for part in range(2):
-        total = None
-        for h in range(HEADS):
-            add = jnp.dot(
-                blocks_ref[h, :, part * HD : (part + 1) * HD],
-                weight_ref[h * HD : (h + 1) * HD, :],
-                preferred_element_type=F32,
-            )
-            total = add if total is None else total + add
-        out_ref[part * half : (part + 1) * half, :] = total.astype(BF16)
-
-
-def call(kernel, name, out_shape, in_specs, scratch=(), flops=0, moved=0):
+    low = lanes((half, 2 * HD)) < HD
+    tops, bottoms = [], []
+    for h in range(0, HEADS, 2):
+        one, two = blocks_ref[h].astype(F32), blocks_ref[h + 1].astype(F32)
+        tops.append(jnp.where(low, one, pltpu.roll(two, HD, 1)).astype(BF16))
+        bottoms.append(jnp.where(low, pltpu.roll(one, HD, 1), two).astype(BF16))
+    combined = jnp.concatenate(
+        [jnp.concatenate(tops, axis=1), jnp.concatenate(bottoms, axis=1)], axis=0
+    )
+    out_ref[...] = jnp.dot(combined, weight_ref[...], preferred_element_type=F32).astype(BF16)
+
+
+def call(kernel, name, out_shape, in_specs, scratch=(), flops=0, moved=0, aliases=None, room=40 * 2**20):
     outs = jax.tree.map(lambda _: VMEM, out_shape)
     return pl.pallas_call(
         kernel,
@@ -196,7 +215,8 @@
         in_specs=in_specs,
         out_specs=outs,
         scratch_shapes=list(scratch),
-        compiler_params=pltpu.CompilerParams(vmem_limit_bytes=40 * 2**20),
+        input_output_aliases=aliases or {},
+        compiler_params=pltpu.CompilerParams(vmem_limit_bytes=room),
         cost_estimate=pl.CostEstimate(flops=flops, bytes_accessed=moved, transcendentals=0),
     )
 
@@ -210,9 +230,15 @@
     narrow = pltpu.VMEM((ROWS, 2 * HD), F32)
     swap = functools.partial(lax.all_to_all, split_axis=0, concat_axis=0, tiled=True)
 
-    packed = call(pack_kernel, "pack", shaped(PEERS, FIRST_BLOCK, 2 * HD), [VMEM] * 4)(
-        queries, keys, values, valid.reshape(1, ROWS)
-    )
+    whole = pltpu.VMEM((ROWS, HEADS * HD), BF16)
+    packed = call(
+        pack_kernel,
+        "pack",
+        shaped(PEERS, FIRST_BLOCK, 2 * HD),
+        [HBM] * 4,
+        [whole, whole, whole, pltpu.VMEM((1, ROWS), jnp.int32), pltpu.SemaphoreType.DMA((4,))],
+        room=ROOM,
+    )(queries, keys, values, valid.reshape(1, ROWS))
     dense = swap(packed, "set")
 
     def pick(which, name, blocks):
@@ -221,7 +247,6 @@
             name,
             shaped(PEERS, KEY_BLOCK, 2 * HD),
             [SMEM, VMEM],
-            [wide],
         )(offsets, blocks)
 
     middle_blocks = swap(pick(0, "pick_middle", dense), "blk")
@@ -249,6 +274,7 @@
         "outer",
         shaped(PEERS, ROWS // 2, 2 * HD),
         [SMEM, VMEM, VMEM, VMEM, VMEM],
+        aliases={4: 0},
     )(offsets, merged, outer_query, outer_blocks, before)
     home = swap(combined, "set")
     return call(project_kernel, "project", shaped(ROWS, 768), [VMEM, VMEM])(home, w_out)

time: 84.2 us -> 82.8 us (0.983)
  local copies, waits for them, and re-layouts: 3.34 us -> 0.01 us
  Pallas kernels: 11 us -> 12.7 us
    unnamed x12 -> x4, local copies, waits for them, and re-layouts: 3.34 us -> 0.01 us
    pallas_call x1, Pallas kernels: 0.21 us -> 2.01 us  [per_device(): call(pack_kernel, 'pack', shaped(PEERS, FIRST_BLOCK, 2 * HD), [HBM] * 4,...]
where the time goes in v2:
time: 82.8 us; the launch traced here: 82.4 us
  blocking collectives  53.1 us (64%)
  starting transfers between devices  13.2 us (16%)
  Pallas kernels  12.7 us (15%)
  waiting for transfers between devices  3.35 us (4%)
    all_to_all x1, blocking collectives, per_device(): dense = swap(packed, 'set')  25.1 us
    all_to_all x1, blocking collectives, per_device(): middle_blocks = swap(pick(0, 'pick_middle', dense), 'blk')  16.3 us
    all_to_all x1, starting transfers between devices, per_device(): outer_blocks = swap(pick(1, 'pick_outer', middle_blocks), 'grp')  13.2 us
    all_to_all x1, blocking collectives, per_device(): home = swap(combined, 'set')  11.7 us
    pallas_call x1, Pallas kernels, per_device(): call(first_kernel, 'first', (shaped(PEERS * ROWS, 2 * HD, dtype=F32), sha...  4.34 us
    all_to_all x1, waiting for transfers between devices, per_device(): outer_blocks = swap(pick(1, 'pick_outer', middle_blocks), 'grp')  3.35 us
    pallas_call x2, Pallas kernels, pick(): call(functools.partial(pick_kernel, which), name, shaped(PEERS, KEY_BLOCK...  2.21 us
    pallas_call x1, Pallas kernels, per_device(): call(pack_kernel, 'pack', shaped(PEERS, FIRST_BLOCK, 2 * HD), [HBM] * 4,...  2.01 us
  transfers between devices with their start and end apart: 1, of which 1 were waited for; matrix products, arithmetic and copies ran while one was open for 0% of the time, Pallas kernels for 7%

profile of v2, /device:TPU:1, one launch (start us, length us, event | category | flops | bytes accessed | tf_op | source)
XLA Modules:
  0.0 82.4 jit_solution(3331505931261049809)
XLA Ops:
  0.0 2.0 %pack.1 = bf16[8,208,128]{2,1,0:T(8,128)(2,1)} custom-call(bf16[128,384]{1,0:T(8,128)(2,1)} %query_hbm.1, bf16[128,384]{1,0:T(8,128)(2,1)} %key_hbm.1, bf16[128,384]{1,0:T(8,128)(2,1)} %value_hbm.1, s32[1,128]{1,0:T(1,128)} %bitcast.1), custom_call_target="tpu_custom_call" | custom-call | tf_op jit(solution)/shard_map/pack/pallas_call | solution.py:234
  2.0 0.0 copy-start.1
  2.0 25.1 %all_to_all.20.blocks_ref = bf16[8,208,128]{2,1,0:T(8,128)(2,1)S(1)} all-to-all(bf16[8,208,128]{2,1,0:T(8,128)(2,1)} %pack.1), channel_id=1, replica_groups=mesh['grp'=8,'blk'=8,'set'=8] {'set'}, dimensions={0} | all-to-all | bytes 851968 | tf_op jit(solution)/shard_map/all_to_all | solution.py:242
  27.1 0.0 copy-done.1
  27.1 0.7 pick_middle.1
  27.9 16.3 %all_to_all.21.blocks_ref = bf16[8,144,128]{2,1,0:T(8,128)(2,1)S(1)} all-to-all(bf16[8,144,128]{2,1,0:T(8,128)(2,1)S(1)} %pick_middle.1), channel_id=1, replica_groups=mesh['grp'=8,'blk'=8,'set'=8] {'blk'}, dimensions={0} | all-to-all | bytes 589824 | tf_op jit(solution)/shard_map/all_to_all | solution.py:252
  44.2 1.5 %pick_outer.1 = bf16[8,144,128]{2,1,0:T(8,128)(2,1)} custom-call(s32[2,6]{1,0:T(2,128)S(1)} %copy-done.1, bf16[8,144,128]{2,1,0:T(8,128)(2,1)S(1)} %all_to_all.21.blocks_ref), custom_call_target="tpu_custom_call" | custom-call | tf_op jit(solution)/shard_map/pick_outer/pallas_call | solution.py:245
  45.6 13.2 %all-to-all-start.2 = ((bf16[8,144,128]{2,1,0:T(8,128)(2,1)}), bf16[8,144,128]{2,1,0:T(8,128)(2,1)S(1)}, u32[]{:S(2)}, u32[]{:S(2)}) async-start(bf16[8,144,128]{2,1,0:T(8,128)(2,1)} %pick_outer.1), calls=%async_computation.2 | async-start | bytes 589824 | tf_op jit(solution)/shard_map/all_to_all | solution.py:262
  58.9 4.3 %first.1 = (f32[1024,128]{1,0:T(8,128)S(1)}, bf16[128,128]{1,0:T(8,128)(2,1)S(1)}, bf16[16,128]{1,0:T(8,128)(2,1)S(1)}) custom-call(s32[2,6]{1,0:T(2,128)S(1)} %copy-done.1, bf16[8,208,128]{2,1,0:T(8,128)(2,1)S(1)} %all_to_all.20.blocks_ref), custom_call_target="tpu_custom_call" | custom-call | flops 6000000000 | bytes 2000000 | tf_op jit(solution)/shard_map/first/pallas_call | solution.py:253
  63.2 1.6 %middle.1 = (bf16[8,64,128]{2,1,0:T(8,128)(2,1)S(1)}, f32[128,128]{1,0:T(8,128)S(1)}) custom-call(s32[2,6]{1,0:T(2,128)S(1)} %copy-done.1, f32[1024,128]{1,0:T(8,128)S(1)} %get-tuple-element.10.state_ref, bf16[128,128]{1,0:T(8,128)(2,1)S(1)} %get-tuple-element.11.query_ref, bf16[8,144,128]{2,1,0:T(8,128)(2,1)S(1)} %all_to_all.21.blocks_ref), custom_call_target="tpu_custom_call" | custom-call | flops 2000000000 | bytes 2000000 | tf_op jit(solution)/shard_map/middle/pallas_call | solution.py:263
  64.9 0.0 copy-start
  64.9 3.3 %all-to-all-done.2.blocks_ref = bf16[8,144,128]{2,1,0:T(8,128)(2,1)S(1)} async-done(((bf16[8,144,128]{2,1,0:T(8,128)(2,1)}), bf16[8,144,128]{2,1,0:T(8,128)(2,1)S(1)}, u32[]{:S(2)}, u32[]{:S(2)}) %all-to-all-start.2) | async-done | bytes 294944 | tf_op jit(solution)/shard_map/all_to_all | solution.py:262
  68.2 1.4 %outer.1 = bf16[8,64,128]{2,1,0:T(8,128)(2,1)S(1)} custom-call(s32[2,6]{1,0:T(2,128)S(1)} %copy-done.1, f32[128,128]{1,0:T(8,128)S(1)} %get-tuple-element.12.merged_ref, bf16[16,128]{1,0:T(8,128)(2,1)S(1)} %get-tuple-element.13.query_ref, bf16[8,144,128]{2,1,0:T(8,128)(2,1)S(1)} %all-to-all-done.2.blocks_ref, ...), custom_call_target="tpu_custom_call", output_to_operand_aliasing={{}: (4, {})} | custom-call | tf_op jit(solution)/shard_map/outer/pallas_call | solution.py:272
  69.7 11.7 %all_to_all.22.blocks_ref = bf16[8,64,128]{2,1,0:T(8,128)(2,1)S(1)} all-to-all(bf16[8,64,128]{2,1,0:T(8,128)(2,1)S(1)} %outer.1), channel_id=1, replica_groups=mesh['grp'=8,'blk'=8,'set'=8] {'set'}, dimensions={0} | all-to-all | bytes 262144 | tf_op jit(solution)/shard_map/all_to_all | solution.py:279
  81.4 0.0 copy-done
  81.4 1.0 %project.1 = bf16[128,768]{1,0:T(8,128)(2,1)} custom-call(bf16[8,64,128]{2,1,0:T(8,128)(2,1)S(1)} %all_to_all.22.blocks_ref, bf16[384,768]{1,0:T(8,128)(2,1)S(1)} %copy-done), custom_call_target="tpu_custom_call" | custom-call | tf_op jit(solution)/shard_map/project/pallas_call | solution.py:280
Async XLA Ops:
  2.0 25.1 %copy-start.1 = (s32[2,6]{1,0:T(2,128)S(1)}, s32[2,6]{1,0:T(2,128)}, u32[]{:S(2)}) copy-start(s32[2,6]{1,0:T(2,128)} %offsets_ref.9) | copy-start | bytes 148
  45.6 22.6 %all-to-all-start.2 = ((bf16[8,144,128]{2,1,0:T(8,128)(2,1)}), bf16[8,144,128]{2,1,0:T(8,128)(2,1)S(1)}, u32[]{:S(2)}, u32[]{:S(2)}) async-start(bf16[8,144,128]{2,1,0:T(8,128)(2,1)} %pick_outer.1), calls=%async_computation.2 | async-start | bytes 589824 | tf_op jit(solution)/shard_map/all_to_all | solution.py:262
  64.9 16.6 %copy-start = (bf16[384,768]{1,0:T(8,128)(2,1)S(1)}, bf16[384,768]{1,0:T(8,128)(2,1)}, u32[]{:S(2)}) copy-start(bf16[384,768]{1,0:T(8,128)(2,1)} %weight_ref.1) | copy-start | bytes 1769476

commit v3 on v2

--- a/solution.py
+++ b/solution.py
@@ -17,12 +17,10 @@
 FIRST_BLOCK = KEY_BLOCK + ROWS // 2
 EXP_SCALE = math.log2(math.e) / math.sqrt(HD)
 FAR = -1e30
-ROOM = 60 * 2**20
 F32 = jnp.float32
 BF16 = jnp.bfloat16
 
 VMEM = pl.BlockSpec(memory_space=pltpu.VMEM)
-SMEM = pl.BlockSpec(memory_space=pltpu.SMEM)
 HBM = pl.BlockSpec(memory_space=pltpu.HBM)
 
 
@@ -39,9 +37,11 @@
 
 
 def shifts(offsets_ref):
-    head = my_head()
-    middle = offsets_ref[0, head]
-    return middle, (offsets_ref[1, head] - middle) // 8
+    both = offsets_ref[...].astype(F32)
+    both = jnp.where(lanes(both.shape) == my_head(), both, F32(0.0))
+    middle = jnp.sum(both[0:1, :]).astype(jnp.int32)
+    outer = jnp.sum(both[1:2, :]).astype(jnp.int32)
+    return middle, (outer - middle) // 8
 
 
 def scores(query, block_ref, index, self_mask):
@@ -206,7 +206,7 @@
     out_ref[...] = jnp.dot(combined, weight_ref[...], preferred_element_type=F32).astype(BF16)
 
 
-def call(kernel, name, out_shape, in_specs, scratch=(), flops=0, moved=0, aliases=None, room=40 * 2**20):
+def call(kernel, name, out_shape, in_specs, scratch=(), flops=0, moved=0, aliases=None):
     outs = jax.tree.map(lambda _: VMEM, out_shape)
     return pl.pallas_call(
         kernel,
@@ -216,7 +216,7 @@
         out_specs=outs,
         scratch_shapes=list(scratch),
         input_output_aliases=aliases or {},
-        compiler_params=pltpu.CompilerParams(vmem_limit_bytes=room),
+        compiler_params=pltpu.CompilerParams(vmem_limit_bytes=40 * 2**20),
         cost_estimate=pl.CostEstimate(flops=flops, bytes_accessed=moved, transcendentals=0),
     )
 
@@ -231,14 +231,14 @@
     swap = functools.partial(lax.all_to_all, split_axis=0, concat_axis=0, tiled=True)
 
     whole = pltpu.VMEM((ROWS, HEADS * HD), BF16)
+    given = (queries, keys, values, valid.reshape(1, ROWS))
     packed = call(
         pack_kernel,
         "pack",
         shaped(PEERS, FIRST_BLOCK, 2 * HD),
         [HBM] * 4,
         [whole, whole, whole, pltpu.VMEM((1, ROWS), jnp.int32), pltpu.SemaphoreType.DMA((4,))],
-        room=ROOM,
-    )(queries, keys, values, valid.reshape(1, ROWS))
+    )(*(pltpu.with_memory_space_constraint(a, pltpu.HBM) for a in given))
     dense = swap(packed, "set")
 
     def pick(which, name, blocks):
@@ -246,7 +246,7 @@
             functools.partial(pick_kernel, which),
             name,
             shaped(PEERS, KEY_BLOCK, 2 * HD),
-            [SMEM, VMEM],
+            [VMEM, VMEM],
         )(offsets, blocks)
 
     middle_blocks = swap(pick(0, "pick_middle", dense), "blk")
@@ -254,7 +254,7 @@
         first_kernel,
         "first",
         (shaped(PEERS * ROWS, 2 * HD, dtype=F32), shaped(ROWS, 2 * HD), shaped(ROWS // 8, 2 * HD)),
-        [SMEM, VMEM],
+        [VMEM, VMEM],
         [wide, narrow],
         flops=6_000_000_000,
         moved=2_000_000,
@@ -264,7 +264,7 @@
         middle_kernel,
         "middle",
         (shaped(PEERS, ROWS // 2, 2 * HD), shaped(ROWS, 2 * HD, dtype=F32)),
-        [SMEM, VMEM, VMEM, VMEM],
+        [VMEM, VMEM, VMEM, VMEM],
         [wide],
         flops=2_000_000_000,
         moved=2_000_000,
@@ -273,7 +273,7 @@
         outer_kernel,
         "outer",
         shaped(PEERS, ROWS // 2, 2 * HD),
-        [SMEM, VMEM, VMEM, VMEM, VMEM],
+        [VMEM, VMEM, VMEM, VMEM, VMEM],
         aliases={4: 0},
     )(offsets, merged, outer_query, outer_blocks, before)
     home = swap(combined, "set")

time: 82.8 us -> 80.4 us (0.971)
  Pallas kernels: 12.7 us -> 9.41 us
  waiting for transfers between devices: 3.35 us -> 4.43 us
    all_to_all x1, waiting for transfers between devices: 3.35 us -> 4.43 us  [per_device(): outer_blocks = swap(pick(1, 'pick_outer', middle_blocks), 'grp')]
    pallas_call x2, Pallas kernels: 2.21 us -> 1.34 us  [pick(): call(functools.partial(pick_kernel, which), name, shaped(PEERS, KEY_BLOCK...]
  transfers between devices with their start and end apart: 1 -> 1, of which waited for: 1 -> 1; matrix products, arithmetic and copies ran while one was open for 0% -> 0% of each run, Pallas kernels for 7% -> 6%
where the time goes in v3:
time: 80.4 us; the launch traced here: 80 us
  blocking collectives  52.9 us (66%)
  starting transfers between devices  13.2 us (16%)
  Pallas kernels  9.41 us (12%)
  waiting for transfers between devices  4.43 us (6%)
    all_to_all x1, blocking collectives, per_device(): dense = swap(packed, 'set')  24.9 us
    all_to_all x1, blocking collectives, per_device(): middle_blocks = swap(pick(0, 'pick_middle', dense), 'blk')  16.3 us
    all_to_all x1, starting transfers between devices, per_device(): outer_blocks = swap(pick(1, 'pick_outer', middle_blocks), 'grp')  13.2 us
    all_to_all x1, blocking collectives, per_device(): home = swap(combined, 'set')  11.7 us
    all_to_all x1, waiting for transfers between devices, per_device(): outer_blocks = swap(pick(1, 'pick_outer', middle_blocks), 'grp')  4.43 us
    pallas_call x1, Pallas kernels, per_device(): call(first_kernel, 'first', (shaped(PEERS * ROWS, 2 * HD, dtype=F32), sha...  3.82 us
  transfers between devices with their start and end apart: 1, of which 1 were waited for; matrix products, arithmetic and copies ran while one was open for 0% of the time, Pallas kernels for 6%

profile of v3, /device:TPU:1, one launch (start us, length us, event | category | flops | bytes accessed | tf_op | source)
XLA Modules:
  0.0 80.0 jit_solution(17736170445977879306)
XLA Ops:
  0.0 1.3 %pack.1 = bf16[8,208,128]{2,1,0:T(8,128)(2,1)S(1)} custom-call(bf16[128,384]{1,0:T(8,128)(2,1)} %query_hbm.1, bf16[128,384]{1,0:T(8,128)(2,1)} %key_hbm.1, bf16[128,384]{1,0:T(8,128)(2,1)} %value_hbm.1, s32[1,128]{1,0:T(1,128)} %bitcast.1), custom_call_target="tpu_custom_call" | custom-call | tf_op jit(solution)/shard_map/pack/pallas_call | solution.py:235
  1.3 0.0 copy-start.1
  1.3 24.9 %all_to_all.20.blocks_ref = bf16[8,208,128]{2,1,0:T(8,128)(2,1)S(1)} all-to-all(bf16[8,208,128]{2,1,0:T(8,128)(2,1)S(1)} %pack.1), channel_id=1, replica_groups=mesh['grp'=8,'blk'=8,'set'=8] {'set'}, dimensions={0} | all-to-all | bytes 851968 | tf_op jit(solution)/shard_map/all_to_all | solution.py:242
  26.2 0.0 copy-done.1
  26.2 0.3 pick_middle.1
  26.5 16.3 %all_to_all.21.blocks_ref = bf16[8,144,128]{2,1,0:T(8,128)(2,1)S(1)} all-to-all(bf16[8,144,128]{2,1,0:T(8,128)(2,1)S(1)} %pick_middle.1), channel_id=1, replica_groups=mesh['grp'=8,'blk'=8,'set'=8] {'blk'}, dimensions={0} | all-to-all | bytes 589824 | tf_op jit(solution)/shard_map/all_to_all | solution.py:252
  42.8 1.0 %pick_outer.1 = bf16[8,144,128]{2,1,0:T(8,128)(2,1)} custom-call(s32[2,6]{1,0:T(2,128)S(1)} %copy-done.1, bf16[8,144,128]{2,1,0:T(8,128)(2,1)S(1)} %all_to_all.21.blocks_ref), custom_call_target="tpu_custom_call" | custom-call | tf_op jit(solution)/shard_map/pick_outer/pallas_call | solution.py:245
  43.8 13.2 %all-to-all-start.2 = ((bf16[8,144,128]{2,1,0:T(8,128)(2,1)}), bf16[8,144,128]{2,1,0:T(8,128)(2,1)S(1)}, u32[]{:S(2)}, u32[]{:S(2)}) async-start(bf16[8,144,128]{2,1,0:T(8,128)(2,1)} %pick_outer.1), calls=%async_computation.2 | async-start | bytes 589824 | tf_op jit(solution)/shard_map/all_to_all | solution.py:262
  57.0 3.8 %first.1 = (f32[1024,128]{1,0:T(8,128)S(1)}, bf16[128,128]{1,0:T(8,128)(2,1)S(1)}, bf16[16,128]{1,0:T(8,128)(2,1)S(1)}) custom-call(s32[2,6]{1,0:T(2,128)S(1)} %copy-done.1, bf16[8,208,128]{2,1,0:T(8,128)(2,1)S(1)} %all_to_all.20.blocks_ref), custom_call_target="tpu_custom_call" | custom-call | flops 6000000000 | bytes 2000000 | tf_op jit(solution)/shard_map/first/pallas_call | solution.py:253
  60.8 1.1 %middle.1 = (bf16[8,64,128]{2,1,0:T(8,128)(2,1)S(1)}, f32[128,128]{1,0:T(8,128)S(1)}) custom-call(s32[2,6]{1,0:T(2,128)S(1)} %copy-done.1, f32[1024,128]{1,0:T(8,128)S(1)} %get-tuple-element.10.state_ref, bf16[128,128]{1,0:T(8,128)(2,1)S(1)} %get-tuple-element.11.query_ref, bf16[8,144,128]{2,1,0:T(8,128)(2,1)S(1)} %all_to_all.21.blocks_ref), custom_call_target="tpu_custom_call" | custom-call | flops 2000000000 | bytes 2000000 | tf_op jit(solution)/shard_map/middle/pallas_call | solution.py:263
  61.9 0.0 copy-start
  62.0 4.4 %all-to-all-done.2.blocks_ref = bf16[8,144,128]{2,1,0:T(8,128)(2,1)S(1)} async-done(((bf16[8,144,128]{2,1,0:T(8,128)(2,1)}), bf16[8,144,128]{2,1,0:T(8,128)(2,1)S(1)}, u32[]{:S(2)}, u32[]{:S(2)}) %all-to-all-start.2) | async-done | bytes 294944 | tf_op jit(solution)/shard_map/all_to_all | solution.py:262
  66.4 0.9 %outer.1 = bf16[8,64,128]{2,1,0:T(8,128)(2,1)S(1)} custom-call(s32[2,6]{1,0:T(2,128)S(1)} %copy-done.1, f32[128,128]{1,0:T(8,128)S(1)} %get-tuple-element.12.merged_ref, bf16[16,128]{1,0:T(8,128)(2,1)S(1)} %get-tuple-element.13.query_ref, bf16[8,144,128]{2,1,0:T(8,128)(2,1)S(1)} %all-to-all-done.2.blocks_ref, ...), custom_call_target="tpu_custom_call", output_to_operand_aliasing={{}: (4, {})} | custom-call | tf_op jit(solution)/shard_map/outer/pallas_call | solution.py:272
  67.3 11.7 %all_to_all.22.blocks_ref = bf16[8,64,128]{2,1,0:T(8,128)(2,1)S(1)} all-to-all(bf16[8,64,128]{2,1,0:T(8,128)(2,1)S(1)} %outer.1), channel_id=1, replica_groups=mesh['grp'=8,'blk'=8,'set'=8] {'set'}, dimensions={0} | all-to-all | bytes 262144 | tf_op jit(solution)/shard_map/all_to_all | solution.py:279
  79.0 0.0 copy-done
  79.0 1.0 %project.1 = bf16[128,768]{1,0:T(8,128)(2,1)} custom-call(bf16[8,64,128]{2,1,0:T(8,128)(2,1)S(1)} %all_to_all.22.blocks_ref, bf16[384,768]{1,0:T(8,128)(2,1)S(1)} %copy-done), custom_call_target="tpu_custom_call" | custom-call | tf_op jit(solution)/shard_map/project/pallas_call | solution.py:280
Async XLA Ops:
  1.3 24.9 %copy-start.1 = (s32[2,6]{1,0:T(2,128)S(1)}, s32[2,6]{1,0:T(2,128)}, u32[]{:S(2)}) copy-start(s32[2,6]{1,0:T(2,128)} %offsets_ref.9) | copy-start | bytes 148
  43.8 22.6 %all-to-all-start.2 = ((bf16[8,144,128]{2,1,0:T(8,128)(2,1)}), bf16[8,144,128]{2,1,0:T(8,128)(2,1)S(1)}, u32[]{:S(2)}, u32[]{:S(2)}) async-start(bf16[8,144,128]{2,1,0:T(8,128)(2,1)} %pick_outer.1), calls=%async_computation.2 | async-start | bytes 589824 | tf_op jit(solution)/shard_map/all_to_all | solution.py:262
  61.9 17.1 %copy-start = (bf16[384,768]{1,0:T(8,128)(2,1)S(1)}, bf16[384,768]{1,0:T(8,128)(2,1)}, u32[]{:S(2)}) copy-start(bf16[384,768]{1,0:T(8,128)(2,1)} %weight_ref.1) | copy-start | bytes 1769476

commit v4 on v3

--- a/solution.py
+++ b/solution.py
@@ -12,9 +12,8 @@
 HD = 64
 PEERS = 8
 ROWS = 128
-FLAG_ROWS = 16
-KEY_BLOCK = ROWS + FLAG_ROWS
-FIRST_BLOCK = KEY_BLOCK + ROWS // 2
+FIRST_BLOCK = ROWS + ROWS // 2
+MARK = 1024.0
 EXP_SCALE = math.log2(math.e) / math.sqrt(HD)
 FAR = -1e30
 F32 = jnp.float32
@@ -44,19 +43,32 @@
     return middle, (outer - middle) // 8
 
 
-def scores(query, block_ref, index, self_mask):
-    raw = lax.dot_general(
+def marks():
+    shape = (16, 2 * HD)
+    row, lane = rows(shape), lanes(shape)
+    chosen = ((row == 0) & (lane == 0)) | ((row == 1) & (lane >= 1) & (lane <= 3))
+    return chosen.astype(F32).astype(BF16)
+
+
+def against(query, block_ref, index):
+    return lax.dot_general(
         query, block_ref[index, 0:ROWS, :], (((1,), (1,)), ((), ())), preferred_element_type=F32
     )
-    flags = block_ref[index, ROWS:KEY_BLOCK, :].astype(F32)[0:1, :]
-    bias = jnp.where(flags > 0.5, F32(0.0), F32(FAR))
-    if self_mask is not None:
-        bias = jnp.where(self_mask, F32(0.0), bias)
-    return raw + bias
-
-
-def level(query, block_ref, self_masks):
-    parts = [scores(query, block_ref, c, self_masks[c]) for c in range(PEERS)]
+
+
+def level(query, block_ref, self_masks, seen=None):
+    count = query.shape[0]
+    parts = []
+    if seen is None:
+        query = jnp.concatenate([query, marks()], axis=0)
+    for c in range(PEERS):
+        part = against(query, block_ref, c)
+        seen_part = part[count:, :] if seen is None else seen[c]
+        hidden = seen_part[0:1, :] > F32(MARK / 2)
+        masked = part[0:count, :] + jnp.where(hidden, F32(FAR), F32(0.0))
+        if self_masks[c] is not None:
+            masked = jnp.where(self_masks[c] & hidden, seen_part[1:2, :], masked)
+        parts.append(masked)
     best = functools.reduce(jnp.maximum, parts)
     top = jnp.max(best, axis=1, keepdims=True)
     sums = None
@@ -98,15 +110,24 @@
         out_ref[h] = jnp.zeros((FIRST_BLOCK, 2 * HD), BF16)
     for copy in copies:
         copy.wait()
-    flags = jnp.broadcast_to(valid_ref[...].astype(F32), (FLAG_ROWS, ROWS)).astype(BF16)
+    square = (ROWS, ROWS)
+    valid = jnp.where(rows(square) == lanes(square), valid_ref[...].astype(F32), F32(0.0))
+    hidden = jnp.sum(valid, axis=1, keepdims=True) < F32(0.5)
     half = ROWS // 2
+    lane = lanes((ROWS, HD))
     for h in range(HEADS):
         at = slice(h * HD, (h + 1) * HD)
-        out_ref[h, 0:ROWS, 0:HD] = key_ref[:, at]
+        key = key_ref[:, at].astype(F32)
+        own = jnp.sum(query_ref[:, at].astype(F32) * key, axis=1, keepdims=True)
+        high = own.astype(BF16).astype(F32)
+        middle = (own - high).astype(BF16).astype(F32)
+        rest = own - high - middle
+        code = jnp.where(lane == 0, F32(MARK), jnp.where(lane == 1, high, F32(0.0)))
+        code = jnp.where(lane == 2, middle, jnp.where(lane == 3, rest, code))
+        out_ref[h, 0:ROWS, 0:HD] = jnp.where(hidden, code, key).astype(BF16)
         out_ref[h, 0:ROWS, HD : 2 * HD] = value_ref[:, at]
-        out_ref[h, ROWS:KEY_BLOCK, :] = flags
-        out_ref[h, KEY_BLOCK:FIRST_BLOCK, 0:HD] = query_ref[0:half, at]
-        out_ref[h, KEY_BLOCK:FIRST_BLOCK, HD : 2 * HD] = query_ref[half:ROWS, at]
+        out_ref[h, ROWS:FIRST_BLOCK, 0:HD] = query_ref[0:half, at]
+        out_ref[h, ROWS:FIRST_BLOCK, HD : 2 * HD] = query_ref[half:ROWS, at]
 
 
 def pick_kernel(which, offsets_ref, blocks_ref, out_ref):
@@ -114,23 +135,10 @@
     count = ROWS // 8
     shape = (count, ROWS)
     selector = (lanes(shape) == shift + 8 * rows(shape)).astype(F32).astype(BF16)
-    flag_rows = jnp.zeros((PEERS, ROWS), F32)
     for c in range(PEERS):
         picked = jnp.dot(selector, blocks_ref[c, 0:ROWS, :], preferred_element_type=F32).astype(BF16)
         for d in range(PEERS):
             out_ref[d, c * count : (c + 1) * count, :] = picked
-        flags = blocks_ref[c, ROWS:KEY_BLOCK, :].astype(F32)[0:PEERS, :]
-        flag_rows = jnp.where(rows((PEERS, ROWS)) == c, flags, flag_rows)
-    square = (ROWS, ROWS)
-    chosen = rows(square) == shift + 8 * (lanes(square) % count)
-    spread = jnp.dot(
-        flag_rows.astype(BF16), chosen.astype(F32).astype(BF16), preferred_element_type=F32
-    )
-    own = rows((PEERS, ROWS)) == lanes((PEERS, ROWS)) // count
-    flags = jnp.sum(jnp.where(own, spread, F32(0.0)), axis=0, keepdims=True)
-    flags = jnp.broadcast_to(flags, (FLAG_ROWS, ROWS)).astype(BF16)
-    for d in range(PEERS):
-        out_ref[d, ROWS:KEY_BLOCK, :] = flags
 
 
 def first_kernel(offsets_ref, blocks_ref, state_ref, middle_ref, outer_ref, wide, narrow):
@@ -138,15 +146,17 @@
     half = ROWS // 2
     low = lanes((half, 2 * HD)) < HD
     diagonal = rows((ROWS, ROWS)) == lanes((ROWS, ROWS))
+    reader = marks()
+    seen = [against(reader, blocks_ref, c) for c in range(PEERS)]
     for j in range(PEERS):
-        pair = blocks_ref[j, KEY_BLOCK:FIRST_BLOCK, :].astype(F32)
+        pair = blocks_ref[j, ROWS:FIRST_BLOCK, :].astype(F32)
         wide[j * ROWS : j * ROWS + half, :] = jnp.where(low, pair, F32(0.0))
         wide[j * ROWS + half : (j + 1) * ROWS, :] = jnp.where(
             low, pltpu.roll(pair, HD, 1), F32(0.0)
         )
         query = wide[j * ROWS : (j + 1) * ROWS, :].astype(BF16)
         masks = [diagonal if c == j else None for c in range(PEERS)]
-        state_ref[j * ROWS : (j + 1) * ROWS, :] = level(query, blocks_ref, masks)
+        state_ref[j * ROWS : (j + 1) * ROWS, :] = level(query, blocks_ref, masks, seen)
     picked = wide[pl.ds(middle, ROWS, stride=8), :]
     middle_ref[...] = picked.astype(BF16)
     narrow[...] = picked
@@ -245,7 +255,7 @@
         return call(
             functools.partial(pick_kernel, which),
             name,
-            shaped(PEERS, KEY_BLOCK, 2 * HD),
+            shaped(PEERS, ROWS, 2 * HD),
             [VMEM, VMEM],
         )(offsets, blocks)
 

time: 80.4 us -> 78.7 us (0.979)
  waiting for transfers between devices: 4.43 us -> 3.58 us
    all_to_all x1, waiting for transfers between devices: 4.43 us -> 3.58 us  [per_device(): outer_blocks = swap(pick(1, 'pick_outer', middle_blocks), 'grp')]
  transfers between devices with their start and end apart: 1 -> 1, of which waited for: 1 -> 1; matrix products, arithmetic and copies ran while one was open for 0% -> 0% of each run, Pallas kernels for 6% -> 7%
where the time goes in v4:
time: 78.7 us; the launch traced here: 78.4 us
  blocking collectives  52.3 us (66%)
  starting transfers between devices  12.5 us (16%)
  Pallas kernels  9.9 us (13%)
  waiting for transfers between devices  3.58 us (5%)
    all_to_all x1, blocking collectives, per_device(): dense = swap(packed, 'set')  24.6 us
    all_to_all x1, blocking collectives, per_device(): middle_blocks = swap(pick(0, 'pick_middle', dense), 'blk')  16 us
    all_to_all x1, starting transfers between devices, per_device(): outer_blocks = swap(pick(1, 'pick_outer', middle_blocks), 'grp')  12.5 us
    all_to_all x1, blocking collectives, per_device(): home = swap(combined, 'set')  11.7 us
    pallas_call x1, Pallas kernels, per_device(): call(first_kernel, 'first', (shaped(PEERS * ROWS, 2 * HD, dtype=F32), sha...  3.96 us
    all_to_all x1, waiting for transfers between devices, per_device(): outer_blocks = swap(pick(1, 'pick_outer', middle_blocks), 'grp')  3.58 us
    pallas_call x1, Pallas kernels, per_device(): call(pack_kernel, 'pack', shaped(PEERS, FIRST_BLOCK, 2 * HD), [HBM] * 4,...  1.64 us
  transfers between devices with their start and end apart: 1, of which 1 were waited for; matrix products, arithmetic and copies ran while one was open for 0% of the time, Pallas kernels for 7%

profile of v4, /device:TPU:1, one launch (start us, length us, event | category | flops | bytes accessed | tf_op | source)
XLA Modules:
  0.0 78.4 jit_solution(9419781212013374443)
XLA Ops:
  0.0 1.6 %pack.1 = bf16[8,192,128]{2,1,0:T(8,128)(2,1)S(1)} custom-call(bf16[128,384]{1,0:T(8,128)(2,1)} %query_hbm.1, bf16[128,384]{1,0:T(8,128)(2,1)} %key_hbm.1, bf16[128,384]{1,0:T(8,128)(2,1)} %value_hbm.1, s32[1,128]{1,0:T(1,128)} %bitcast.1), custom_call_target="tpu_custom_call" | custom-call | tf_op jit(solution)/shard_map/pack/pallas_call | solution.py:245
  1.6 0.0 copy-start.1
  1.7 24.6 %all_to_all.20.blocks_ref = bf16[8,192,128]{2,1,0:T(8,128)(2,1)S(1)} all-to-all(bf16[8,192,128]{2,1,0:T(8,128)(2,1)S(1)} %pack.1), channel_id=1, replica_groups=mesh['grp'=8,'blk'=8,'set'=8] {'set'}, dimensions={0} | all-to-all | bytes 786432 | tf_op jit(solution)/shard_map/all_to_all | solution.py:252
  26.3 0.0 copy-done.1
  26.3 0.3 pick_middle.1
  26.6 16.0 %all_to_all.21.blocks_ref = bf16[8,128,128]{2,1,0:T(8,128)(2,1)S(1)} all-to-all(bf16[8,128,128]{2,1,0:T(8,128)(2,1)S(1)} %pick_middle.1), channel_id=1, replica_groups=mesh['grp'=8,'blk'=8,'set'=8] {'blk'}, dimensions={0} | all-to-all | bytes 524288 | tf_op jit(solution)/shard_map/all_to_all | solution.py:262
  42.5 1.0 %pick_outer.1 = bf16[8,128,128]{2,1,0:T(8,128)(2,1)} custom-call(s32[2,6]{1,0:T(2,128)S(1)} %copy-done.1, bf16[8,128,128]{2,1,0:T(8,128)(2,1)S(1)} %all_to_all.21.blocks_ref), custom_call_target="tpu_custom_call" | custom-call | tf_op jit(solution)/shard_map/pick_outer/pallas_call | solution.py:255
  43.5 12.5 %all-to-all-start.2 = ((bf16[8,128,128]{2,1,0:T(8,128)(2,1)}), bf16[8,128,128]{2,1,0:T(8,128)(2,1)S(1)}, u32[]{:S(2)}, u32[]{:S(2)}) async-start(bf16[8,128,128]{2,1,0:T(8,128)(2,1)} %pick_outer.1), calls=%async_computation.2 | async-start | bytes 524288 | tf_op jit(solution)/shard_map/all_to_all | solution.py:272
  56.0 4.0 %first.1 = (f32[1024,128]{1,0:T(8,128)S(1)}, bf16[128,128]{1,0:T(8,128)(2,1)S(1)}, bf16[16,128]{1,0:T(8,128)(2,1)S(1)}) custom-call(s32[2,6]{1,0:T(2,128)S(1)} %copy-done.1, bf16[8,192,128]{2,1,0:T(8,128)(2,1)S(1)} %all_to_all.20.blocks_ref), custom_call_target="tpu_custom_call" | custom-call | flops 6000000000 | bytes 2000000 | tf_op jit(solution)/shard_map/first/pallas_call | solution.py:263
  60.0 1.1 %middle.1 = (bf16[8,64,128]{2,1,0:T(8,128)(2,1)S(1)}, f32[128,128]{1,0:T(8,128)S(1)}) custom-call(s32[2,6]{1,0:T(2,128)S(1)} %copy-done.1, f32[1024,128]{1,0:T(8,128)S(1)} %get-tuple-element.10.state_ref, bf16[128,128]{1,0:T(8,128)(2,1)S(1)} %get-tuple-element.11.query_ref, bf16[8,128,128]{2,1,0:T(8,128)(2,1)S(1)} %all_to_all.21.blocks_ref), custom_call_target="tpu_custom_call" | custom-call | flops 2000000000 | bytes 2000000 | tf_op jit(solution)/shard_map/middle/pallas_call | solution.py:273
  61.1 0.0 copy-start
  61.2 3.6 %all-to-all-done.2.blocks_ref = bf16[8,128,128]{2,1,0:T(8,128)(2,1)S(1)} async-done(((bf16[8,128,128]{2,1,0:T(8,128)(2,1)}), bf16[8,128,128]{2,1,0:T(8,128)(2,1)S(1)}, u32[]{:S(2)}, u32[]{:S(2)}) %all-to-all-start.2) | async-done | bytes 262176 | tf_op jit(solution)/shard_map/all_to_all | solution.py:272
  64.7 0.9 %outer.1 = bf16[8,64,128]{2,1,0:T(8,128)(2,1)S(1)} custom-call(s32[2,6]{1,0:T(2,128)S(1)} %copy-done.1, f32[128,128]{1,0:T(8,128)S(1)} %get-tuple-element.12.merged_ref, bf16[16,128]{1,0:T(8,128)(2,1)S(1)} %get-tuple-element.13.query_ref, bf16[8,128,128]{2,1,0:T(8,128)(2,1)S(1)} %all-to-all-done.2.blocks_ref, ...), custom_call_target="tpu_custom_call", output_to_operand_aliasing={{}: (4, {})} | custom-call | tf_op jit(solution)/shard_map/outer/pallas_call | solution.py:282
  65.6 11.7 %all_to_all.22.blocks_ref = bf16[8,64,128]{2,1,0:T(8,128)(2,1)S(1)} all-to-all(bf16[8,64,128]{2,1,0:T(8,128)(2,1)S(1)} %outer.1), channel_id=1, replica_groups=mesh['grp'=8,'blk'=8,'set'=8] {'set'}, dimensions={0} | all-to-all | bytes 262144 | tf_op jit(solution)/shard_map/all_to_all | solution.py:289
  77.4 0.0 copy-done
  77.4 1.0 %project.1 = bf16[128,768]{1,0:T(8,128)(2,1)} custom-call(bf16[8,64,128]{2,1,0:T(8,128)(2,1)S(1)} %all_to_all.22.blocks_ref, bf16[384,768]{1,0:T(8,128)(2,1)S(1)} %copy-done), custom_call_target="tpu_custom_call" | custom-call | tf_op jit(solution)/shard_map/project/pallas_call | solution.py:290
Async XLA Ops:
  1.6 24.6 %copy-start.1 = (s32[2,6]{1,0:T(2,128)S(1)}, s32[2,6]{1,0:T(2,128)}, u32[]{:S(2)}) copy-start(s32[2,6]{1,0:T(2,128)} %offsets_ref.9) | copy-start | bytes 148
  43.5 21.2 %all-to-all-start.2 = ((bf16[8,128,128]{2,1,0:T(8,128)(2,1)}), bf16[8,128,128]{2,1,0:T(8,128)(2,1)S(1)}, u32[]{:S(2)}, u32[]{:S(2)}) async-start(bf16[8,128,128]{2,1,0:T(8,128)(2,1)} %pick_outer.1), calls=%async_computation.2 | async-start | bytes 524288 | tf_op jit(solution)/shard_map/all_to_all | solution.py:272
  61.1 16.2 %copy-start = (bf16[384,768]{1,0:T(8,128)(2,1)S(1)}, bf16[384,768]{1,0:T(8,128)(2,1)}, u32[]{:S(2)}) copy-start(bf16[384,768]{1,0:T(8,128)(2,1)} %weight_ref.1) | copy-start | bytes 1769476

commit v5 on v4

--- a/solution.py
+++ b/solution.py
@@ -16,6 +16,7 @@
 MARK = 1024.0
 EXP_SCALE = math.log2(math.e) / math.sqrt(HD)
 FAR = -1e30
+THIRD = 256
 F32 = jnp.float32
 BF16 = jnp.bfloat16
 
@@ -96,6 +97,10 @@
     return state / state[:, 32:33]
 
 
+def product_of(one, two):
+    return jnp.dot(one, two, preferred_element_type=F32)
+
+
 def pack_kernel(query_hbm, key_hbm, value_hbm, valid_hbm, out_ref, query_ref, key_ref, value_ref, valid_ref, sems):
     pairs = (
         (valid_hbm, valid_ref),
@@ -110,35 +115,60 @@
         out_ref[h] = jnp.zeros((FIRST_BLOCK, 2 * HD), BF16)
     for copy in copies:
         copy.wait()
-    square = (ROWS, ROWS)
-    valid = jnp.where(rows(square) == lanes(square), valid_ref[...].astype(F32), F32(0.0))
-    hidden = jnp.sum(valid, axis=1, keepdims=True) < F32(0.5)
+    square = (ROWS, 2 * HD)
+    row, lane = rows(square), lanes(square)
+    valid = jnp.where(row == lane, valid_ref[...].astype(F32), F32(0.0)).astype(BF16)
+    hidden = product_of(valid, jnp.ones(square, BF16)) < F32(0.5)
+    same_head = ((row // HD) == (lane // HD)).astype(F32).astype(BF16)
+    column = lane % HD
     half = ROWS // 2
-    lane = lanes((ROWS, HD))
-    for h in range(HEADS):
-        at = slice(h * HD, (h + 1) * HD)
+    for h in range(0, HEADS, 2):
+        at = slice(h * HD, (h + 2) * HD)
         key = key_ref[:, at].astype(F32)
-        own = jnp.sum(query_ref[:, at].astype(F32) * key, axis=1, keepdims=True)
+        product = query_ref[:, at].astype(F32) * key
+        upper = product.astype(BF16)
+        lower = (product - upper.astype(F32)).astype(BF16)
+        own = product_of(upper, same_head) + product_of(lower, same_head)
         high = own.astype(BF16).astype(F32)
         middle = (own - high).astype(BF16).astype(F32)
         rest = own - high - middle
-        code = jnp.where(lane == 0, F32(MARK), jnp.where(lane == 1, high, F32(0.0)))
-        code = jnp.where(lane == 2, middle, jnp.where(lane == 3, rest, code))
-        out_ref[h, 0:ROWS, 0:HD] = jnp.where(hidden, code, key).astype(BF16)
-        out_ref[h, 0:ROWS, HD : 2 * HD] = value_ref[:, at]
-        out_ref[h, ROWS:FIRST_BLOCK, 0:HD] = query_ref[0:half, at]
-        out_ref[h, ROWS:FIRST_BLOCK, HD : 2 * HD] = query_ref[half:ROWS, at]
-
-
-def pick_kernel(which, offsets_ref, blocks_ref, out_ref):
-    shift = shifts(offsets_ref)[which]
+        code = jnp.where(column == 0, F32(MARK), jnp.where(column == 1, high, F32(0.0)))
+        code = jnp.where(column == 2, middle, jnp.where(column == 3, rest, code))
+        coded = jnp.where(hidden, code, key).astype(BF16)
+        for part in range(2):
+            inner = slice(part * HD, (part + 1) * HD)
+            at = slice((h + part) * HD, (h + part + 1) * HD)
+            out_ref[h + part, 0:ROWS, 0:HD] = coded[:, inner]
+            out_ref[h + part, 0:ROWS, HD : 2 * HD] = value_ref[:, at]
+            out_ref[h + part, ROWS:FIRST_BLOCK, 0:HD] = query_ref[0:half, at]
+            out_ref[h + part, ROWS:FIRST_BLOCK, HD : 2 * HD] = query_ref[half:ROWS, at]
+
+
+def selector_of(shift):
+    shape = (ROWS // 8, ROWS)
+    return (lanes(shape) == shift + 8 * rows(shape)).astype(F32).astype(BF16)
+
+
+def pick_middle_kernel(offsets_ref, blocks_ref, out_ref):
+    selector = selector_of(shifts(offsets_ref)[0])
     count = ROWS // 8
-    shape = (count, ROWS)
-    selector = (lanes(shape) == shift + 8 * rows(shape)).astype(F32).astype(BF16)
     for c in range(PEERS):
-        picked = jnp.dot(selector, blocks_ref[c, 0:ROWS, :], preferred_element_type=F32).astype(BF16)
+        picked = product_of(selector, blocks_ref[c, 0:ROWS, :]).astype(BF16)
         for d in range(PEERS):
             out_ref[d, c * count : (c + 1) * count, :] = picked
+
+
+def pick_outer_kernel(offsets_ref, blocks_ref, out_hbm, picked_ref, sems):
+    selector = selector_of(shifts(offsets_ref)[1])
+    count = ROWS // 8
+    for c in range(PEERS):
+        picked = product_of(selector, blocks_ref[c, 0:ROWS, :]).astype(BF16)
+        picked_ref[c * count : (c + 1) * count, :] = picked
+    copies = [pltpu.make_async_copy(picked_ref, out_hbm.at[d], sems.at[d]) for d in range(PEERS)]
+    for copy in copies:
+        copy.start()
+    for copy in copies:
+        copy.wait()
 
 
 def first_kernel(offsets_ref, blocks_ref, state_ref, middle_ref, outer_ref, wide, narrow):
@@ -202,7 +232,7 @@
         out_ref[j, pl.ds(start, tile), :] = jnp.where(here, row, kept).astype(BF16)
 
 
-def project_kernel(blocks_ref, weight_ref, out_ref):
+def project_kernel(blocks_ref, weight_ref, out_hbm, out_ref, sems):
     half = ROWS // 2
     low = lanes((half, 2 * HD)) < HD
     tops, bottoms = [], []
@@ -213,11 +243,18 @@
     combined = jnp.concatenate(
         [jnp.concatenate(tops, axis=1), jnp.concatenate(bottoms, axis=1)], axis=0
     )
-    out_ref[...] = jnp.dot(combined, weight_ref[...], preferred_element_type=F32).astype(BF16)
-
-
-def call(kernel, name, out_shape, in_specs, scratch=(), flops=0, moved=0, aliases=None):
-    outs = jax.tree.map(lambda _: VMEM, out_shape)
+    copies = []
+    for n in range(out_ref.shape[1] // THIRD):
+        at = slice(n * THIRD, (n + 1) * THIRD)
+        out_ref[:, at] = product_of(combined, weight_ref[:, at]).astype(BF16)
+        copies.append(pltpu.make_async_copy(out_ref.at[:, at], out_hbm.at[:, at], sems.at[n]))
+        copies[-1].start()
+    for copy in copies:
+        copy.wait()
+
+
+def call(kernel, name, out_shape, in_specs, scratch=(), flops=0, moved=0, aliases=None, out_spec=VMEM):
+    outs = jax.tree.map(lambda _: out_spec, out_shape)
     return pl.pallas_call(
         kernel,
         name=name,
@@ -251,15 +288,10 @@
     )(*(pltpu.with_memory_space_constraint(a, pltpu.HBM) for a in given))
     dense = swap(packed, "set")
 
-    def pick(which, name, blocks):
-        return call(
-            functools.partial(pick_kernel, which),
-            name,
-            shaped(PEERS, ROWS, 2 * HD),
-            [VMEM, VMEM],
-        )(offsets, blocks)
-
-    middle_blocks = swap(pick(0, "pick_middle", dense), "blk")
+    middle_send = call(
+        pick_middle_kernel, "pick_middle", shaped(PEERS, ROWS, 2 * HD), [VMEM, VMEM]
+    )(offsets, dense)
+    middle_blocks = swap(middle_send, "blk")
     state, middle_query, outer_query = call(
         first_kernel,
         "first",
@@ -269,7 +301,15 @@
         flops=6_000_000_000,
         moved=2_000_000,
     )(offsets, dense)
-    outer_blocks = swap(pick(1, "pick_outer", middle_blocks), "grp")
+    outer_send = call(
+        pick_outer_kernel,
+        "pick_outer",
+        shaped(PEERS, ROWS, 2 * HD),
+        [VMEM, VMEM],
+        [pltpu.VMEM((ROWS, 2 * HD), BF16), pltpu.SemaphoreType.DMA((PEERS,))],
+        out_spec=HBM,
+    )(offsets, middle_blocks)
+    outer_blocks = swap(outer_send, "grp")
     before, merged = call(
         middle_kernel,
         "middle",
@@ -287,7 +327,15 @@
         aliases={4: 0},
     )(offsets, merged, outer_query, outer_blocks, before)
     home = swap(combined, "set")
-    return call(project_kernel, "project", shaped(ROWS, 768), [VMEM, VMEM])(home, w_out)
+    width = w_out.shape[1]
+    return call(
+        project_kernel,
+        "project",
+        shaped(ROWS, width),
+        [VMEM, VMEM],
+        [pltpu.VMEM((ROWS, width), BF16), pltpu.SemaphoreType.DMA((width // THIRD,))],
+        out_spec=HBM,
+    )(home, w_out)
 
 
 def solution(mesh):

time: 78.7 us -> 78.5 us (level)
  no operation moved by 1% of the time
where the time goes in v5:
time: 78.5 us; the launch traced here: 78.2 us
  blocking collectives  52.3 us (67%)
  starting transfers between devices  12.5 us (16%)
  Pallas kernels  9.72 us (12%)
  waiting for transfers between devices  3.58 us (5%)
    all_to_all x1, blocking collectives, per_device(): dense = swap(packed, 'set')  24.6 us
    all_to_all x1, blocking collectives, per_device(): middle_blocks = swap(middle_send, 'blk')  16 us
    all_to_all x1, starting transfers between devices, per_device(): outer_blocks = swap(outer_send, 'grp')  12.5 us
    all_to_all x1, blocking collectives, per_device(): home = swap(combined, 'set')  11.7 us
    pallas_call x1, Pallas kernels, per_device(): call(first_kernel, 'first', (shaped(PEERS * ROWS, 2 * HD, dtype=F32), sha...  3.96 us
    all_to_all x1, waiting for transfers between devices, per_device(): outer_blocks = swap(outer_send, 'grp')  3.58 us
  transfers between devices with their start and end apart: 1, of which 1 were waited for; matrix products, arithmetic and copies ran while one was open for 0% of the time, Pallas kernels for 7%

profile of v5, /device:TPU:1, one launch (start us, length us, event | category | flops | bytes accessed | tf_op | source)
XLA Modules:
  0.0 78.2 jit_solution(1079896024917508142)
XLA Ops:
  0.0 1.4 %pack.1 = bf16[8,192,128]{2,1,0:T(8,128)(2,1)S(1)} custom-call(bf16[128,384]{1,0:T(8,128)(2,1)} %query_hbm.1, bf16[128,384]{1,0:T(8,128)(2,1)} %key_hbm.1, bf16[128,384]{1,0:T(8,128)(2,1)} %value_hbm.1, s32[1,128]{1,0:T(1,128)} %bitcast.1), custom_call_target="tpu_custom_call" | custom-call | tf_op jit(solution)/shard_map/pack/pallas_call | solution.py:282
  1.4 0.0 copy-start.1
  1.4 24.6 %all_to_all.20.blocks_ref = bf16[8,192,128]{2,1,0:T(8,128)(2,1)S(1)} all-to-all(bf16[8,192,128]{2,1,0:T(8,128)(2,1)S(1)} %pack.1), channel_id=1, replica_groups=mesh['grp'=8,'blk'=8,'set'=8] {'set'}, dimensions={0} | all-to-all | bytes 786432 | tf_op jit(solution)/shard_map/all_to_all | solution.py:289
  26.0 0.0 copy-done.1
  26.0 0.3 pick_middle.1
  26.3 16.0 %all_to_all.21.blocks_ref = bf16[8,128,128]{2,1,0:T(8,128)(2,1)S(1)} all-to-all(bf16[8,128,128]{2,1,0:T(8,128)(2,1)S(1)} %pick_middle.1), channel_id=1, replica_groups=mesh['grp'=8,'blk'=8,'set'=8] {'blk'}, dimensions={0} | all-to-all | bytes 524288 | tf_op jit(solution)/shard_map/all_to_all | solution.py:294
  42.3 1.1 %pick_outer.1 = bf16[8,128,128]{2,1,0:T(8,128)(2,1)} custom-call(s32[2,6]{1,0:T(2,128)S(1)} %copy-done.1, bf16[8,128,128]{2,1,0:T(8,128)(2,1)S(1)} %all_to_all.21.blocks_ref), custom_call_target="tpu_custom_call" | custom-call | tf_op jit(solution)/shard_map/pick_outer/pallas_call | solution.py:304
  43.3 12.5 %all-to-all-start.2 = ((bf16[8,128,128]{2,1,0:T(8,128)(2,1)}), bf16[8,128,128]{2,1,0:T(8,128)(2,1)S(1)}, u32[]{:S(2)}, u32[]{:S(2)}) async-start(bf16[8,128,128]{2,1,0:T(8,128)(2,1)} %pick_outer.1), calls=%async_computation.2 | async-start | bytes 524288 | tf_op jit(solution)/shard_map/all_to_all | solution.py:312
  55.9 4.0 %first.1 = (f32[1024,128]{1,0:T(8,128)S(1)}, bf16[128,128]{1,0:T(8,128)(2,1)S(1)}, bf16[16,128]{1,0:T(8,128)(2,1)S(1)}) custom-call(s32[2,6]{1,0:T(2,128)S(1)} %copy-done.1, bf16[8,192,128]{2,1,0:T(8,128)(2,1)S(1)} %all_to_all.20.blocks_ref), custom_call_target="tpu_custom_call" | custom-call | flops 6000000000 | bytes 2000000 | tf_op jit(solution)/shard_map/first/pallas_call | solution.py:295
  59.8 1.1 %middle.1 = (bf16[8,64,128]{2,1,0:T(8,128)(2,1)S(1)}, f32[128,128]{1,0:T(8,128)S(1)}) custom-call(s32[2,6]{1,0:T(2,128)S(1)} %copy-done.1, f32[1024,128]{1,0:T(8,128)S(1)} %get-tuple-element.10.state_ref, bf16[128,128]{1,0:T(8,128)(2,1)S(1)} %get-tuple-element.11.query_ref, bf16[8,128,128]{2,1,0:T(8,128)(2,1)S(1)} %all_to_all.21.blocks_ref), custom_call_target="tpu_custom_call" | custom-call | flops 2000000000 | bytes 2000000 | tf_op jit(solution)/shard_map/middle/pallas_call | solution.py:313
  61.0 0.0 copy-start
  61.0 3.6 %all-to-all-done.2.blocks_ref = bf16[8,128,128]{2,1,0:T(8,128)(2,1)S(1)} async-done(((bf16[8,128,128]{2,1,0:T(8,128)(2,1)}), bf16[8,128,128]{2,1,0:T(8,128)(2,1)S(1)}, u32[]{:S(2)}, u32[]{:S(2)}) %all-to-all-start.2) | async-done | bytes 262176 | tf_op jit(solution)/shard_map/all_to_all | solution.py:312
  64.6 0.9 %outer.1 = bf16[8,64,128]{2,1,0:T(8,128)(2,1)S(1)} custom-call(s32[2,6]{1,0:T(2,128)S(1)} %copy-done.1, f32[128,128]{1,0:T(8,128)S(1)} %get-tuple-element.12.merged_ref, bf16[16,128]{1,0:T(8,128)(2,1)S(1)} %get-tuple-element.13.query_ref, bf16[8,128,128]{2,1,0:T(8,128)(2,1)S(1)} %all-to-all-done.2.blocks_ref, ...), custom_call_target="tpu_custom_call", output_to_operand_aliasing={{}: (4, {})} | custom-call | tf_op jit(solution)/shard_map/outer/pallas_call | solution.py:322
  65.5 11.7 %all_to_all.22.blocks_ref = bf16[8,64,128]{2,1,0:T(8,128)(2,1)S(1)} all-to-all(bf16[8,64,128]{2,1,0:T(8,128)(2,1)S(1)} %outer.1), channel_id=1, replica_groups=mesh['grp'=8,'blk'=8,'set'=8] {'set'}, dimensions={0} | all-to-all | bytes 262144 | tf_op jit(solution)/shard_map/all_to_all | solution.py:329
  77.2 0.0 copy-done
  77.2 1.0 %project.1 = bf16[128,768]{1,0:T(8,128)(2,1)} custom-call(bf16[8,64,128]{2,1,0:T(8,128)(2,1)S(1)} %all_to_all.22.blocks_ref, bf16[384,768]{1,0:T(8,128)(2,1)S(1)} %copy-done), custom_call_target="tpu_custom_call" | custom-call | tf_op jit(solution)/shard_map/project/pallas_call | solution.py:331
Async XLA Ops:
  1.4 24.6 %copy-start.1 = (s32[2,6]{1,0:T(2,128)S(1)}, s32[2,6]{1,0:T(2,128)}, u32[]{:S(2)}) copy-start(s32[2,6]{1,0:T(2,128)} %offsets_ref.9) | copy-start | bytes 148
  43.3 21.2 %all-to-all-start.2 = ((bf16[8,128,128]{2,1,0:T(8,128)(2,1)}), bf16[8,128,128]{2,1,0:T(8,128)(2,1)S(1)}, u32[]{:S(2)}, u32[]{:S(2)}) async-start(bf16[8,128,128]{2,1,0:T(8,128)(2,1)} %pick_outer.1), calls=%async_computation.2 | async-start | bytes 524288 | tf_op jit(solution)/shard_map/all_to_all | solution.py:312
  61.0 16.2 %copy-start = (bf16[384,768]{1,0:T(8,128)(2,1)S(1)}, bf16[384,768]{1,0:T(8,128)(2,1)}, u32[]{:S(2)}) copy-start(bf16[384,768]{1,0:T(8,128)(2,1)} %weight_ref.1) | copy-start | bytes 1769476

commit v6 on v5

--- a/solution.py
+++ b/solution.py
@@ -11,6 +11,8 @@
 HEADS = 6
 HD = 64
 PEERS = 8
+NEAR = 4
+HALF_HEADS = HEADS // 2
 ROWS = 128
 FIRST_BLOCK = ROWS + ROWS // 2
 MARK = 1024.0
@@ -32,16 +34,26 @@
     return lax.broadcasted_iota(jnp.int32, shape, len(shape) - 2)
 
 
-def my_head():
-    return jnp.minimum(lax.axis_index("set"), HEADS - 1)
-
-
-def shifts(offsets_ref):
+def my_half():
+    return lax.div(lax.axis_index("set"), NEAR)
+
+
+def head_at(half):
+    column = lax.rem(lax.axis_index("set"), NEAR)
+    return half * HALF_HEADS + jnp.minimum(column, HALF_HEADS - 1)
+
+
+def shifts(offsets_ref, head=None):
+    head = head_at(my_half()) if head is None else head
     both = offsets_ref[...].astype(F32)
-    both = jnp.where(lanes(both.shape) == my_head(), both, F32(0.0))
+    both = jnp.where(lanes(both.shape) == head, both, F32(0.0))
     middle = jnp.sum(both[0:1, :]).astype(jnp.int32)
     outer = jnp.sum(both[1:2, :]).astype(jnp.int32)
     return middle, (outer - middle) // 8
+
+
+def place_of(half):
+    return pl.multiple_of(jnp.where(half == my_half(), 0, FIRST_BLOCK), FIRST_BLOCK)
 
 
 def marks():
@@ -111,8 +123,8 @@
     copies = [pltpu.make_async_copy(a, b, sems.at[i]) for i, (a, b) in enumerate(pairs)]
     for copy in copies:
         copy.start()
-    for h in range(HEADS, PEERS):
-        out_ref[h] = jnp.zeros((FIRST_BLOCK, 2 * HD), BF16)
+    for c in range(HALF_HEADS, NEAR):
+        out_ref[c] = jnp.zeros((2 * FIRST_BLOCK, 2 * HD), BF16)
     for copy in copies:
         copy.wait()
     square = (ROWS, 2 * HD)
@@ -136,12 +148,16 @@
         code = jnp.where(column == 2, middle, jnp.where(column == 3, rest, code))
         coded = jnp.where(hidden, code, key).astype(BF16)
         for part in range(2):
+            head = h + part
             inner = slice(part * HD, (part + 1) * HD)
-            at = slice((h + part) * HD, (h + part + 1) * HD)
-            out_ref[h + part, 0:ROWS, 0:HD] = coded[:, inner]
-            out_ref[h + part, 0:ROWS, HD : 2 * HD] = value_ref[:, at]
-            out_ref[h + part, ROWS:FIRST_BLOCK, 0:HD] = query_ref[0:half, at]
-            out_ref[h + part, ROWS:FIRST_BLOCK, HD : 2 * HD] = query_ref[half:ROWS, at]
+            at = slice(head * HD, (head + 1) * HD)
+            to = head % HALF_HEADS
+            start = place_of(head // HALF_HEADS)
+            whole, ends = pl.ds(start, ROWS), pl.ds(start + ROWS, half)
+            out_ref[to, whole, 0:HD] = coded[:, inner]
+            out_ref[to, whole, HD : 2 * HD] = value_ref[:, at]
+            out_ref[to, ends, 0:HD] = query_ref[0:half, at]
+            out_ref[to, ends, HD : 2 * HD] = query_ref[half:ROWS, at]
 
 
 def selector_of(shift):
@@ -149,13 +165,17 @@
     return (lanes(shape) == shift + 8 * rows(shape)).astype(F32).astype(BF16)
 
 
-def pick_middle_kernel(offsets_ref, blocks_ref, out_ref):
-    selector = selector_of(shifts(offsets_ref)[0])
+def pick_middle_kernel(offsets_ref, blocks_ref, out_ref, cross_ref):
     count = ROWS // 8
-    for c in range(PEERS):
-        picked = product_of(selector, blocks_ref[c, 0:ROWS, :]).astype(BF16)
-        for d in range(PEERS):
-            out_ref[d, c * count : (c + 1) * count, :] = picked
+    for half in range(2):
+        selector = selector_of(shifts(offsets_ref, head_at(half))[0])
+        start = place_of(half)
+        for c in range(NEAR):
+            picked = product_of(selector, blocks_ref[c, pl.ds(start, ROWS), :]).astype(BF16)
+            for d in range(PEERS):
+                out_ref[2 * d + half, c * count : (c + 1) * count, :] = picked
+    for c in range(NEAR):
+        cross_ref[c] = blocks_ref[c, FIRST_BLOCK : 2 * FIRST_BLOCK, :]
 
 
 def pick_outer_kernel(offsets_ref, blocks_ref, out_hbm, picked_ref, sems):
@@ -171,8 +191,14 @@
         copy.wait()
 
 
-def first_kernel(offsets_ref, blocks_ref, state_ref, middle_ref, outer_ref, wide, narrow):
+def first_kernel(
+    offsets_ref, near_ref, far_ref, state_ref, middle_ref, outer_ref, blocks_ref, wide, narrow
+):
     middle, stride = shifts(offsets_ref)
+    mine = my_half()
+    for c in range(NEAR):
+        blocks_ref[mine * NEAR + c] = near_ref[c, 0:FIRST_BLOCK, :]
+        blocks_ref[(1 - mine) * NEAR + c] = far_ref[c]
     half = ROWS // 2
     low = lanes((half, 2 * HD)) < HD
     diagonal = rows((ROWS, ROWS)) == lanes((ROWS, ROWS))
@@ -236,8 +262,9 @@
     half = ROWS // 2
     low = lanes((half, 2 * HD)) < HD
     tops, bottoms = [], []
+    places = [h // HALF_HEADS * NEAR + h % HALF_HEADS for h in range(HEADS)]
     for h in range(0, HEADS, 2):
-        one, two = blocks_ref[h].astype(F32), blocks_ref[h + 1].astype(F32)
+        one, two = blocks_ref[places[h]].astype(F32), blocks_ref[places[h + 1]].astype(F32)
         tops.append(jnp.where(low, one, pltpu.roll(two, HD, 1)).astype(BF16))
         bottoms.append(jnp.where(low, pltpu.roll(one, HD, 1), two).astype(BF16))
     combined = jnp.concatenate(
@@ -282,25 +309,33 @@
     packed = call(
         pack_kernel,
         "pack",
-        shaped(PEERS, FIRST_BLOCK, 2 * HD),
+        shaped(NEAR, 2 * FIRST_BLOCK, 2 * HD),
         [HBM] * 4,
         [whole, whole, whole, pltpu.VMEM((1, ROWS), jnp.int32), pltpu.SemaphoreType.DMA((4,))],
     )(*(pltpu.with_memory_space_constraint(a, pltpu.HBM) for a in given))
-    dense = swap(packed, "set")
-
-    middle_send = call(
-        pick_middle_kernel, "pick_middle", shaped(PEERS, ROWS, 2 * HD), [VMEM, VMEM]
-    )(offsets, dense)
-    middle_blocks = swap(middle_send, "blk")
+    near_groups = [[z * NEAR + x for x in range(NEAR)] for z in range(2)]
+    near = swap(packed, "set", axis_index_groups=near_groups)
+    middle_send, cross = call(
+        pick_middle_kernel,
+        "pick_middle",
+        (shaped(2 * PEERS, ROWS // 2, 2 * HD), shaped(NEAR, FIRST_BLOCK, 2 * HD)),
+        [VMEM, VMEM],
+    )(offsets, near)
+    middle_groups = [
+        [b * PEERS + z * NEAR + x for b in range(PEERS) for z in range(2)] for x in range(NEAR)
+    ]
+    middle_blocks = swap(middle_send, ("blk", "set"), axis_index_groups=middle_groups)
+    middle_blocks = middle_blocks.reshape(PEERS, ROWS, 2 * HD)
+    far = lax.ppermute(cross, "set", [(i, (i + NEAR) % PEERS) for i in range(PEERS)])
     state, middle_query, outer_query = call(
         first_kernel,
         "first",
         (shaped(PEERS * ROWS, 2 * HD, dtype=F32), shaped(ROWS, 2 * HD), shaped(ROWS // 8, 2 * HD)),
-        [VMEM, VMEM],
-        [wide, narrow],
+        [VMEM, VMEM, VMEM],
+        [pltpu.VMEM((PEERS, FIRST_BLOCK, 2 * HD), BF16), wide, narrow],
         flops=6_000_000_000,
         moved=2_000_000,
-    )(offsets, dense)
+    )(offsets, near, far)
     outer_send = call(
         pick_outer_kernel,
         "pick_outer",

time: 78.5 us -> 75.1 us (0.957)
  blocking collectives: 52.3 us -> 22.6 us
  starting transfers between devices: 12.5 us -> 31.3 us
  waiting for transfers between devices: 3.58 us -> 10.2 us
    all_to_all x2 -> x1, blocking collectives: 40.6 us -> 10.9 us  [per_device(): near = swap(packed, 'set', axis_index_groups=near_groups)]
    all_to_all x0 -> x1, starting transfers between devices: none -> 16.3 us  [per_device(): swap(middle_send, ('blk', 'set'), axis_index_groups=middle_groups)]
    ppermute x0 -> x1, starting transfers between devices: none -> 7.17 us  [per_device(): lax.ppermute(cross, 'set', [(i, (i + NEAR) % PEERS) for i in range(PEERS)])]
    all_to_all x0 -> x1, waiting for transfers between devices: none -> 6.63 us  [per_device(): swap(middle_send, ('blk', 'set'), axis_index_groups=middle_groups)]
    all_to_all x1, starting transfers between devices: 12.5 us -> 7.83 us  [per_device(): outer_blocks = swap(outer_send, 'grp')]
  transfers between devices with their start and end apart: 1 -> 3, of which waited for: 1 -> 2; matrix products, arithmetic and copies ran while one was open for 0% -> 0% of each run, Pallas kernels for 7% -> 8%
where the time goes in v6:
time: 75.1 us; the launch traced here: 74.6 us
  starting transfers between devices  31.3 us (42%)
  blocking collectives  22.6 us (30%)
  Pallas kernels  10.5 us (14%)
  waiting for transfers between devices  10.2 us (14%)
    all_to_all x1, starting transfers between devices, per_device(): swap(middle_send, ('blk', 'set'), axis_index_groups=middle_groups)  16.3 us
    all_to_all x1, blocking collectives, per_device(): home = swap(combined, 'set')  11.7 us
    all_to_all x1, blocking collectives, per_device(): near = swap(packed, 'set', axis_index_groups=near_groups)  10.9 us
    all_to_all x1, starting transfers between devices, per_device(): outer_blocks = swap(outer_send, 'grp')  7.83 us
    ppermute x1, starting transfers between devices, per_device(): lax.ppermute(cross, 'set', [(i, (i + NEAR) % PEERS) for i in range(PEERS)])  7.17 us
    all_to_all x1, waiting for transfers between devices, per_device(): swap(middle_send, ('blk', 'set'), axis_index_groups=middle_groups)  6.63 us
    pallas_call x1, Pallas kernels, per_device(): call(first_kernel, 'first', (shaped(PEERS * ROWS, 2 * HD, dtype=F32), sha...  4 us
    all_to_all x1, waiting for transfers between devices, per_device(): outer_blocks = swap(outer_send, 'grp')  3.54 us
  transfers between devices with their start and end apart: 3, of which 2 were waited for; matrix products, arithmetic and copies ran while one was open for 0% of the time, Pallas kernels for 8%

profile of v6, /device:TPU:1, one launch (start us, length us, event | category | flops | bytes accessed | tf_op | source)
XLA Modules:
  0.0 74.6 jit_solution(9507807369920904125)
XLA Ops:
  0.0 1.4 %pack.1 = bf16[4,384,128]{2,1,0:T(8,128)(2,1)S(1)} custom-call(bf16[128,384]{1,0:T(8,128)(2,1)} %query_hbm.1, bf16[128,384]{1,0:T(8,128)(2,1)} %key_hbm.1, bf16[128,384]{1,0:T(8,128)(2,1)} %value_hbm.1, s32[1,128]{1,0:T(1,128)} %bitcast.4), custom_call_target="tpu_custom_call" | custom-call | tf_op jit(solution)/shard_map/pack/pallas_call | solution.py:309
  1.4 0.0 copy-start.1
  1.4 10.9 %all_to_all.20.blocks_ref.near_ref = bf16[4,384,128]{2,1,0:T(8,128)(2,1)S(1)} all-to-all(bf16[4,384,128]{2,1,0:T(8,128)(2,1)S(1)} %pack.1), channel_id=1, replica_groups={{0,1,2,3},{4,5,6,7},{8,9,10,11},{12,13,14,15},{16,17,18,19},{20,21,22,2..., dimensions={0} | all-to-all | bytes 786432 | tf_op jit(solution)/shard_map/all_to_all | solution.py:317
  12.3 0.0 copy-done.1
  12.3 1.0 %pick_middle.1 = (bf16[16,64,128]{2,1,0:T(8,128)(2,1)}, bf16[4,192,128]{2,1,0:T(8,128)(2,1)S(1)}) custom-call(s32[2,6]{1,0:T(2,128)S(1)} %copy-done.1, bf16[4,384,128]{2,1,0:T(8,128)(2,1)S(1)} %all_to_all.20.blocks_ref.near_ref), custom_call_target="tpu_custom_call" | custom-call | tf_op jit(solution)/shard_map/pick_middle/pallas_call | solution.py:318
  13.3 16.3 %all-to-all-start.1 = ((bf16[16,64,128]{2,1,0:T(8,128)(2,1)}), bf16[16,64,128]{2,1,0:T(8,128)(2,1)S(1)}, u32[]{:S(2)}, u32[]{:S(2)}) async-start(bf16[16,64,128]{2,1,0:T(8,128)(2,1)} %get-tuple-element.15), calls=%async_computation.1 | async-start | bytes 524288 | tf_op jit(solution)/shard_map/all_to_all | solution.py:327
  29.6 7.2 %collective-permute-start = (bf16[4,192,128]{2,1,0:T(8,128)(2,1)S(1)}, bf16[4,192,128]{2,1,0:T(8,128)(2,1)S(1)}, u32[]{:S(2)}, u32[]{:S(2)}) collective-permute-start(bf16[4,192,128]{2,1,0:T(8,128)(2,1)S(1)} %get-tuple-element.12), channel_id=1, source_target_pairs={{0,4},{1,5},{2,6},{3,7},{4,0},{5,1},{6,2},{7,3},{8,12},{9,13},{10,... | collective-permute-start | bytes 589832 | tf_op jit(solution)/shard_map/ppermute | solution.py:329
  36.8 6.6 %all-to-all-done.1 = bf16[16,64,128]{2,1,0:T(8,128)(2,1)S(1)} async-done(((bf16[16,64,128]{2,1,0:T(8,128)(2,1)}), bf16[16,64,128]{2,1,0:T(8,128)(2,1)S(1)}, u32[]{:S(2)}, u32[]{:S(2)}) %all-to-all-start.1) | async-done | bytes 262176 | tf_op jit(solution)/shard_map/all_to_all | solution.py:327
  43.4 1.1 %pick_outer.1 = bf16[8,128,128]{2,1,0:T(8,128)(2,1)} custom-call(s32[2,6]{1,0:T(2,128)S(1)} %copy-done.1, bf16[8,128,128]{2,1,0:T(8,128)(2,1)S(1)} %bitcast.2), custom_call_target="tpu_custom_call" | custom-call | tf_op jit(solution)/shard_map/pick_outer/pallas_call | solution.py:339
  44.5 7.8 %all-to-all-start.2 = ((bf16[8,128,128]{2,1,0:T(8,128)(2,1)}), bf16[8,128,128]{2,1,0:T(8,128)(2,1)S(1)}, u32[]{:S(2)}, u32[]{:S(2)}) async-start(bf16[8,128,128]{2,1,0:T(8,128)(2,1)} %pick_outer.1), calls=%async_computation.2 | async-start | bytes 524288 | tf_op jit(solution)/shard_map/all_to_all | solution.py:347
  52.3 0.0 collective-permute-done.far_ref
  52.3 4.0 %first.1 = (f32[1024,128]{1,0:T(8,128)S(1)}, bf16[128,128]{1,0:T(8,128)(2,1)S(1)}, bf16[16,128]{1,0:T(8,128)(2,1)S(1)}) custom-call(s32[2,6]{1,0:T(2,128)S(1)} %copy-done.1, bf16[4,384,128]{2,1,0:T(8,128)(2,1)S(1)} %all_to_all.20.blocks_ref.near_ref, bf16[4,192,128]{2,1,0:T(8,128)(2,1)S(1)} %collective-permute-done.far_ref), custom_call_target="tpu_custom_call" | custom-call | flops 6000000000 | bytes 2000000 | tf_op jit(solution)/shard_map/first/pallas_call | solution.py:330
  56.3 1.1 %middle.1 = (bf16[8,64,128]{2,1,0:T(8,128)(2,1)S(1)}, f32[128,128]{1,0:T(8,128)S(1)}) custom-call(s32[2,6]{1,0:T(2,128)S(1)} %copy-done.1, f32[1024,128]{1,0:T(8,128)S(1)} %get-tuple-element.13.state_ref, bf16[128,128]{1,0:T(8,128)(2,1)S(1)} %get-tuple-element.14.query_ref, bf16[8,128,128]{2,1,0:T(8,128)(2,1)S(1)} %bitcast.3), custom_call_target="tpu_custom_call" | custom-call | flops 2000000000 | bytes 2000000 | tf_op jit(solution)/shard_map/middle/pallas_call | solution.py:348
  57.5 0.0 copy-start
  57.5 3.5 %all-to-all-done.2.blocks_ref = bf16[8,128,128]{2,1,0:T(8,128)(2,1)S(1)} async-done(((bf16[8,128,128]{2,1,0:T(8,128)(2,1)}), bf16[8,128,128]{2,1,0:T(8,128)(2,1)S(1)}, u32[]{:S(2)}, u32[]{:S(2)}) %all-to-all-start.2) | async-done | bytes 262176 | tf_op jit(solution)/shard_map/all_to_all | solution.py:347
  61.0 0.9 %outer.1 = bf16[8,64,128]{2,1,0:T(8,128)(2,1)S(1)} custom-call(s32[2,6]{1,0:T(2,128)S(1)} %copy-done.1, f32[128,128]{1,0:T(8,128)S(1)} %get-tuple-element.16.merged_ref, bf16[16,128]{1,0:T(8,128)(2,1)S(1)} %get-tuple-element.17.query_ref, bf16[8,128,128]{2,1,0:T(8,128)(2,1)S(1)} %all-to-all-done.2.blocks_ref, ...), custom_call_target="tpu_custom_call", output_to_operand_aliasing={{}: (4, {})} | custom-call | tf_op jit(solution)/shard_map/outer/pallas_call | solution.py:357
  61.9 11.7 %all_to_all.21.blocks_ref = bf16[8,64,128]{2,1,0:T(8,128)(2,1)S(1)} all-to-all(bf16[8,64,128]{2,1,0:T(8,128)(2,1)S(1)} %outer.1), channel_id=1, replica_groups=mesh['grp'=8,'blk'=8,'set'=8] {'set'}, dimensions={0} | all-to-all | bytes 262144 | tf_op jit(solution)/shard_map/all_to_all | solution.py:364
  73.6 0.0 copy-done
  73.6 1.0 %project.1 = bf16[128,768]{1,0:T(8,128)(2,1)} custom-call(bf16[8,64,128]{2,1,0:T(8,128)(2,1)S(1)} %all_to_all.21.blocks_ref, bf16[384,768]{1,0:T(8,128)(2,1)S(1)} %copy-done), custom_call_target="tpu_custom_call" | custom-call | tf_op jit(solution)/shard_map/project/pallas_call | solution.py:366
Async XLA Ops:
  1.4 10.9 %copy-start.1 = (s32[2,6]{1,0:T(2,128)S(1)}, s32[2,6]{1,0:T(2,128)}, u32[]{:S(2)}) copy-start(s32[2,6]{1,0:T(2,128)} %offsets_ref.9) | copy-start | bytes 148
  13.3 30.1 %all-to-all-start.1 = ((bf16[16,64,128]{2,1,0:T(8,128)(2,1)}), bf16[16,64,128]{2,1,0:T(8,128)(2,1)S(1)}, u32[]{:S(2)}, u32[]{:S(2)}) async-start(bf16[16,64,128]{2,1,0:T(8,128)(2,1)} %get-tuple-element.15), calls=%async_computation.1 | async-start | bytes 524288 | tf_op jit(solution)/shard_map/all_to_all | solution.py:327
  29.6 22.7 %collective-permute-start = (bf16[4,192,128]{2,1,0:T(8,128)(2,1)S(1)}, bf16[4,192,128]{2,1,0:T(8,128)(2,1)S(1)}, u32[]{:S(2)}, u32[]{:S(2)}) collective-permute-start(bf16[4,192,128]{2,1,0:T(8,128)(2,1)S(1)} %get-tuple-element.12), channel_id=1, source_target_pairs={{0,4},{1,5},{2,6},{3,7},{4,0},{5,1},{6,2},{7,3},{8,12},{9,13},{10,... | collective-permute-start | bytes 589832 | tf_op jit(solution)/shard_map/ppermute | solution.py:329
  44.5 16.5 %all-to-all-start.2 = ((bf16[8,128,128]{2,1,0:T(8,128)(2,1)}), bf16[8,128,128]{2,1,0:T(8,128)(2,1)S(1)}, u32[]{:S(2)}, u32[]{:S(2)}) async-start(bf16[8,128,128]{2,1,0:T(8,128)(2,1)} %pick_outer.1), calls=%async_computation.2 | async-start | bytes 524288 | tf_op jit(solution)/shard_map/all_to_all | solution.py:347
  57.5 16.2 %copy-start = (bf16[384,768]{1,0:T(8,128)(2,1)S(1)}, bf16[384,768]{1,0:T(8,128)(2,1)}, u32[]{:S(2)}) copy-start(bf16[384,768]{1,0:T(8,128)(2,1)} %weight_ref.1) | copy-start | bytes 1769476

commit v7 on v6

--- a/solution.py
+++ b/solution.py
@@ -165,15 +165,27 @@
     return (lanes(shape) == shift + 8 * rows(shape)).astype(F32).astype(BF16)
 
 
-def pick_middle_kernel(offsets_ref, blocks_ref, out_ref, cross_ref):
+def pick_middle_kernel(offsets_ref, blocks_ref, own_ref, partner_ref):
     count = ROWS // 8
-    for half in range(2):
+    for out_ref, half, start in (
+        (own_ref, my_half(), 0),
+        (partner_ref, 1 - my_half(), FIRST_BLOCK),
+    ):
         selector = selector_of(shifts(offsets_ref, head_at(half))[0])
-        start = place_of(half)
         for c in range(NEAR):
-            picked = product_of(selector, blocks_ref[c, pl.ds(start, ROWS), :]).astype(BF16)
-            for d in range(PEERS):
-                out_ref[2 * d + half, c * count : (c + 1) * count, :] = picked
+            rows_of = blocks_ref[c, start : start + ROWS, :]
+            out_ref[c * count : (c + 1) * count, :] = product_of(selector, rows_of).astype(BF16)
+
+
+def join_kernel(own_ref, partner_ref, blocks_ref, out_ref, cross_ref):
+    count = ROWS // 2
+    mine = my_half()
+    own, other = own_ref[...].astype(F32), partner_ref[...].astype(F32)
+    first = jnp.where(mine == 0, own, other).astype(BF16)
+    second = jnp.where(mine == 0, other, own).astype(BF16)
+    for d in range(PEERS):
+        out_ref[d, 0:count, :] = first
+        out_ref[d, count:ROWS, :] = second
     for c in range(NEAR):
         cross_ref[c] = blocks_ref[c, FIRST_BLOCK : 2 * FIRST_BLOCK, :]
 
@@ -315,18 +327,19 @@
     )(*(pltpu.with_memory_space_constraint(a, pltpu.HBM) for a in given))
     near_groups = [[z * NEAR + x for x in range(NEAR)] for z in range(2)]
     near = swap(packed, "set", axis_index_groups=near_groups)
+    partners = [(i, (i + NEAR) % PEERS) for i in range(PEERS)]
+    half_rows = shaped(ROWS // 2, 2 * HD)
+    own_rows, partner_rows = call(
+        pick_middle_kernel, "pick_middle", (half_rows, half_rows), [VMEM, VMEM]
+    )(offsets, near)
     middle_send, cross = call(
-        pick_middle_kernel,
-        "pick_middle",
-        (shaped(2 * PEERS, ROWS // 2, 2 * HD), shaped(NEAR, FIRST_BLOCK, 2 * HD)),
-        [VMEM, VMEM],
-    )(offsets, near)
-    middle_groups = [
-        [b * PEERS + z * NEAR + x for b in range(PEERS) for z in range(2)] for x in range(NEAR)
-    ]
-    middle_blocks = swap(middle_send, ("blk", "set"), axis_index_groups=middle_groups)
-    middle_blocks = middle_blocks.reshape(PEERS, ROWS, 2 * HD)
-    far = lax.ppermute(cross, "set", [(i, (i + NEAR) % PEERS) for i in range(PEERS)])
+        join_kernel,
+        "join",
+        (shaped(PEERS, ROWS, 2 * HD), shaped(NEAR, FIRST_BLOCK, 2 * HD)),
+        [VMEM, VMEM, VMEM],
+    )(own_rows, lax.ppermute(partner_rows, "set", partners), near)
+    middle_blocks = swap(middle_send, "blk")
+    far = lax.ppermute(cross, "set", partners)
     state, middle_query, outer_query = call(
         first_kernel,
         "first",

time: 75.1 us -> 79.7 us (1.061)
  blocking collectives: 22.6 us -> 27.5 us
  waiting for transfers between devices: 10.2 us -> 6.64 us
  starting transfers between devices: 31.3 us -> 34.5 us
    ppermute x1 -> x2, starting transfers between devices: 7.17 us -> 19 us  [the longest x1 11.6 us: per_device(): lax.ppermute(partner_rows, 'set', partners)]
    all_to_all x1, starting transfers between devices: 16.3 us -> 6.82 us  [per_device(): middle_blocks = swap(middle_send, 'blk')]
    all_to_all x1, blocking collectives: 11.7 us -> 16.7 us  [per_device(): home = swap(combined, 'set')]
    all_to_all x1, waiting for transfers between devices: 6.63 us -> 1.97 us  [per_device(): middle_blocks = swap(middle_send, 'blk')]
    ppermute x1 -> x2, waiting for transfers between devices: 0.01 us -> 1.13 us  [the longest x1 1.13 us: per_device(): lax.ppermute(partner_rows, 'set', partners)]
    all_to_all x1, starting transfers between devices: 7.83 us -> 8.65 us  [per_device(): outer_blocks = swap(outer_send, 'grp')]
  transfers between devices with their start and end apart: 3 -> 4, of which waited for: 2 -> 3; matrix products, arithmetic and copies ran while one was open for 0% -> 0% of each run, Pallas kernels for 8% -> 8%
where the time goes in v7:
time: 79.7 us; the launch traced here: 79.2 us
  starting transfers between devices  34.5 us (43%)
  blocking collectives  27.5 us (35%)
  Pallas kernels  10.5 us (13%)
  waiting for transfers between devices  6.64 us (8%)
    all_to_all x1, blocking collectives, per_device(): home = swap(combined, 'set')  16.7 us
    ppermute x1, starting transfers between devices, per_device(): lax.ppermute(partner_rows, 'set', partners)  11.6 us
    all_to_all x1, blocking collectives, per_device(): near = swap(packed, 'set', axis_index_groups=near_groups)  10.9 us
    all_to_all x1, starting transfers between devices, per_device(): outer_blocks = swap(outer_send, 'grp')  8.65 us
    ppermute x1, starting transfers between devices, per_device(): far = lax.ppermute(cross, 'set', partners)  7.42 us
    all_to_all x1, starting transfers between devices, per_device(): middle_blocks = swap(middle_send, 'blk')  6.82 us
    pallas_call x1, Pallas kernels, per_device(): call(first_kernel, 'first', (shaped(PEERS * ROWS, 2 * HD, dtype=F32), sha...  4 us
    all_to_all x1, waiting for transfers between devices, per_device(): outer_blocks = swap(outer_send, 'grp')  3.54 us
  transfers between devices with their start and end apart: 4, of which 3 were waited for; matrix products, arithmetic and copies ran while one was open for 0% of the time, Pallas kernels for 8%

profile of v7, /device:TPU:1, one launch (start us, length us, event | category | flops | bytes accessed | tf_op | source)
XLA Modules:
  0.0 79.2 jit_solution(9236912660128399631)
XLA Ops:
  0.0 1.4 %pack.1 = bf16[4,384,128]{2,1,0:T(8,128)(2,1)S(1)} custom-call(bf16[128,384]{1,0:T(8,128)(2,1)} %query_hbm.1, bf16[128,384]{1,0:T(8,128)(2,1)} %key_hbm.1, bf16[128,384]{1,0:T(8,128)(2,1)} %value_hbm.1, s32[1,128]{1,0:T(1,128)} %bitcast.1), custom_call_target="tpu_custom_call" | custom-call | tf_op jit(solution)/shard_map/pack/pallas_call | solution.py:321
  1.4 0.0 copy-start.1
  1.4 10.9 %all_to_all.20.blocks_ref.near_ref = bf16[4,384,128]{2,1,0:T(8,128)(2,1)S(1)} all-to-all(bf16[4,384,128]{2,1,0:T(8,128)(2,1)S(1)} %pack.1), channel_id=1, replica_groups={{0,1,2,3},{4,5,6,7},{8,9,10,11},{12,13,14,15},{16,17,18,19},{20,21,22,2..., dimensions={0} | all-to-all | bytes 786432 | tf_op jit(solution)/shard_map/all_to_all | solution.py:329
  12.3 0.0 copy-done.1
  12.3 0.3 pick_middle.1
  12.6 11.6 %collective-permute-start = (bf16[64,128]{1,0:T(8,128)(2,1)S(1)}, bf16[64,128]{1,0:T(8,128)(2,1)S(1)}, u32[]{:S(2)}, u32[]{:S(2)}) collective-permute-start(bf16[64,128]{1,0:T(8,128)(2,1)S(1)} %get-tuple-element.15), channel_id=1, source_target_pairs={{0,4},{1,5},{2,6},{3,7},{4,0},{5,1},{6,2},{7,3},{8,12},{9,13},{10,... | collective-permute-start | bytes 49160 | tf_op jit(solution)/shard_map/ppermute | solution.py:340
  24.1 1.1 %collective-permute-done.partner_ref = bf16[64,128]{1,0:T(8,128)(2,1)S(1)} collective-permute-done((bf16[64,128]{1,0:T(8,128)(2,1)S(1)}, bf16[64,128]{1,0:T(8,128)(2,1)S(1)}, u32[]{:S(2)}, u32[]{:S(2)}) %collective-permute-start) | collective-permute-done | bytes 16416 | tf_op jit(solution)/shard_map/ppermute | solution.py:340
  25.3 0.7 join.1
  26.0 6.8 %all-to-all-start.1 = ((bf16[8,128,128]{2,1,0:T(8,128)(2,1)}), bf16[8,128,128]{2,1,0:T(8,128)(2,1)S(1)}, u32[]{:S(2)}, u32[]{:S(2)}) async-start(bf16[8,128,128]{2,1,0:T(8,128)(2,1)} %get-tuple-element.19), calls=%async_computation.1 | async-start | bytes 524288 | tf_op jit(solution)/shard_map/all_to_all | solution.py:341
  32.8 7.4 %collective-permute-start.1 = (bf16[4,192,128]{2,1,0:T(8,128)(2,1)S(1)}, bf16[4,192,128]{2,1,0:T(8,128)(2,1)S(1)}, u32[]{:S(2)}, u32[]{:S(2)}) collective-permute-start(bf16[4,192,128]{2,1,0:T(8,128)(2,1)S(1)} %get-tuple-element.16), channel_id=1, source_target_pairs={{0,4},{1,5},{2,6},{3,7},{4,0},{5,1},{6,2},{7,3},{8,12},{9,13},{10,... | collective-permute-start | bytes 589832 | tf_op jit(solution)/shard_map/ppermute | solution.py:342
  40.3 2.0 %all-to-all-done.1.blocks_ref = bf16[8,128,128]{2,1,0:T(8,128)(2,1)S(1)} async-done(((bf16[8,128,128]{2,1,0:T(8,128)(2,1)}), bf16[8,128,128]{2,1,0:T(8,128)(2,1)S(1)}, u32[]{:S(2)}, u32[]{:S(2)}) %all-to-all-start.1) | async-done | bytes 262176 | tf_op jit(solution)/shard_map/all_to_all | solution.py:341
  42.2 1.1 %pick_outer.1 = bf16[8,128,128]{2,1,0:T(8,128)(2,1)} custom-call(s32[2,6]{1,0:T(2,128)S(1)} %copy-done.1, bf16[8,128,128]{2,1,0:T(8,128)(2,1)S(1)} %all-to-all-done.1.blocks_ref), custom_call_target="tpu_custom_call" | custom-call | tf_op jit(solution)/shard_map/pick_outer/pallas_call | solution.py:352
  43.3 8.7 %all-to-all-start.2 = ((bf16[8,128,128]{2,1,0:T(8,128)(2,1)}), bf16[8,128,128]{2,1,0:T(8,128)(2,1)S(1)}, u32[]{:S(2)}, u32[]{:S(2)}) async-start(bf16[8,128,128]{2,1,0:T(8,128)(2,1)} %pick_outer.1), calls=%async_computation.2 | async-start | bytes 524288 | tf_op jit(solution)/shard_map/all_to_all | solution.py:360
  52.0 0.0 collective-permute-done.1.far_ref
  52.0 4.0 %first.1 = (f32[1024,128]{1,0:T(8,128)S(1)}, bf16[128,128]{1,0:T(8,128)(2,1)S(1)}, bf16[16,128]{1,0:T(8,128)(2,1)S(1)}) custom-call(s32[2,6]{1,0:T(2,128)S(1)} %copy-done.1, bf16[4,384,128]{2,1,0:T(8,128)(2,1)S(1)} %all_to_all.20.blocks_ref.near_ref, bf16[4,192,128]{2,1,0:T(8,128)(2,1)S(1)} %collective-permute-done.1.far_ref), custom_call_target="tpu_custom_call" | custom-call | flops 6000000000 | bytes 2000000 | tf_op jit(solution)/shard_map/first/pallas_call | solution.py:343
  56.0 1.1 %middle.1 = (bf16[8,64,128]{2,1,0:T(8,128)(2,1)S(1)}, f32[128,128]{1,0:T(8,128)S(1)}) custom-call(s32[2,6]{1,0:T(2,128)S(1)} %copy-done.1, f32[1024,128]{1,0:T(8,128)S(1)} %get-tuple-element.17.state_ref, bf16[128,128]{1,0:T(8,128)(2,1)S(1)} %get-tuple-element.18.query_ref, bf16[8,128,128]{2,1,0:T(8,128)(2,1)S(1)} %all-to-all-done.1.blocks_ref), custom_call_target="tpu_custom_call" | custom-call | flops 2000000000 | bytes 2000000 | tf_op jit(solution)/shard_map/middle/pallas_call | solution.py:361
  57.1 0.0 copy-start
  57.2 3.5 %all-to-all-done.2.blocks_ref = bf16[8,128,128]{2,1,0:T(8,128)(2,1)S(1)} async-done(((bf16[8,128,128]{2,1,0:T(8,128)(2,1)}), bf16[8,128,128]{2,1,0:T(8,128)(2,1)S(1)}, u32[]{:S(2)}, u32[]{:S(2)}) %all-to-all-start.2) | async-done | bytes 262176 | tf_op jit(solution)/shard_map/all_to_all | solution.py:360
  60.7 0.9 %outer.1 = bf16[8,64,128]{2,1,0:T(8,128)(2,1)S(1)} custom-call(s32[2,6]{1,0:T(2,128)S(1)} %copy-done.1, f32[128,128]{1,0:T(8,128)S(1)} %get-tuple-element.20.merged_ref, bf16[16,128]{1,0:T(8,128)(2,1)S(1)} %get-tuple-element.21.query_ref, bf16[8,128,128]{2,1,0:T(8,128)(2,1)S(1)} %all-to-all-done.2.blocks_ref, ...), custom_call_target="tpu_custom_call", output_to_operand_aliasing={{}: (4, {})} | custom-call | tf_op jit(solution)/shard_map/outer/pallas_call | solution.py:370
  61.6 16.7 %all_to_all.21.blocks_ref = bf16[8,64,128]{2,1,0:T(8,128)(2,1)S(1)} all-to-all(bf16[8,64,128]{2,1,0:T(8,128)(2,1)S(1)} %outer.1), channel_id=1, replica_groups=mesh['grp'=8,'blk'=8,'set'=8] {'set'}, dimensions={0} | all-to-all | bytes 262144 | tf_op jit(solution)/shard_map/all_to_all | solution.py:377
  78.2 0.0 copy-done
  78.3 1.0 %project.1 = bf16[128,768]{1,0:T(8,128)(2,1)} custom-call(bf16[8,64,128]{2,1,0:T(8,128)(2,1)S(1)} %all_to_all.21.blocks_ref, bf16[384,768]{1,0:T(8,128)(2,1)S(1)} %copy-done), custom_call_target="tpu_custom_call" | custom-call | tf_op jit(solution)/shard_map/project/pallas_call | solution.py:379
Async XLA Ops:
  1.4 10.9 %copy-start.1 = (s32[2,6]{1,0:T(2,128)S(1)}, s32[2,6]{1,0:T(2,128)}, u32[]{:S(2)}) copy-start(s32[2,6]{1,0:T(2,128)} %offsets_ref.9) | copy-start | bytes 148
  12.6 12.7 %collective-permute-start = (bf16[64,128]{1,0:T(8,128)(2,1)S(1)}, bf16[64,128]{1,0:T(8,128)(2,1)S(1)}, u32[]{:S(2)}, u32[]{:S(2)}) collective-permute-start(bf16[64,128]{1,0:T(8,128)(2,1)S(1)} %get-tuple-element.15), channel_id=1, source_target_pairs={{0,4},{1,5},{2,6},{3,7},{4,0},{5,1},{6,2},{7,3},{8,12},{9,13},{10,... | collective-permute-start | bytes 49160 | tf_op jit(solution)/shard_map/ppermute | solution.py:340
  26.0 16.2 %all-to-all-start.1 = ((bf16[8,128,128]{2,1,0:T(8,128)(2,1)}), bf16[8,128,128]{2,1,0:T(8,128)(2,1)S(1)}, u32[]{:S(2)}, u32[]{:S(2)}) async-start(bf16[8,128,128]{2,1,0:T(8,128)(2,1)} %get-tuple-element.19), calls=%async_computation.1 | async-start | bytes 524288 | tf_op jit(solution)/shard_map/all_to_all | solution.py:341
  32.8 19.2 %collective-permute-start.1 = (bf16[4,192,128]{2,1,0:T(8,128)(2,1)S(1)}, bf16[4,192,128]{2,1,0:T(8,128)(2,1)S(1)}, u32[]{:S(2)}, u32[]{:S(2)}) collective-permute-start(bf16[4,192,128]{2,1,0:T(8,128)(2,1)S(1)} %get-tuple-element.16), channel_id=1, source_target_pairs={{0,4},{1,5},{2,6},{3,7},{4,0},{5,1},{6,2},{7,3},{8,12},{9,13},{10,... | collective-permute-start | bytes 589832 | tf_op jit(solution)/shard_map/ppermute | solution.py:342
  43.3 17.4 %all-to-all-start.2 = ((bf16[8,128,128]{2,1,0:T(8,128)(2,1)}), bf16[8,128,128]{2,1,0:T(8,128)(2,1)S(1)}, u32[]{:S(2)}, u32[]{:S(2)}) async-start(bf16[8,128,128]{2,1,0:T(8,128)(2,1)} %pick_outer.1), calls=%async_computation.2 | async-start | bytes 524288 | tf_op jit(solution)/shard_map/all_to_all | solution.py:360
  57.1 21.1 %copy-start = (bf16[384,768]{1,0:T(8,128)(2,1)S(1)}, bf16[384,768]{1,0:T(8,128)(2,1)}, u32[]{:S(2)}) copy-start(bf16[384,768]{1,0:T(8,128)(2,1)} %weight_ref.1) | copy-start | bytes 1769476

commit v8 on v6

--- a/solution.py
+++ b/solution.py
@@ -13,6 +13,10 @@
 PEERS = 8
 NEAR = 4
 HALF_HEADS = HEADS // 2
+NEAR_TURN = 3
+BLOCK_TURN = 4
+HALF_TURN = 1
+GROUP_TURN = 4
 ROWS = 128
 FIRST_BLOCK = ROWS + ROWS // 2
 MARK = 1024.0
@@ -124,7 +128,7 @@
     for copy in copies:
         copy.start()
     for c in range(HALF_HEADS, NEAR):
-        out_ref[c] = jnp.zeros((2 * FIRST_BLOCK, 2 * HD), BF16)
+        out_ref[c ^ NEAR_TURN] = jnp.zeros((2 * FIRST_BLOCK, 2 * HD), BF16)
     for copy in copies:
         copy.wait()
     square = (ROWS, 2 * HD)
@@ -151,7 +155,7 @@
             head = h + part
             inner = slice(part * HD, (part + 1) * HD)
             at = slice(head * HD, (head + 1) * HD)
-            to = head % HALF_HEADS
+            to = (head % HALF_HEADS) ^ NEAR_TURN
             start = place_of(head // HALF_HEADS)
             whole, ends = pl.ds(start, ROWS), pl.ds(start + ROWS, half)
             out_ref[to, whole, 0:HD] = coded[:, inner]
@@ -160,9 +164,13 @@
             out_ref[to, ends, HD : 2 * HD] = query_ref[half:ROWS, at]
 
 
-def selector_of(shift):
+def turned(row):
+    return (row + HALF_TURN * ROWS // 2) % ROWS
+
+
+def selector_of(shift, place=lambda row: row):
     shape = (ROWS // 8, ROWS)
-    return (lanes(shape) == shift + 8 * rows(shape)).astype(F32).astype(BF16)
+    return (lanes(shape) == place(shift + 8 * rows(shape))).astype(F32).astype(BF16)
 
 
 def pick_middle_kernel(offsets_ref, blocks_ref, out_ref, cross_ref):
@@ -171,18 +179,20 @@
         selector = selector_of(shifts(offsets_ref, head_at(half))[0])
         start = place_of(half)
         for c in range(NEAR):
-            picked = product_of(selector, blocks_ref[c, pl.ds(start, ROWS), :]).astype(BF16)
+            rows_of = blocks_ref[c ^ NEAR_TURN, pl.ds(start, ROWS), :]
+            picked = product_of(selector, rows_of).astype(BF16)
             for d in range(PEERS):
-                out_ref[2 * d + half, c * count : (c + 1) * count, :] = picked
+                place = 2 * d + (half ^ HALF_TURN)
+                out_ref[place, c * count : (c + 1) * count, :] = picked
     for c in range(NEAR):
-        cross_ref[c] = blocks_ref[c, FIRST_BLOCK : 2 * FIRST_BLOCK, :]
+        cross_ref[c] = blocks_ref[c ^ NEAR_TURN, FIRST_BLOCK : 2 * FIRST_BLOCK, :]
 
 
 def pick_outer_kernel(offsets_ref, blocks_ref, out_hbm, picked_ref, sems):
-    selector = selector_of(shifts(offsets_ref)[1])
+    selector = selector_of(shifts(offsets_ref)[1], turned)
     count = ROWS // 8
     for c in range(PEERS):
-        picked = product_of(selector, blocks_ref[c, 0:ROWS, :]).astype(BF16)
+        picked = product_of(selector, blocks_ref[c ^ BLOCK_TURN, 0:ROWS, :]).astype(BF16)
         picked_ref[c * count : (c + 1) * count, :] = picked
     copies = [pltpu.make_async_copy(picked_ref, out_hbm.at[d], sems.at[d]) for d in range(PEERS)]
     for copy in copies:
@@ -197,7 +207,7 @@
     middle, stride = shifts(offsets_ref)
     mine = my_half()
     for c in range(NEAR):
-        blocks_ref[mine * NEAR + c] = near_ref[c, 0:FIRST_BLOCK, :]
+        blocks_ref[mine * NEAR + c] = near_ref[c ^ NEAR_TURN, 0:FIRST_BLOCK, :]
         blocks_ref[(1 - mine) * NEAR + c] = far_ref[c]
     half = ROWS // 2
     low = lanes((half, 2 * HD)) < HD
@@ -222,8 +232,8 @@
 def middle_kernel(offsets_ref, state_ref, query_ref, blocks_ref, out_ref, merged_ref, wide):
     middle, _ = shifts(offsets_ref)
     mine = lax.axis_index("blk")
-    diagonal = rows((ROWS, ROWS)) == lanes((ROWS, ROWS))
-    masks = [diagonal & (mine == c) for c in range(PEERS)]
+    diagonal = turned(rows((ROWS, ROWS))) == lanes((ROWS, ROWS))
+    masks = [diagonal & (mine == c ^ BLOCK_TURN) for c in range(PEERS)]
     found = level(query_ref[...], blocks_ref, masks)
     both = merge(state_ref[pl.ds(middle, ROWS, stride=8), :], found)
     merged_ref[...] = both
@@ -243,17 +253,17 @@
     count = ROWS // 8
     shape = (count, ROWS)
     diagonal = lanes(shape) == block * count + rows(shape)
-    masks = [diagonal & (group == c) for c in range(PEERS)]
+    masks = [diagonal & (group == c ^ GROUP_TURN) for c in range(PEERS)]
     found = level(query_ref[...], blocks_ref, masks)
     both = divided(merge(merged_ref[pl.ds(stride, count, stride=8), :], found))
-    turned = pltpu.roll(both, HD, 1)
+    rolled = pltpu.roll(both, HD, 1)
     tile = 16
     token = middle + 8 * stride
     start = pl.multiple_of((token // tile) * tile, tile)
     here = rows((tile, 2 * HD)) == token - start
     low = lanes((1, 2 * HD)) < HD
     for j in range(PEERS):
-        row = jnp.where(low, turned[2 * j : 2 * j + 1, :], both[2 * j + 1 : 2 * j + 2, :])
+        row = jnp.where(low, rolled[2 * j : 2 * j + 1, :], both[2 * j + 1 : 2 * j + 2, :])
         kept = before_ref[j, pl.ds(start, tile), :].astype(F32)
         out_ref[j, pl.ds(start, tile), :] = jnp.where(here, row, kept).astype(BF16)
 
@@ -313,7 +323,7 @@
         [HBM] * 4,
         [whole, whole, whole, pltpu.VMEM((1, ROWS), jnp.int32), pltpu.SemaphoreType.DMA((4,))],
     )(*(pltpu.with_memory_space_constraint(a, pltpu.HBM) for a in given))
-    near_groups = [[z * NEAR + x for x in range(NEAR)] for z in range(2)]
+    near_groups = [[z * NEAR + (x ^ NEAR_TURN) for x in range(NEAR)] for z in range(2)]
     near = swap(packed, "set", axis_index_groups=near_groups)
     middle_send, cross = call(
         pick_middle_kernel,
@@ -322,7 +332,12 @@
         [VMEM, VMEM],
     )(offsets, near)
     middle_groups = [
-        [b * PEERS + z * NEAR + x for b in range(PEERS) for z in range(2)] for x in range(NEAR)
+        [
+            (b ^ BLOCK_TURN) * PEERS + (z ^ HALF_TURN) * NEAR + x
+            for b in range(PEERS)
+            for z in range(2)
+        ]
+        for x in range(NEAR)
     ]
     middle_blocks = swap(middle_send, ("blk", "set"), axis_index_groups=middle_groups)
     middle_blocks = middle_blocks.reshape(PEERS, ROWS, 2 * HD)
@@ -344,7 +359,8 @@
         [pltpu.VMEM((ROWS, 2 * HD), BF16), pltpu.SemaphoreType.DMA((PEERS,))],
         out_spec=HBM,
     )(offsets, middle_blocks)
-    outer_blocks = swap(outer_send, "grp")
+    outer_groups = [[g ^ GROUP_TURN for g in range(PEERS)]]
+    outer_blocks = swap(outer_send, "grp", axis_index_groups=outer_groups)
     before, merged = call(
         middle_kernel,
         "middle",

time: 75.1 us -> 72.4 us (0.964)
  the two profiles are of different devices: /device:TPU:1 before, /device:TPU:8 now
where the time goes in v8:
time: 72.4 us; the launch traced here: 72 us
  blocking collectives  29 us (40%)
  starting transfers between devices  24.9 us (34%)
  Pallas kernels  10.5 us (15%)
  waiting for transfers between devices  7.52 us (10%)
    all_to_all x1, blocking collectives, per_device(): home = swap(combined, 'set')  17.6 us
    all_to_all x1, starting transfers between devices, per_device(): swap(middle_send, ('blk', 'set'), axis_index_groups=middle_groups)  16.6 us
    all_to_all x1, blocking collectives, per_device(): near = swap(packed, 'set', axis_index_groups=near_groups)  11.4 us
    all_to_all x1, starting transfers between devices, per_device(): outer_blocks = swap(outer_send, 'grp', axis_index_groups=outer_groups)  5.81 us
    all_to_all x1, waiting for transfers between devices, per_device(): swap(middle_send, ('blk', 'set'), axis_index_groups=middle_groups)  4.23 us
    pallas_call x1, Pallas kernels, per_device(): call(first_kernel, 'first', (shaped(PEERS * ROWS, 2 * HD, dtype=F32), sha...  4 us
    all_to_all x1, waiting for transfers between devices, per_device(): outer_blocks = swap(outer_send, 'grp', axis_index_groups=outer_groups)  2.49 us
    ppermute x1, starting transfers between devices, per_device(): lax.ppermute(cross, 'set', [(i, (i + NEAR) % PEERS) for i in range(PEERS)])  2.45 us
  transfers between devices with their start and end apart: 3, of which 3 were waited for; matrix products, arithmetic and copies ran while one was open for 0% of the time, Pallas kernels for 9%

profile of v8, /device:TPU:8, one launch (start us, length us, event | category | flops | bytes accessed | tf_op | source)
XLA Modules:
  0.0 72.0 jit_solution(17636770464641926740)
XLA Ops:
  0.0 1.4 %pack.1 = bf16[4,384,128]{2,1,0:T(8,128)(2,1)S(1)} custom-call(bf16[128,384]{1,0:T(8,128)(2,1)} %query_hbm.1, bf16[128,384]{1,0:T(8,128)(2,1)} %key_hbm.1, bf16[128,384]{1,0:T(8,128)(2,1)} %value_hbm.1, s32[1,128]{1,0:T(1,128)} %bitcast.4), custom_call_target="tpu_custom_call" | custom-call | tf_op jit(solution)/shard_map/pack/pallas_call | solution.py:319
  1.4 0.0 copy-start.1
  1.4 11.4 %all_to_all.20.blocks_ref.near_ref = bf16[4,384,128]{2,1,0:T(8,128)(2,1)S(1)} all-to-all(bf16[4,384,128]{2,1,0:T(8,128)(2,1)S(1)} %pack.1), channel_id=1, replica_groups={{3,2,1,0},{7,6,5,4},{11,10,9,8},{15,14,13,12},{19,18,17,16},{23,22,21,2..., dimensions={0} | all-to-all | bytes 786432 | tf_op jit(solution)/shard_map/all_to_all | solution.py:327
  12.8 0.0 copy-done.1
  12.8 1.0 %pick_middle.1 = (bf16[16,64,128]{2,1,0:T(8,128)(2,1)}, bf16[4,192,128]{2,1,0:T(8,128)(2,1)S(1)}) custom-call(s32[2,6]{1,0:T(2,128)S(1)} %copy-done.1, bf16[4,384,128]{2,1,0:T(8,128)(2,1)S(1)} %all_to_all.20.blocks_ref.near_ref), custom_call_target="tpu_custom_call" | custom-call | tf_op jit(solution)/shard_map/pick_middle/pallas_call | solution.py:328
  13.8 16.6 %all-to-all-start.1 = ((bf16[16,64,128]{2,1,0:T(8,128)(2,1)}), bf16[16,64,128]{2,1,0:T(8,128)(2,1)S(1)}, u32[]{:S(2)}, u32[]{:S(2)}) async-start(bf16[16,64,128]{2,1,0:T(8,128)(2,1)} %get-tuple-element.15), calls=%async_computation.1 | async-start | bytes 524288 | tf_op jit(solution)/shard_map/all_to_all | solution.py:342
  30.5 2.5 %collective-permute-start = (bf16[4,192,128]{2,1,0:T(8,128)(2,1)S(1)}, bf16[4,192,128]{2,1,0:T(8,128)(2,1)S(1)}, u32[]{:S(2)}, u32[]{:S(2)}) collective-permute-start(bf16[4,192,128]{2,1,0:T(8,128)(2,1)S(1)} %get-tuple-element.12), channel_id=1, source_target_pairs={{0,4},{1,5},{2,6},{3,7},{4,0},{5,1},{6,2},{7,3},{8,12},{9,13},{10,... | collective-permute-start | bytes 589832 | tf_op jit(solution)/shard_map/ppermute | solution.py:344
  32.9 4.2 %all-to-all-done.1 = bf16[16,64,128]{2,1,0:T(8,128)(2,1)S(1)} async-done(((bf16[16,64,128]{2,1,0:T(8,128)(2,1)}), bf16[16,64,128]{2,1,0:T(8,128)(2,1)S(1)}, u32[]{:S(2)}, u32[]{:S(2)}) %all-to-all-start.1) | async-done | bytes 262176 | tf_op jit(solution)/shard_map/all_to_all | solution.py:342
  37.2 1.1 %pick_outer.1 = bf16[8,128,128]{2,1,0:T(8,128)(2,1)} custom-call(s32[2,6]{1,0:T(2,128)S(1)} %copy-done.1, bf16[8,128,128]{2,1,0:T(8,128)(2,1)S(1)} %bitcast.2), custom_call_target="tpu_custom_call" | custom-call | tf_op jit(solution)/shard_map/pick_outer/pallas_call | solution.py:354
  38.3 5.8 %all-to-all-start.2 = ((bf16[8,128,128]{2,1,0:T(8,128)(2,1)}), bf16[8,128,128]{2,1,0:T(8,128)(2,1)S(1)}, u32[]{:S(2)}, u32[]{:S(2)}) async-start(bf16[8,128,128]{2,1,0:T(8,128)(2,1)} %pick_outer.1), calls=%async_computation.2 | async-start | bytes 524288 | tf_op jit(solution)/shard_map/all_to_all | solution.py:363
  44.1 0.8 %collective-permute-done.far_ref = bf16[4,192,128]{2,1,0:T(8,128)(2,1)S(1)} collective-permute-done((bf16[4,192,128]{2,1,0:T(8,128)(2,1)S(1)}, bf16[4,192,128]{2,1,0:T(8,128)(2,1)S(1)}, u32[]{:S(2)}, u32[]{:S(2)}) %collective-permute-start) | collective-permute-done | bytes 196640 | tf_op jit(solution)/shard_map/ppermute | solution.py:344
  44.9 4.0 %first.1 = (f32[1024,128]{1,0:T(8,128)S(1)}, bf16[128,128]{1,0:T(8,128)(2,1)S(1)}, bf16[16,128]{1,0:T(8,128)(2,1)S(1)}) custom-call(s32[2,6]{1,0:T(2,128)S(1)} %copy-done.1, bf16[4,384,128]{2,1,0:T(8,128)(2,1)S(1)} %all_to_all.20.blocks_ref.near_ref, bf16[4,192,128]{2,1,0:T(8,128)(2,1)S(1)} %collective-permute-done.far_ref), custom_call_target="tpu_custom_call" | custom-call | flops 6000000000 | bytes 2000000 | tf_op jit(solution)/shard_map/first/pallas_call | solution.py:345
  48.9 1.1 %middle.1 = (bf16[8,64,128]{2,1,0:T(8,128)(2,1)S(1)}, f32[128,128]{1,0:T(8,128)S(1)}) custom-call(s32[2,6]{1,0:T(2,128)S(1)} %copy-done.1, f32[1024,128]{1,0:T(8,128)S(1)} %get-tuple-element.13.state_ref, bf16[128,128]{1,0:T(8,128)(2,1)S(1)} %get-tuple-element.14.query_ref, bf16[8,128,128]{2,1,0:T(8,128)(2,1)S(1)} %bitcast.3), custom_call_target="tpu_custom_call" | custom-call | flops 2000000000 | bytes 2000000 | tf_op jit(solution)/shard_map/middle/pallas_call | solution.py:364
  50.0 0.0 copy-start
  50.0 2.5 %all-to-all-done.2.blocks_ref = bf16[8,128,128]{2,1,0:T(8,128)(2,1)S(1)} async-done(((bf16[8,128,128]{2,1,0:T(8,128)(2,1)}), bf16[8,128,128]{2,1,0:T(8,128)(2,1)S(1)}, u32[]{:S(2)}, u32[]{:S(2)}) %all-to-all-start.2) | async-done | bytes 262176 | tf_op jit(solution)/shard_map/all_to_all | solution.py:363
  52.5 0.9 %outer.1 = bf16[8,64,128]{2,1,0:T(8,128)(2,1)S(1)} custom-call(s32[2,6]{1,0:T(2,128)S(1)} %copy-done.1, f32[128,128]{1,0:T(8,128)S(1)} %get-tuple-element.16.merged_ref, bf16[16,128]{1,0:T(8,128)(2,1)S(1)} %get-tuple-element.17.query_ref, bf16[8,128,128]{2,1,0:T(8,128)(2,1)S(1)} %all-to-all-done.2.blocks_ref, ...), custom_call_target="tpu_custom_call", output_to_operand_aliasing={{}: (4, {})} | custom-call | tf_op jit(solution)/shard_map/outer/pallas_call | solution.py:373
  53.4 17.6 %all_to_all.21.blocks_ref = bf16[8,64,128]{2,1,0:T(8,128)(2,1)S(1)} all-to-all(bf16[8,64,128]{2,1,0:T(8,128)(2,1)S(1)} %outer.1), channel_id=1, replica_groups=mesh['grp'=8,'blk'=8,'set'=8] {'set'}, dimensions={0} | all-to-all | bytes 262144 | tf_op jit(solution)/shard_map/all_to_all | solution.py:380
  71.0 0.0 copy-done
  71.0 1.0 %project.1 = bf16[128,768]{1,0:T(8,128)(2,1)} custom-call(bf16[8,64,128]{2,1,0:T(8,128)(2,1)S(1)} %all_to_all.21.blocks_ref, bf16[384,768]{1,0:T(8,128)(2,1)S(1)} %copy-done), custom_call_target="tpu_custom_call" | custom-call | tf_op jit(solution)/shard_map/project/pallas_call | solution.py:382
Async XLA Ops:
  1.4 11.5 %copy-start.1 = (s32[2,6]{1,0:T(2,128)S(1)}, s32[2,6]{1,0:T(2,128)}, u32[]{:S(2)}) copy-start(s32[2,6]{1,0:T(2,128)} %offsets_ref.9) | copy-start | bytes 148
  13.8 23.3 %all-to-all-start.1 = ((bf16[16,64,128]{2,1,0:T(8,128)(2,1)}), bf16[16,64,128]{2,1,0:T(8,128)(2,1)S(1)}, u32[]{:S(2)}, u32[]{:S(2)}) async-start(bf16[16,64,128]{2,1,0:T(8,128)(2,1)} %get-tuple-element.15), calls=%async_computation.1 | async-start | bytes 524288 | tf_op jit(solution)/shard_map/all_to_all | solution.py:342
  30.5 14.4 %collective-permute-start = (bf16[4,192,128]{2,1,0:T(8,128)(2,1)S(1)}, bf16[4,192,128]{2,1,0:T(8,128)(2,1)S(1)}, u32[]{:S(2)}, u32[]{:S(2)}) collective-permute-start(bf16[4,192,128]{2,1,0:T(8,128)(2,1)S(1)} %get-tuple-element.12), channel_id=1, source_target_pairs={{0,4},{1,5},{2,6},{3,7},{4,0},{5,1},{6,2},{7,3},{8,12},{9,13},{10,... | collective-permute-start | bytes 589832 | tf_op jit(solution)/shard_map/ppermute | solution.py:344
  38.3 14.3 %all-to-all-start.2 = ((bf16[8,128,128]{2,1,0:T(8,128)(2,1)}), bf16[8,128,128]{2,1,0:T(8,128)(2,1)S(1)}, u32[]{:S(2)}, u32[]{:S(2)}) async-start(bf16[8,128,128]{2,1,0:T(8,128)(2,1)} %pick_outer.1), calls=%async_computation.2 | async-start | bytes 524288 | tf_op jit(solution)/shard_map/all_to_all | solution.py:363
  50.0 21.0 %copy-start = (bf16[384,768]{1,0:T(8,128)(2,1)S(1)}, bf16[384,768]{1,0:T(8,128)(2,1)}, u32[]{:S(2)}) copy-start(bf16[384,768]{1,0:T(8,128)(2,1)} %weight_ref.1) | copy-start | bytes 1769476

commit v9 on v8

--- a/solution.py
+++ b/solution.py
@@ -17,6 +17,7 @@
 BLOCK_TURN = 4
 HALF_TURN = 1
 GROUP_TURN = 4
+HOME_TURN = 7
 ROWS = 128
 FIRST_BLOCK = ROWS + ROWS // 2
 MARK = 1024.0
@@ -244,7 +245,7 @@
     for j in range(PEERS):
         one = divided(wide[j * ROWS : j * ROWS + half, :])
         two = divided(wide[j * ROWS + half : (j + 1) * ROWS, :])
-        out_ref[j] = jnp.where(low, pltpu.roll(one, HD, 1), two).astype(BF16)
+        out_ref[j ^ HOME_TURN] = jnp.where(low, pltpu.roll(one, HD, 1), two).astype(BF16)
 
 
 def outer_kernel(offsets_ref, merged_ref, query_ref, blocks_ref, before_ref, out_ref):
@@ -264,15 +265,16 @@
     low = lanes((1, 2 * HD)) < HD
     for j in range(PEERS):
         row = jnp.where(low, rolled[2 * j : 2 * j + 1, :], both[2 * j + 1 : 2 * j + 2, :])
-        kept = before_ref[j, pl.ds(start, tile), :].astype(F32)
-        out_ref[j, pl.ds(start, tile), :] = jnp.where(here, row, kept).astype(BF16)
+        place = j ^ HOME_TURN
+        kept = before_ref[place, pl.ds(start, tile), :].astype(F32)
+        out_ref[place, pl.ds(start, tile), :] = jnp.where(here, row, kept).astype(BF16)
 
 
 def project_kernel(blocks_ref, weight_ref, out_hbm, out_ref, sems):
     half = ROWS // 2
     low = lanes((half, 2 * HD)) < HD
     tops, bottoms = [], []
-    places = [h // HALF_HEADS * NEAR + h % HALF_HEADS for h in range(HEADS)]
+    places = [(h // HALF_HEADS * NEAR + h % HALF_HEADS) ^ HOME_TURN for h in range(HEADS)]
     for h in range(0, HEADS, 2):
         one, two = blocks_ref[places[h]].astype(F32), blocks_ref[places[h + 1]].astype(F32)
         tops.append(jnp.where(low, one, pltpu.roll(two, HD, 1)).astype(BF16))
@@ -377,7 +379,7 @@
         [VMEM, VMEM, VMEM, VMEM, VMEM],
         aliases={4: 0},
     )(offsets, merged, outer_query, outer_blocks, before)
-    home = swap(combined, "set")
+    home = swap(combined, "set", axis_index_groups=[[s ^ HOME_TURN for s in range(PEERS)]])
     width = w_out.shape[1]
     return call(
         project_kernel,

time: 72.4 us -> 68.7 us (0.949)
  the two profiles are of different devices: /device:TPU:8 before, /device:TPU:1 now
where the time goes in v9:
time: 68.7 us; the launch traced here: 68.3 us
  starting transfers between devices  29 us (42%)
  blocking collectives  22 us (32%)
  Pallas kernels  10.5 us (15%)
  waiting for transfers between devices  6.69 us (10%)
    all_to_all x1, starting transfers between devices, per_device(): swap(middle_send, ('blk', 'set'), axis_index_groups=middle_groups)  18.2 us
    all_to_all x1, blocking collectives, per_device(): swap(combined, 'set', axis_index_groups=[[s ^ HOME_TURN for s in range(PE...  11.9 us
    all_to_all x1, blocking collectives, per_device(): near = swap(packed, 'set', axis_index_groups=near_groups)  10.1 us
    all_to_all x1, starting transfers between devices, per_device(): outer_blocks = swap(outer_send, 'grp', axis_index_groups=outer_groups)  8.6 us
    pallas_call x1, Pallas kernels, per_device(): call(first_kernel, 'first', (shaped(PEERS * ROWS, 2 * HD, dtype=F32), sha...  4 us
    all_to_all x1, waiting for transfers between devices, per_device(): outer_blocks = swap(outer_send, 'grp', axis_index_groups=outer_groups)  3.54 us
    all_to_all x1, waiting for transfers between devices, per_device(): swap(middle_send, ('blk', 'set'), axis_index_groups=middle_groups)  3.14 us
    ppermute x1, starting transfers between devices, per_device(): lax.ppermute(cross, 'set', [(i, (i + NEAR) % PEERS) for i in range(PEERS)])  2.17 us
  transfers between devices with their start and end apart: 3, of which 2 were waited for; matrix products, arithmetic and copies ran while one was open for 0% of the time, Pallas kernels for 9%

profile of v9, /device:TPU:1, one launch (start us, length us, event | category | flops | bytes accessed | tf_op | source)
XLA Modules:
  0.0 68.3 jit_solution(7253863943566286147)
XLA Ops:
  0.0 1.4 %pack.1 = bf16[4,384,128]{2,1,0:T(8,128)(2,1)S(1)} custom-call(bf16[128,384]{1,0:T(8,128)(2,1)} %query_hbm.1, bf16[128,384]{1,0:T(8,128)(2,1)} %key_hbm.1, bf16[128,384]{1,0:T(8,128)(2,1)} %value_hbm.1, s32[1,128]{1,0:T(1,128)} %bitcast.4), custom_call_target="tpu_custom_call" | custom-call | tf_op jit(solution)/shard_map/pack/pallas_call | solution.py:321
  1.4 0.0 copy-start.1
  1.4 10.1 %all_to_all.20.blocks_ref.near_ref = bf16[4,384,128]{2,1,0:T(8,128)(2,1)S(1)} all-to-all(bf16[4,384,128]{2,1,0:T(8,128)(2,1)S(1)} %pack.1), channel_id=1, replica_groups={{3,2,1,0},{7,6,5,4},{11,10,9,8},{15,14,13,12},{19,18,17,16},{23,22,21,2..., dimensions={0} | all-to-all | bytes 786432 | tf_op jit(solution)/shard_map/all_to_all | solution.py:329
  11.5 0.0 copy-done.1
  11.5 1.0 %pick_middle.1 = (bf16[16,64,128]{2,1,0:T(8,128)(2,1)}, bf16[4,192,128]{2,1,0:T(8,128)(2,1)S(1)}) custom-call(s32[2,6]{1,0:T(2,128)S(1)} %copy-done.1, bf16[4,384,128]{2,1,0:T(8,128)(2,1)S(1)} %all_to_all.20.blocks_ref.near_ref), custom_call_target="tpu_custom_call" | custom-call | tf_op jit(solution)/shard_map/pick_middle/pallas_call | solution.py:330
  12.5 18.2 %all-to-all-start.1 = ((bf16[16,64,128]{2,1,0:T(8,128)(2,1)}), bf16[16,64,128]{2,1,0:T(8,128)(2,1)S(1)}, u32[]{:S(2)}, u32[]{:S(2)}) async-start(bf16[16,64,128]{2,1,0:T(8,128)(2,1)} %get-tuple-element.15), calls=%async_computation.1 | async-start | bytes 524288 | tf_op jit(solution)/shard_map/all_to_all | solution.py:344
  30.8 2.2 %collective-permute-start = (bf16[4,192,128]{2,1,0:T(8,128)(2,1)S(1)}, bf16[4,192,128]{2,1,0:T(8,128)(2,1)S(1)}, u32[]{:S(2)}, u32[]{:S(2)}) collective-permute-start(bf16[4,192,128]{2,1,0:T(8,128)(2,1)S(1)} %get-tuple-element.12), channel_id=1, source_target_pairs={{0,4},{1,5},{2,6},{3,7},{4,0},{5,1},{6,2},{7,3},{8,12},{9,13},{10,... | collective-permute-start | bytes 589832 | tf_op jit(solution)/shard_map/ppermute | solution.py:346
  32.9 3.1 %all-to-all-done.1 = bf16[16,64,128]{2,1,0:T(8,128)(2,1)S(1)} async-done(((bf16[16,64,128]{2,1,0:T(8,128)(2,1)}), bf16[16,64,128]{2,1,0:T(8,128)(2,1)S(1)}, u32[]{:S(2)}, u32[]{:S(2)}) %all-to-all-start.1) | async-done | bytes 262176 | tf_op jit(solution)/shard_map/all_to_all | solution.py:344
  36.1 1.1 %pick_outer.1 = bf16[8,128,128]{2,1,0:T(8,128)(2,1)} custom-call(s32[2,6]{1,0:T(2,128)S(1)} %copy-done.1, bf16[8,128,128]{2,1,0:T(8,128)(2,1)S(1)} %bitcast.2), custom_call_target="tpu_custom_call" | custom-call | tf_op jit(solution)/shard_map/pick_outer/pallas_call | solution.py:356
  37.2 8.6 %all-to-all-start.2 = ((bf16[8,128,128]{2,1,0:T(8,128)(2,1)}), bf16[8,128,128]{2,1,0:T(8,128)(2,1)S(1)}, u32[]{:S(2)}, u32[]{:S(2)}) async-start(bf16[8,128,128]{2,1,0:T(8,128)(2,1)} %pick_outer.1), calls=%async_computation.2 | async-start | bytes 524288 | tf_op jit(solution)/shard_map/all_to_all | solution.py:365
  45.8 0.0 collective-permute-done.far_ref
  45.8 4.0 %first.1 = (f32[1024,128]{1,0:T(8,128)S(1)}, bf16[128,128]{1,0:T(8,128)(2,1)S(1)}, bf16[16,128]{1,0:T(8,128)(2,1)S(1)}) custom-call(s32[2,6]{1,0:T(2,128)S(1)} %copy-done.1, bf16[4,384,128]{2,1,0:T(8,128)(2,1)S(1)} %all_to_all.20.blocks_ref.near_ref, bf16[4,192,128]{2,1,0:T(8,128)(2,1)S(1)} %collective-permute-done.far_ref), custom_call_target="tpu_custom_call" | custom-call | flops 6000000000 | bytes 2000000 | tf_op jit(solution)/shard_map/first/pallas_call | solution.py:347
  49.8 1.1 %middle.1 = (bf16[8,64,128]{2,1,0:T(8,128)(2,1)S(1)}, f32[128,128]{1,0:T(8,128)S(1)}) custom-call(s32[2,6]{1,0:T(2,128)S(1)} %copy-done.1, f32[1024,128]{1,0:T(8,128)S(1)} %get-tuple-element.13.state_ref, bf16[128,128]{1,0:T(8,128)(2,1)S(1)} %get-tuple-element.14.query_ref, bf16[8,128,128]{2,1,0:T(8,128)(2,1)S(1)} %bitcast.3), custom_call_target="tpu_custom_call" | custom-call | flops 2000000000 | bytes 2000000 | tf_op jit(solution)/shard_map/middle/pallas_call | solution.py:366
  50.9 0.0 copy-start
  50.9 3.5 %all-to-all-done.2.blocks_ref = bf16[8,128,128]{2,1,0:T(8,128)(2,1)S(1)} async-done(((bf16[8,128,128]{2,1,0:T(8,128)(2,1)}), bf16[8,128,128]{2,1,0:T(8,128)(2,1)S(1)}, u32[]{:S(2)}, u32[]{:S(2)}) %all-to-all-start.2) | async-done | bytes 262176 | tf_op jit(solution)/shard_map/all_to_all | solution.py:365
  54.5 0.9 %outer.1 = bf16[8,64,128]{2,1,0:T(8,128)(2,1)S(1)} custom-call(s32[2,6]{1,0:T(2,128)S(1)} %copy-done.1, f32[128,128]{1,0:T(8,128)S(1)} %get-tuple-element.16.merged_ref, bf16[16,128]{1,0:T(8,128)(2,1)S(1)} %get-tuple-element.17.query_ref, bf16[8,128,128]{2,1,0:T(8,128)(2,1)S(1)} %all-to-all-done.2.blocks_ref, ...), custom_call_target="tpu_custom_call", output_to_operand_aliasing={{}: (4, {})} | custom-call | tf_op jit(solution)/shard_map/outer/pallas_call | solution.py:375
  55.4 11.9 %all_to_all.21.blocks_ref = bf16[8,64,128]{2,1,0:T(8,128)(2,1)S(1)} all-to-all(bf16[8,64,128]{2,1,0:T(8,128)(2,1)S(1)} %outer.1), channel_id=1, replica_groups={{7,6,5,4,3,2,1,0},{15,14,13,12,11,10,9,8},{23,22,21,20,19,18,17,16},{31..., dimensions={0} | all-to-all | bytes 262144 | tf_op jit(solution)/shard_map/all_to_all | solution.py:382
  67.3 0.0 copy-done
  67.3 1.0 %project.1 = bf16[128,768]{1,0:T(8,128)(2,1)} custom-call(bf16[8,64,128]{2,1,0:T(8,128)(2,1)S(1)} %all_to_all.21.blocks_ref, bf16[384,768]{1,0:T(8,128)(2,1)S(1)} %copy-done), custom_call_target="tpu_custom_call" | custom-call | tf_op jit(solution)/shard_map/project/pallas_call | solution.py:384
Async XLA Ops:
  1.4 10.2 %copy-start.1 = (s32[2,6]{1,0:T(2,128)S(1)}, s32[2,6]{1,0:T(2,128)}, u32[]{:S(2)}) copy-start(s32[2,6]{1,0:T(2,128)} %offsets_ref.9) | copy-start | bytes 148
  12.5 23.5 %all-to-all-start.1 = ((bf16[16,64,128]{2,1,0:T(8,128)(2,1)}), bf16[16,64,128]{2,1,0:T(8,128)(2,1)S(1)}, u32[]{:S(2)}, u32[]{:S(2)}) async-start(bf16[16,64,128]{2,1,0:T(8,128)(2,1)} %get-tuple-element.15), calls=%async_computation.1 | async-start | bytes 524288 | tf_op jit(solution)/shard_map/all_to_all | solution.py:344
  30.8 15.0 %collective-permute-start = (bf16[4,192,128]{2,1,0:T(8,128)(2,1)S(1)}, bf16[4,192,128]{2,1,0:T(8,128)(2,1)S(1)}, u32[]{:S(2)}, u32[]{:S(2)}) collective-permute-start(bf16[4,192,128]{2,1,0:T(8,128)(2,1)S(1)} %get-tuple-element.12), channel_id=1, source_target_pairs={{0,4},{1,5},{2,6},{3,7},{4,0},{5,1},{6,2},{7,3},{8,12},{9,13},{10,... | collective-permute-start | bytes 589832 | tf_op jit(solution)/shard_map/ppermute | solution.py:346
  37.2 17.3 %all-to-all-start.2 = ((bf16[8,128,128]{2,1,0:T(8,128)(2,1)}), bf16[8,128,128]{2,1,0:T(8,128)(2,1)S(1)}, u32[]{:S(2)}, u32[]{:S(2)}) async-start(bf16[8,128,128]{2,1,0:T(8,128)(2,1)} %pick_outer.1), calls=%async_computation.2 | async-start | bytes 524288 | tf_op jit(solution)/shard_map/all_to_all | solution.py:365
  50.9 16.3 %copy-start = (bf16[384,768]{1,0:T(8,128)(2,1)S(1)}, bf16[384,768]{1,0:T(8,128)(2,1)}, u32[]{:S(2)}) copy-start(bf16[384,768]{1,0:T(8,128)(2,1)} %weight_ref.1) | copy-start | bytes 1769476

commit v10 on v9

--- a/solution.py
+++ b/solution.py
@@ -16,7 +16,7 @@
 NEAR_TURN = 3
 BLOCK_TURN = 4
 HALF_TURN = 1
-GROUP_TURN = 4
+GROUP_ORDER = (4, 2, 6, 0, 5, 3, 7, 1)
 HOME_TURN = 7
 ROWS = 128
 FIRST_BLOCK = ROWS + ROWS // 2
@@ -165,13 +165,9 @@
             out_ref[to, ends, HD : 2 * HD] = query_ref[half:ROWS, at]
 
 
-def turned(row):
-    return (row + HALF_TURN * ROWS // 2) % ROWS
-
-
-def selector_of(shift, place=lambda row: row):
+def selector_of(shift):
     shape = (ROWS // 8, ROWS)
-    return (lanes(shape) == place(shift + 8 * rows(shape))).astype(F32).astype(BF16)
+    return (lanes(shape) == shift + 8 * rows(shape)).astype(F32).astype(BF16)
 
 
 def pick_middle_kernel(offsets_ref, blocks_ref, out_ref, cross_ref):
@@ -183,17 +179,17 @@
             rows_of = blocks_ref[c ^ NEAR_TURN, pl.ds(start, ROWS), :]
             picked = product_of(selector, rows_of).astype(BF16)
             for d in range(PEERS):
-                place = 2 * d + (half ^ HALF_TURN)
+                place = (half ^ HALF_TURN) * PEERS + d
                 out_ref[place, c * count : (c + 1) * count, :] = picked
     for c in range(NEAR):
         cross_ref[c] = blocks_ref[c ^ NEAR_TURN, FIRST_BLOCK : 2 * FIRST_BLOCK, :]
 
 
 def pick_outer_kernel(offsets_ref, blocks_ref, out_hbm, picked_ref, sems):
-    selector = selector_of(shifts(offsets_ref)[1], turned)
+    selector = selector_of(shifts(offsets_ref)[1])
     count = ROWS // 8
     for c in range(PEERS):
-        picked = product_of(selector, blocks_ref[c ^ BLOCK_TURN, 0:ROWS, :]).astype(BF16)
+        picked = product_of(selector, blocks_ref[c, 0:ROWS, :]).astype(BF16)
         picked_ref[c * count : (c + 1) * count, :] = picked
     copies = [pltpu.make_async_copy(picked_ref, out_hbm.at[d], sems.at[d]) for d in range(PEERS)]
     for copy in copies:
@@ -232,9 +228,14 @@
 
 def middle_kernel(offsets_ref, state_ref, query_ref, blocks_ref, out_ref, merged_ref, wide):
     middle, _ = shifts(offsets_ref)
-    mine = lax.axis_index("blk")
-    diagonal = turned(rows((ROWS, ROWS))) == lanes((ROWS, ROWS))
-    masks = [diagonal & (mine == c ^ BLOCK_TURN) for c in range(PEERS)]
+    mine = lax.axis_index("blk") ^ BLOCK_TURN
+    row, lane = rows((ROWS, ROWS)), lanes((ROWS, ROWS))
+    count = ROWS // 2
+    diagonal = lane == row % count + count * lax.rem(mine, 2)
+    masks = [
+        diagonal & (row // count == (c // 4) ^ HALF_TURN) & (lax.div(mine, 2) == c % 4)
+        for c in range(PEERS)
+    ]
     found = level(query_ref[...], blocks_ref, masks)
     both = merge(state_ref[pl.ds(middle, ROWS, stride=8), :], found)
     merged_ref[...] = both
@@ -250,11 +251,13 @@
 
 def outer_kernel(offsets_ref, merged_ref, query_ref, blocks_ref, before_ref, out_ref):
     middle, stride = shifts(offsets_ref)
-    block, group = lax.axis_index("blk"), lax.axis_index("grp")
+    block, group = lax.axis_index("blk") ^ BLOCK_TURN, lax.axis_index("grp")
     count = ROWS // 8
     shape = (count, ROWS)
-    diagonal = lanes(shape) == block * count + rows(shape)
-    masks = [diagonal & (group == c ^ GROUP_TURN) for c in range(PEERS)]
+    row = rows(shape)
+    place = ((row // 8) ^ HALF_TURN) * (ROWS // 2) + block * 8 + row % 8
+    diagonal = lanes(shape) == place
+    masks = [diagonal & (group == g) for g in GROUP_ORDER]
     found = level(query_ref[...], blocks_ref, masks)
     both = divided(merge(merged_ref[pl.ds(stride, count, stride=8), :], found))
     rolled = pltpu.roll(both, HD, 1)
@@ -336,8 +339,8 @@
     middle_groups = [
         [
             (b ^ BLOCK_TURN) * PEERS + (z ^ HALF_TURN) * NEAR + x
+            for z in range(2)
             for b in range(PEERS)
-            for z in range(2)
         ]
         for x in range(NEAR)
     ]
@@ -361,8 +364,7 @@
         [pltpu.VMEM((ROWS, 2 * HD), BF16), pltpu.SemaphoreType.DMA((PEERS,))],
         out_spec=HBM,
     )(offsets, middle_blocks)
-    outer_groups = [[g ^ GROUP_TURN for g in range(PEERS)]]
-    outer_blocks = swap(outer_send, "grp", axis_index_groups=outer_groups)
+    outer_blocks = swap(outer_send, "grp", axis_index_groups=[list(GROUP_ORDER)])
     before, merged = call(
         middle_kernel,
         "middle",

time: 68.7 us -> 67.5 us (0.983)
  waiting for transfers between devices: 6.69 us -> 4.87 us
  blocking collectives: 22 us -> 23.4 us
  starting transfers between devices: 29 us -> 28.3 us
    all_to_all x1, waiting for transfers between devices: 3.54 us -> 1.75 us  [per_device(): swap(outer_send, 'grp', axis_index_groups=[list(GROUP_ORDER)])]
    all_to_all x1, blocking collectives: 11.9 us -> 13.3 us  [per_device(): swap(combined, 'set', axis_index_groups=[[s ^ HOME_TURN for s in range(PE...]
    all_to_all x1, starting transfers between devices: 8.6 us -> 7.9 us  [per_device(): swap(outer_send, 'grp', axis_index_groups=[list(GROUP_ORDER)])]
where the time goes in v10:
time: 67.5 us; the launch traced here: 67.1 us
  starting transfers between devices  28.3 us (42%)
  blocking collectives  23.4 us (35%)
  Pallas kernels  10.5 us (16%)
  waiting for transfers between devices  4.87 us (7%)
    all_to_all x1, starting transfers between devices, per_device(): swap(middle_send, ('blk', 'set'), axis_index_groups=middle_groups)  18.2 us
    all_to_all x1, blocking collectives, per_device(): swap(combined, 'set', axis_index_groups=[[s ^ HOME_TURN for s in range(PE...  13.3 us
    all_to_all x1, blocking collectives, per_device(): near = swap(packed, 'set', axis_index_groups=near_groups)  10.1 us
    all_to_all x1, starting transfers between devices, per_device(): swap(outer_send, 'grp', axis_index_groups=[list(GROUP_ORDER)])  7.9 us
    pallas_call x1, Pallas kernels, per_device(): call(first_kernel, 'first', (shaped(PEERS * ROWS, 2 * HD, dtype=F32), sha...  4 us
    all_to_all x1, waiting for transfers between devices, per_device(): swap(middle_send, ('blk', 'set'), axis_index_groups=middle_groups)  3.12 us
    ppermute x1, starting transfers between devices, per_device(): lax.ppermute(cross, 'set', [(i, (i + NEAR) % PEERS) for i in range(PEERS)])  2.13 us
    all_to_all x1, waiting for transfers between devices, per_device(): swap(outer_send, 'grp', axis_index_groups=[list(GROUP_ORDER)])  1.75 us
  transfers between devices with their start and end apart: 3, of which 2 were waited for; matrix products, arithmetic and copies ran while one was open for 0% of the time, Pallas kernels for 9%

profile of v10, /device:TPU:1, one launch (start us, length us, event | category | flops | bytes accessed | tf_op | source)
XLA Modules:
  0.0 67.1 jit_solution(16625089370961471113)
XLA Ops:
  0.0 1.4 %pack.1 = bf16[4,384,128]{2,1,0:T(8,128)(2,1)S(1)} custom-call(bf16[128,384]{1,0:T(8,128)(2,1)} %query_hbm.1, bf16[128,384]{1,0:T(8,128)(2,1)} %key_hbm.1, bf16[128,384]{1,0:T(8,128)(2,1)} %value_hbm.1, s32[1,128]{1,0:T(1,128)} %bitcast.4), custom_call_target="tpu_custom_call" | custom-call | tf_op jit(solution)/shard_map/pack/pallas_call | solution.py:324
  1.4 0.0 copy-start.1
  1.4 10.1 %all_to_all.20.blocks_ref.near_ref = bf16[4,384,128]{2,1,0:T(8,128)(2,1)S(1)} all-to-all(bf16[4,384,128]{2,1,0:T(8,128)(2,1)S(1)} %pack.1), channel_id=1, replica_groups={{3,2,1,0},{7,6,5,4},{11,10,9,8},{15,14,13,12},{19,18,17,16},{23,22,21,2..., dimensions={0} | all-to-all | bytes 786432 | tf_op jit(solution)/shard_map/all_to_all | solution.py:332
  11.5 0.0 copy-done.1
  11.5 1.0 %pick_middle.1 = (bf16[16,64,128]{2,1,0:T(8,128)(2,1)}, bf16[4,192,128]{2,1,0:T(8,128)(2,1)S(1)}) custom-call(s32[2,6]{1,0:T(2,128)S(1)} %copy-done.1, bf16[4,384,128]{2,1,0:T(8,128)(2,1)S(1)} %all_to_all.20.blocks_ref.near_ref), custom_call_target="tpu_custom_call" | custom-call | tf_op jit(solution)/shard_map/pick_middle/pallas_call | solution.py:333
  12.5 18.2 %all-to-all-start.1 = ((bf16[16,64,128]{2,1,0:T(8,128)(2,1)}), bf16[16,64,128]{2,1,0:T(8,128)(2,1)S(1)}, u32[]{:S(2)}, u32[]{:S(2)}) async-start(bf16[16,64,128]{2,1,0:T(8,128)(2,1)} %get-tuple-element.15), calls=%async_computation.1 | async-start | bytes 524288 | tf_op jit(solution)/shard_map/all_to_all | solution.py:347
  30.8 2.1 %collective-permute-start = (bf16[4,192,128]{2,1,0:T(8,128)(2,1)S(1)}, bf16[4,192,128]{2,1,0:T(8,128)(2,1)S(1)}, u32[]{:S(2)}, u32[]{:S(2)}) collective-permute-start(bf16[4,192,128]{2,1,0:T(8,128)(2,1)S(1)} %get-tuple-element.12), channel_id=1, source_target_pairs={{0,4},{1,5},{2,6},{3,7},{4,0},{5,1},{6,2},{7,3},{8,12},{9,13},{10,... | collective-permute-start | bytes 589832 | tf_op jit(solution)/shard_map/ppermute | solution.py:349
  32.9 3.1 %all-to-all-done.1 = bf16[16,64,128]{2,1,0:T(8,128)(2,1)S(1)} async-done(((bf16[16,64,128]{2,1,0:T(8,128)(2,1)}), bf16[16,64,128]{2,1,0:T(8,128)(2,1)S(1)}, u32[]{:S(2)}, u32[]{:S(2)}) %all-to-all-start.1) | async-done | bytes 262176 | tf_op jit(solution)/shard_map/all_to_all | solution.py:347
  36.0 1.1 %pick_outer.1 = bf16[8,128,128]{2,1,0:T(8,128)(2,1)} custom-call(s32[2,6]{1,0:T(2,128)S(1)} %copy-done.1, bf16[8,128,128]{2,1,0:T(8,128)(2,1)S(1)} %bitcast.2), custom_call_target="tpu_custom_call" | custom-call | tf_op jit(solution)/shard_map/pick_outer/pallas_call | solution.py:359
  37.1 7.9 %all-to-all-start.2 = ((bf16[8,128,128]{2,1,0:T(8,128)(2,1)}), bf16[8,128,128]{2,1,0:T(8,128)(2,1)S(1)}, u32[]{:S(2)}, u32[]{:S(2)}) async-start(bf16[8,128,128]{2,1,0:T(8,128)(2,1)} %pick_outer.1), calls=%async_computation.2 | async-start | bytes 524288 | tf_op jit(solution)/shard_map/all_to_all | solution.py:367
  45.0 0.0 collective-permute-done.far_ref
  45.0 4.0 %first.1 = (f32[1024,128]{1,0:T(8,128)S(1)}, bf16[128,128]{1,0:T(8,128)(2,1)S(1)}, bf16[16,128]{1,0:T(8,128)(2,1)S(1)}) custom-call(s32[2,6]{1,0:T(2,128)S(1)} %copy-done.1, bf16[4,384,128]{2,1,0:T(8,128)(2,1)S(1)} %all_to_all.20.blocks_ref.near_ref, bf16[4,192,128]{2,1,0:T(8,128)(2,1)S(1)} %collective-permute-done.far_ref), custom_call_target="tpu_custom_call" | custom-call | flops 6000000000 | bytes 2000000 | tf_op jit(solution)/shard_map/first/pallas_call | solution.py:350
  49.0 1.1 %middle.1 = (bf16[8,64,128]{2,1,0:T(8,128)(2,1)S(1)}, f32[128,128]{1,0:T(8,128)S(1)}) custom-call(s32[2,6]{1,0:T(2,128)S(1)} %copy-done.1, f32[1024,128]{1,0:T(8,128)S(1)} %get-tuple-element.13.state_ref, bf16[128,128]{1,0:T(8,128)(2,1)S(1)} %get-tuple-element.14.query_ref, bf16[8,128,128]{2,1,0:T(8,128)(2,1)S(1)} %bitcast.3), custom_call_target="tpu_custom_call" | custom-call | flops 2000000000 | bytes 2000000 | tf_op jit(solution)/shard_map/middle/pallas_call | solution.py:368
  50.2 0.0 copy-start
  50.2 1.7 %all-to-all-done.2.blocks_ref = bf16[8,128,128]{2,1,0:T(8,128)(2,1)S(1)} async-done(((bf16[8,128,128]{2,1,0:T(8,128)(2,1)}), bf16[8,128,128]{2,1,0:T(8,128)(2,1)S(1)}, u32[]{:S(2)}, u32[]{:S(2)}) %all-to-all-start.2) | async-done | bytes 262176 | tf_op jit(solution)/shard_map/all_to_all | solution.py:367
  51.9 0.9 %outer.1 = bf16[8,64,128]{2,1,0:T(8,128)(2,1)S(1)} custom-call(s32[2,6]{1,0:T(2,128)S(1)} %copy-done.1, f32[128,128]{1,0:T(8,128)S(1)} %get-tuple-element.16.merged_ref, bf16[16,128]{1,0:T(8,128)(2,1)S(1)} %get-tuple-element.17.query_ref, bf16[8,128,128]{2,1,0:T(8,128)(2,1)S(1)} %all-to-all-done.2.blocks_ref, ...), custom_call_target="tpu_custom_call", output_to_operand_aliasing={{}: (4, {})} | custom-call | tf_op jit(solution)/shard_map/outer/pallas_call | solution.py:377
  52.8 13.3 %all_to_all.21.blocks_ref = bf16[8,64,128]{2,1,0:T(8,128)(2,1)S(1)} all-to-all(bf16[8,64,128]{2,1,0:T(8,128)(2,1)S(1)} %outer.1), channel_id=1, replica_groups={{7,6,5,4,3,2,1,0},{15,14,13,12,11,10,9,8},{23,22,21,20,19,18,17,16},{31..., dimensions={0} | all-to-all | bytes 262144 | tf_op jit(solution)/shard_map/all_to_all | solution.py:384
  66.1 0.0 copy-done
  66.1 1.0 %project.1 = bf16[128,768]{1,0:T(8,128)(2,1)} custom-call(bf16[8,64,128]{2,1,0:T(8,128)(2,1)S(1)} %all_to_all.21.blocks_ref, bf16[384,768]{1,0:T(8,128)(2,1)S(1)} %copy-done), custom_call_target="tpu_custom_call" | custom-call | tf_op jit(solution)/shard_map/project/pallas_call | solution.py:386
Async XLA Ops:
  1.4 10.2 %copy-start.1 = (s32[2,6]{1,0:T(2,128)S(1)}, s32[2,6]{1,0:T(2,128)}, u32[]{:S(2)}) copy-start(s32[2,6]{1,0:T(2,128)} %offsets_ref.9) | copy-start | bytes 148
  12.5 23.5 %all-to-all-start.1 = ((bf16[16,64,128]{2,1,0:T(8,128)(2,1)}), bf16[16,64,128]{2,1,0:T(8,128)(2,1)S(1)}, u32[]{:S(2)}, u32[]{:S(2)}) async-start(bf16[16,64,128]{2,1,0:T(8,128)(2,1)} %get-tuple-element.15), calls=%async_computation.1 | async-start | bytes 524288 | tf_op jit(solution)/shard_map/all_to_all | solution.py:347
  30.8 14.2 %collective-permute-start = (bf16[4,192,128]{2,1,0:T(8,128)(2,1)S(1)}, bf16[4,192,128]{2,1,0:T(8,128)(2,1)S(1)}, u32[]{:S(2)}, u32[]{:S(2)}) collective-permute-start(bf16[4,192,128]{2,1,0:T(8,128)(2,1)S(1)} %get-tuple-element.12), channel_id=1, source_target_pairs={{0,4},{1,5},{2,6},{3,7},{4,0},{5,1},{6,2},{7,3},{8,12},{9,13},{10,... | collective-permute-start | bytes 589832 | tf_op jit(solution)/shard_map/ppermute | solution.py:349
  37.1 14.8 %all-to-all-start.2 = ((bf16[8,128,128]{2,1,0:T(8,128)(2,1)}), bf16[8,128,128]{2,1,0:T(8,128)(2,1)S(1)}, u32[]{:S(2)}, u32[]{:S(2)}) async-start(bf16[8,128,128]{2,1,0:T(8,128)(2,1)} %pick_outer.1), calls=%async_computation.2 | async-start | bytes 524288 | tf_op jit(solution)/shard_map/all_to_all | solution.py:367
  50.2 15.9 %copy-start = (bf16[384,768]{1,0:T(8,128)(2,1)S(1)}, bf16[384,768]{1,0:T(8,128)(2,1)}, u32[]{:S(2)}) copy-start(bf16[384,768]{1,0:T(8,128)(2,1)} %weight_ref.1) | copy-start | bytes 1769476

commit v11 on v10

--- a/solution.py
+++ b/solution.py
@@ -68,35 +68,37 @@
     return chosen.astype(F32).astype(BF16)
 
 
-def against(query, block_ref, index):
+def product_of(one, two):
+    return jnp.dot(one, two, preferred_element_type=F32)
+
+
+def against(query, keys_ref):
     return lax.dot_general(
-        query, block_ref[index, 0:ROWS, :], (((1,), (1,)), ((), ())), preferred_element_type=F32
+        query, keys_ref[...], (((1,), (1,)), ((), ())), preferred_element_type=F32
     )
 
 
-def level(query, block_ref, self_masks, seen=None):
+def level(query, keys_ref, self_masks, seen=None):
     count = query.shape[0]
+    if seen is None:
+        found = against(jnp.concatenate([query, marks()], axis=0), keys_ref)
+        seen = found[count:, :]
+    else:
+        found = against(query, keys_ref)
     parts = []
-    if seen is None:
-        query = jnp.concatenate([query, marks()], axis=0)
     for c in range(PEERS):
-        part = against(query, block_ref, c)
-        seen_part = part[count:, :] if seen is None else seen[c]
-        hidden = seen_part[0:1, :] > F32(MARK / 2)
-        masked = part[0:count, :] + jnp.where(hidden, F32(FAR), F32(0.0))
+        at = slice(c * ROWS, (c + 1) * ROWS)
+        hidden = seen[0:1, at] > F32(MARK / 2)
+        masked = found[0:count, at] + jnp.where(hidden, F32(FAR), F32(0.0))
         if self_masks[c] is not None:
-            masked = jnp.where(self_masks[c] & hidden, seen_part[1:2, :], masked)
+            masked = jnp.where(self_masks[c] & hidden, seen[1:2, at], masked)
         parts.append(masked)
     best = functools.reduce(jnp.maximum, parts)
     top = jnp.max(best, axis=1, keepdims=True)
-    sums = None
-    mixture = None
-    for c in range(PEERS):
-        weight = jnp.exp2((parts[c] - top) * F32(EXP_SCALE))
-        sums = weight if sums is None else sums + weight
-        add = jnp.dot(weight.astype(BF16), block_ref[c, 0:ROWS, :], preferred_element_type=F32)
-        mixture = add if mixture is None else mixture + add
-    total = jnp.sum(sums, axis=1, keepdims=True)
+    weights = [jnp.exp2((part - top) * F32(EXP_SCALE)) for part in parts]
+    total = jnp.sum(functools.reduce(jnp.add, weights), axis=1, keepdims=True)
+    probs = jnp.concatenate([weight.astype(BF16) for weight in weights], axis=1)
+    mixture = product_of(probs, keys_ref[...])
     lane = lanes(mixture.shape)
     return jnp.where(lane < 32, top, jnp.where(lane < 64, total, mixture))
 
@@ -112,10 +114,6 @@
 
 def divided(state):
     return state / state[:, 32:33]
-
-
-def product_of(one, two):
-    return jnp.dot(one, two, preferred_element_type=F32)
 
 
 def pack_kernel(query_hbm, key_hbm, value_hbm, valid_hbm, out_ref, query_ref, key_ref, value_ref, valid_ref, sems):
@@ -199,27 +197,29 @@
 
 
 def first_kernel(
-    offsets_ref, near_ref, far_ref, state_ref, middle_ref, outer_ref, blocks_ref, wide, narrow
+    offsets_ref, near_ref, far_ref, state_ref, middle_ref, outer_ref, keys_ref, pairs_ref, wide, narrow
 ):
     middle, stride = shifts(offsets_ref)
     mine = my_half()
     for c in range(NEAR):
-        blocks_ref[mine * NEAR + c] = near_ref[c ^ NEAR_TURN, 0:FIRST_BLOCK, :]
-        blocks_ref[(1 - mine) * NEAR + c] = far_ref[c]
+        for half, ref, place in ((mine, near_ref, c ^ NEAR_TURN), (1 - mine, far_ref, c)):
+            block = half * NEAR + c
+            start = pl.multiple_of(block * ROWS, ROWS)
+            keys_ref[pl.ds(start, ROWS), :] = ref[place, 0:ROWS, :]
+            pairs_ref[block] = ref[place, ROWS:FIRST_BLOCK, :]
     half = ROWS // 2
     low = lanes((half, 2 * HD)) < HD
     diagonal = rows((ROWS, ROWS)) == lanes((ROWS, ROWS))
-    reader = marks()
-    seen = [against(reader, blocks_ref, c) for c in range(PEERS)]
+    seen = against(marks(), keys_ref)
     for j in range(PEERS):
-        pair = blocks_ref[j, ROWS:FIRST_BLOCK, :].astype(F32)
+        pair = pairs_ref[j].astype(F32)
         wide[j * ROWS : j * ROWS + half, :] = jnp.where(low, pair, F32(0.0))
         wide[j * ROWS + half : (j + 1) * ROWS, :] = jnp.where(
             low, pltpu.roll(pair, HD, 1), F32(0.0)
         )
         query = wide[j * ROWS : (j + 1) * ROWS, :].astype(BF16)
         masks = [diagonal if c == j else None for c in range(PEERS)]
-        state_ref[j * ROWS : (j + 1) * ROWS, :] = level(query, blocks_ref, masks, seen)
+        state_ref[j * ROWS : (j + 1) * ROWS, :] = level(query, keys_ref, masks, seen)
     picked = wide[pl.ds(middle, ROWS, stride=8), :]
     middle_ref[...] = picked.astype(BF16)
     narrow[...] = picked
@@ -352,7 +352,12 @@
         "first",
         (shaped(PEERS * ROWS, 2 * HD, dtype=F32), shaped(ROWS, 2 * HD), shaped(ROWS // 8, 2 * HD)),
         [VMEM, VMEM, VMEM],
-        [pltpu.VMEM((PEERS, FIRST_BLOCK, 2 * HD), BF16), wide, narrow],
+        [
+            pltpu.VMEM((PEERS * ROWS, 2 * HD), BF16),
+            pltpu.VMEM((PEERS, ROWS // 2, 2 * HD), BF16),
+            wide,
+            narrow,
+        ],
         flops=6_000_000_000,
         moved=2_000_000,
     )(offsets, near, far)
@@ -373,14 +378,14 @@
         [wide],
         flops=2_000_000_000,
         moved=2_000_000,
-    )(offsets, state, middle_query, middle_blocks)
+    )(offsets, state, middle_query, middle_blocks.reshape(PEERS * ROWS, 2 * HD))
     combined = call(
         outer_kernel,
         "outer",
         shaped(PEERS, ROWS // 2, 2 * HD),
         [VMEM, VMEM, VMEM, VMEM, VMEM],
         aliases={4: 0},
-    )(offsets, merged, outer_query, outer_blocks, before)
+    )(offsets, merged, outer_query, outer_blocks.reshape(PEERS * ROWS, 2 * HD), before)
     home = swap(combined, "set", axis_index_groups=[[s ^ HOME_TURN for s in range(PEERS)]])
     width = w_out.shape[1]
     return call(

time: 67.5 us -> 67.3 us (level)
  Pallas kernels: 10.5 us -> 9.09 us
  waiting for transfers between devices: 4.87 us -> 6.03 us
    all_to_all x1, waiting for transfers between devices: 1.75 us -> 2.91 us  [per_device(): swap(outer_send, 'grp', axis_index_groups=[list(GROUP_ORDER)])]
    pallas_call x1, Pallas kernels: 4 us -> 3.05 us  [per_device(): call(first_kernel, 'first', (shaped(PEERS * ROWS, 2 * HD, dtype=F32), sha...]
  transfers between devices with their start and end apart: 3 -> 3, of which waited for: 2 -> 2; matrix products, arithmetic and copies ran while one was open for 0% -> 0% of each run, Pallas kernels for 9% -> 8%
where the time goes in v11:
time: 67.3 us; the launch traced here: 66.9 us
  starting transfers between devices  28.3 us (42%)
  blocking collectives  23.4 us (35%)
  Pallas kernels  9.09 us (14%)
  waiting for transfers between devices  6.03 us (9%)
    all_to_all x1, starting transfers between devices, per_device(): swap(middle_send, ('blk', 'set'), axis_index_groups=middle_groups)  18.2 us
    all_to_all x1, blocking collectives, per_device(): swap(combined, 'set', axis_index_groups=[[s ^ HOME_TURN for s in range(PE...  13.3 us
    all_to_all x1, blocking collectives, per_device(): near = swap(packed, 'set', axis_index_groups=near_groups)  10.1 us
    all_to_all x1, starting transfers between devices, per_device(): swap(outer_send, 'grp', axis_index_groups=[list(GROUP_ORDER)])  7.9 us
    all_to_all x1, waiting for transfers between devices, per_device(): swap(middle_send, ('blk', 'set'), axis_index_groups=middle_groups)  3.12 us
    pallas_call x1, Pallas kernels, per_device(): call(first_kernel, 'first', (shaped(PEERS * ROWS, 2 * HD, dtype=F32), sha...  3.05 us
    all_to_all x1, waiting for transfers between devices, per_device(): swap(outer_send, 'grp', axis_index_groups=[list(GROUP_ORDER)])  2.91 us
    ppermute x1, starting transfers between devices, per_device(): lax.ppermute(cross, 'set', [(i, (i + NEAR) % PEERS) for i in range(PEERS)])  2.13 us
  transfers between devices with their start and end apart: 3, of which 2 were waited for; matrix products, arithmetic and copies ran while one was open for 0% of the time, Pallas kernels for 8%

profile of v11, /device:TPU:1, one launch (start us, length us, event | category | flops | bytes accessed | tf_op | source)
XLA Modules:
  0.0 66.9 jit_solution(2535440765940670151)
XLA Ops:
  0.0 1.4 %pack.1 = bf16[4,384,128]{2,1,0:T(8,128)(2,1)S(1)} custom-call(bf16[128,384]{1,0:T(8,128)(2,1)} %query_hbm.1, bf16[128,384]{1,0:T(8,128)(2,1)} %key_hbm.1, bf16[128,384]{1,0:T(8,128)(2,1)} %value_hbm.1, s32[1,128]{1,0:T(1,128)} %bitcast.7), custom_call_target="tpu_custom_call" | custom-call | tf_op jit(solution)/shard_map/pack/pallas_call | solution.py:324
  1.4 0.0 copy-start.1
  1.4 10.1 %all_to_all.20.blocks_ref.near_ref = bf16[4,384,128]{2,1,0:T(8,128)(2,1)S(1)} all-to-all(bf16[4,384,128]{2,1,0:T(8,128)(2,1)S(1)} %pack.1), channel_id=1, replica_groups={{3,2,1,0},{7,6,5,4},{11,10,9,8},{15,14,13,12},{19,18,17,16},{23,22,21,2..., dimensions={0} | all-to-all | bytes 786432 | tf_op jit(solution)/shard_map/all_to_all | solution.py:332
  11.5 0.0 copy-done.1
  11.5 1.0 %pick_middle.1 = (bf16[16,64,128]{2,1,0:T(8,128)(2,1)}, bf16[4,192,128]{2,1,0:T(8,128)(2,1)S(1)}) custom-call(s32[2,6]{1,0:T(2,128)S(1)} %copy-done.1, bf16[4,384,128]{2,1,0:T(8,128)(2,1)S(1)} %all_to_all.20.blocks_ref.near_ref), custom_call_target="tpu_custom_call" | custom-call | tf_op jit(solution)/shard_map/pick_middle/pallas_call | solution.py:333
  12.5 18.2 %all-to-all-start.1 = ((bf16[16,64,128]{2,1,0:T(8,128)(2,1)}), bf16[16,64,128]{2,1,0:T(8,128)(2,1)S(1)}, u32[]{:S(2)}, u32[]{:S(2)}) async-start(bf16[16,64,128]{2,1,0:T(8,128)(2,1)} %get-tuple-element.15), calls=%async_computation.1 | async-start | bytes 524288 | tf_op jit(solution)/shard_map/all_to_all | solution.py:347
  30.8 2.1 %collective-permute-start = (bf16[4,192,128]{2,1,0:T(8,128)(2,1)S(1)}, bf16[4,192,128]{2,1,0:T(8,128)(2,1)S(1)}, u32[]{:S(2)}, u32[]{:S(2)}) collective-permute-start(bf16[4,192,128]{2,1,0:T(8,128)(2,1)S(1)} %get-tuple-element.12), channel_id=1, source_target_pairs={{0,4},{1,5},{2,6},{3,7},{4,0},{5,1},{6,2},{7,3},{8,12},{9,13},{10,... | collective-permute-start | bytes 589832 | tf_op jit(solution)/shard_map/ppermute | solution.py:349
  32.9 3.1 %all-to-all-done.1 = bf16[16,64,128]{2,1,0:T(8,128)(2,1)S(1)} async-done(((bf16[16,64,128]{2,1,0:T(8,128)(2,1)}), bf16[16,64,128]{2,1,0:T(8,128)(2,1)S(1)}, u32[]{:S(2)}, u32[]{:S(2)}) %all-to-all-start.1) | async-done | bytes 262176 | tf_op jit(solution)/shard_map/all_to_all | solution.py:347
  36.0 1.1 %pick_outer.1 = bf16[8,128,128]{2,1,0:T(8,128)(2,1)} custom-call(s32[2,6]{1,0:T(2,128)S(1)} %copy-done.1, bf16[8,128,128]{2,1,0:T(8,128)(2,1)S(1)} %bitcast.5), custom_call_target="tpu_custom_call" | custom-call | tf_op jit(solution)/shard_map/pick_outer/pallas_call | solution.py:364
  37.1 7.9 %all-to-all-start.2 = ((bf16[8,128,128]{2,1,0:T(8,128)(2,1)}), bf16[8,128,128]{2,1,0:T(8,128)(2,1)S(1)}, u32[]{:S(2)}, u32[]{:S(2)}) async-start(bf16[8,128,128]{2,1,0:T(8,128)(2,1)} %pick_outer.1), calls=%async_computation.2 | async-start | bytes 524288 | tf_op jit(solution)/shard_map/all_to_all | solution.py:372
  45.0 0.0 collective-permute-done.far_ref
  45.0 3.0 %first.1 = (f32[1024,128]{1,0:T(8,128)S(1)}, bf16[128,128]{1,0:T(8,128)(2,1)S(1)}, bf16[16,128]{1,0:T(8,128)(2,1)S(1)}) custom-call(s32[2,6]{1,0:T(2,128)S(1)} %copy-done.1, bf16[4,384,128]{2,1,0:T(8,128)(2,1)S(1)} %all_to_all.20.blocks_ref.near_ref, bf16[4,192,128]{2,1,0:T(8,128)(2,1)S(1)} %collective-permute-done.far_ref), custom_call_target="tpu_custom_call" | custom-call | flops 6000000000 | bytes 2000000 | tf_op jit(solution)/shard_map/first/pallas_call | solution.py:350
  48.1 0.9 %middle.1 = (bf16[8,64,128]{2,1,0:T(8,128)(2,1)S(1)}, f32[128,128]{1,0:T(8,128)S(1)}) custom-call(s32[2,6]{1,0:T(2,128)S(1)} %copy-done.1, f32[1024,128]{1,0:T(8,128)S(1)} %get-tuple-element.13.state_ref, bf16[128,128]{1,0:T(8,128)(2,1)S(1)} %get-tuple-element.14.query_ref, bf16[1024,128]{1,0:T(8,128)(2,1)S(1)} %bitcast.6), custom_call_target="tpu_custom_call" | custom-call | flops 2000000000 | bytes 2000000 | tf_op jit(solution)/shard_map/middle/pallas_call | solution.py:373
  49.0 0.0 copy-start
  49.0 2.9 %all-to-all-done.2 = bf16[8,128,128]{2,1,0:T(8,128)(2,1)S(1)} async-done(((bf16[8,128,128]{2,1,0:T(8,128)(2,1)}), bf16[8,128,128]{2,1,0:T(8,128)(2,1)S(1)}, u32[]{:S(2)}, u32[]{:S(2)}) %all-to-all-start.2) | async-done | bytes 262176 | tf_op jit(solution)/shard_map/all_to_all | solution.py:372
  51.9 0.7 %outer.1 = bf16[8,64,128]{2,1,0:T(8,128)(2,1)S(1)} custom-call(s32[2,6]{1,0:T(2,128)S(1)} %copy-done.1, f32[128,128]{1,0:T(8,128)S(1)} %get-tuple-element.16.merged_ref, bf16[16,128]{1,0:T(8,128)(2,1)S(1)} %get-tuple-element.17.query_ref, bf16[1024,128]{1,0:T(8,128)(2,1)S(1)} %bitcast.4, ...), custom_call_target="tpu_custom_call", output_to_operand_aliasing={{}: (4, {})} | custom-call | tf_op jit(solution)/shard_map/outer/pallas_call | solution.py:382
  52.6 13.3 %all_to_all.21.blocks_ref = bf16[8,64,128]{2,1,0:T(8,128)(2,1)S(1)} all-to-all(bf16[8,64,128]{2,1,0:T(8,128)(2,1)S(1)} %outer.1), channel_id=1, replica_groups={{7,6,5,4,3,2,1,0},{15,14,13,12,11,10,9,8},{23,22,21,20,19,18,17,16},{31..., dimensions={0} | all-to-all | bytes 262144 | tf_op jit(solution)/shard_map/all_to_all | solution.py:389
  65.9 0.0 copy-done
  65.9 1.0 %project.1 = bf16[128,768]{1,0:T(8,128)(2,1)} custom-call(bf16[8,64,128]{2,1,0:T(8,128)(2,1)S(1)} %all_to_all.21.blocks_ref, bf16[384,768]{1,0:T(8,128)(2,1)S(1)} %copy-done), custom_call_target="tpu_custom_call" | custom-call | tf_op jit(solution)/shard_map/project/pallas_call | solution.py:391
Async XLA Ops:
  1.4 10.2 %copy-start.1 = (s32[2,6]{1,0:T(2,128)S(1)}, s32[2,6]{1,0:T(2,128)}, u32[]{:S(2)}) copy-start(s32[2,6]{1,0:T(2,128)} %offsets_ref.9) | copy-start | bytes 148
  12.5 23.5 %all-to-all-start.1 = ((bf16[16,64,128]{2,1,0:T(8,128)(2,1)}), bf16[16,64,128]{2,1,0:T(8,128)(2,1)S(1)}, u32[]{:S(2)}, u32[]{:S(2)}) async-start(bf16[16,64,128]{2,1,0:T(8,128)(2,1)} %get-tuple-element.15), calls=%async_computation.1 | async-start | bytes 524288 | tf_op jit(solution)/shard_map/all_to_all | solution.py:347
  30.8 14.2 %collective-permute-start = (bf16[4,192,128]{2,1,0:T(8,128)(2,1)S(1)}, bf16[4,192,128]{2,1,0:T(8,128)(2,1)S(1)}, u32[]{:S(2)}, u32[]{:S(2)}) collective-permute-start(bf16[4,192,128]{2,1,0:T(8,128)(2,1)S(1)} %get-tuple-element.12), channel_id=1, source_target_pairs={{0,4},{1,5},{2,6},{3,7},{4,0},{5,1},{6,2},{7,3},{8,12},{9,13},{10,... | collective-permute-start | bytes 589832 | tf_op jit(solution)/shard_map/ppermute | solution.py:349
  37.1 14.8 %all-to-all-start.2 = ((bf16[8,128,128]{2,1,0:T(8,128)(2,1)}), bf16[8,128,128]{2,1,0:T(8,128)(2,1)S(1)}, u32[]{:S(2)}, u32[]{:S(2)}) async-start(bf16[8,128,128]{2,1,0:T(8,128)(2,1)} %pick_outer.1), calls=%async_computation.2 | async-start | bytes 524288 | tf_op jit(solution)/shard_map/all_to_all | solution.py:372
  49.0 16.9 %copy-start = (bf16[384,768]{1,0:T(8,128)(2,1)S(1)}, bf16[384,768]{1,0:T(8,128)(2,1)}, u32[]{:S(2)}) copy-start(bf16[384,768]{1,0:T(8,128)(2,1)} %weight_ref.1) | copy-start | bytes 1769476

commit v12 on v11

--- a/solution.py
+++ b/solution.py
@@ -16,7 +16,7 @@
 NEAR_TURN = 3
 BLOCK_TURN = 4
 HALF_TURN = 1
-GROUP_ORDER = (4, 2, 6, 0, 5, 3, 7, 1)
+GROUP_ORDER = (6, 4, 2, 0, 7, 5, 3, 1)
 HOME_TURN = 7
 ROWS = 128
 FIRST_BLOCK = ROWS + ROWS // 2

time: 67.3 us -> 66.5 us (0.988)
  blocking collectives: 23.4 us -> 22 us
  starting transfers between devices: 28.3 us -> 29.1 us
    all_to_all x1, blocking collectives: 13.3 us -> 11.9 us  [per_device(): swap(combined, 'set', axis_index_groups=[[s ^ HOME_TURN for s in range(PE...]
    all_to_all x1, starting transfers between devices: 7.9 us -> 8.77 us  [per_device(): swap(outer_send, 'grp', axis_index_groups=[list(GROUP_ORDER)])]
where the time goes in v12:
time: 66.5 us; the launch traced here: 66 us
  starting transfers between devices  29.1 us (44%)
  blocking collectives  22 us (33%)
  Pallas kernels  9.07 us (14%)
  waiting for transfers between devices  5.72 us (9%)
    all_to_all x1, starting transfers between devices, per_device(): swap(middle_send, ('blk', 'set'), axis_index_groups=middle_groups)  18.2 us
    all_to_all x1, blocking collectives, per_device(): swap(combined, 'set', axis_index_groups=[[s ^ HOME_TURN for s in range(PE...  11.9 us
    all_to_all x1, blocking collectives, per_device(): near = swap(packed, 'set', axis_index_groups=near_groups)  10.1 us
    all_to_all x1, starting transfers between devices, per_device(): swap(outer_send, 'grp', axis_index_groups=[list(GROUP_ORDER)])  8.77 us
    all_to_all x1, waiting for transfers between devices, per_device(): swap(middle_send, ('blk', 'set'), axis_index_groups=middle_groups)  3.12 us
    pallas_call x1, Pallas kernels, per_device(): call(first_kernel, 'first', (shaped(PEERS * ROWS, 2 * HD, dtype=F32), sha...  3.03 us
    all_to_all x1, waiting for transfers between devices, per_device(): swap(outer_send, 'grp', axis_index_groups=[list(GROUP_ORDER)])  2.6 us
    ppermute x1, starting transfers between devices, per_device(): lax.ppermute(cross, 'set', [(i, (i + NEAR) % PEERS) for i in range(PEERS)])  2.13 us
  transfers between devices with their start and end apart: 3, of which 2 were waited for; matrix products, arithmetic and copies ran while one was open for 0% of the time, Pallas kernels for 8%

profile of v12, /device:TPU:1, one launch (start us, length us, event | category | flops | bytes accessed | tf_op | source)
XLA Modules:
  0.0 66.0 jit_solution(15652774172188678100)
XLA Ops:
  0.0 1.4 %pack.1 = bf16[4,384,128]{2,1,0:T(8,128)(2,1)S(1)} custom-call(bf16[128,384]{1,0:T(8,128)(2,1)} %query_hbm.1, bf16[128,384]{1,0:T(8,128)(2,1)} %key_hbm.1, bf16[128,384]{1,0:T(8,128)(2,1)} %value_hbm.1, s32[1,128]{1,0:T(1,128)} %bitcast.7), custom_call_target="tpu_custom_call" | custom-call | tf_op jit(solution)/shard_map/pack/pallas_call | solution.py:324
  1.4 0.0 copy-start.1
  1.4 10.1 %all_to_all.20.blocks_ref.near_ref = bf16[4,384,128]{2,1,0:T(8,128)(2,1)S(1)} all-to-all(bf16[4,384,128]{2,1,0:T(8,128)(2,1)S(1)} %pack.1), channel_id=1, replica_groups={{3,2,1,0},{7,6,5,4},{11,10,9,8},{15,14,13,12},{19,18,17,16},{23,22,21,2..., dimensions={0} | all-to-all | bytes 786432 | tf_op jit(solution)/shard_map/all_to_all | solution.py:332
  11.5 0.0 copy-done.1
  11.5 1.0 %pick_middle.1 = (bf16[16,64,128]{2,1,0:T(8,128)(2,1)}, bf16[4,192,128]{2,1,0:T(8,128)(2,1)S(1)}) custom-call(s32[2,6]{1,0:T(2,128)S(1)} %copy-done.1, bf16[4,384,128]{2,1,0:T(8,128)(2,1)S(1)} %all_to_all.20.blocks_ref.near_ref), custom_call_target="tpu_custom_call" | custom-call | tf_op jit(solution)/shard_map/pick_middle/pallas_call | solution.py:333
  12.5 18.2 %all-to-all-start.1 = ((bf16[16,64,128]{2,1,0:T(8,128)(2,1)}), bf16[16,64,128]{2,1,0:T(8,128)(2,1)S(1)}, u32[]{:S(2)}, u32[]{:S(2)}) async-start(bf16[16,64,128]{2,1,0:T(8,128)(2,1)} %get-tuple-element.15), calls=%async_computation.1 | async-start | bytes 524288 | tf_op jit(solution)/shard_map/all_to_all | solution.py:347
  30.8 2.1 %collective-permute-start = (bf16[4,192,128]{2,1,0:T(8,128)(2,1)S(1)}, bf16[4,192,128]{2,1,0:T(8,128)(2,1)S(1)}, u32[]{:S(2)}, u32[]{:S(2)}) collective-permute-start(bf16[4,192,128]{2,1,0:T(8,128)(2,1)S(1)} %get-tuple-element.12), channel_id=1, source_target_pairs={{0,4},{1,5},{2,6},{3,7},{4,0},{5,1},{6,2},{7,3},{8,12},{9,13},{10,... | collective-permute-start | bytes 589832 | tf_op jit(solution)/shard_map/ppermute | solution.py:349
  32.9 3.1 %all-to-all-done.1 = bf16[16,64,128]{2,1,0:T(8,128)(2,1)S(1)} async-done(((bf16[16,64,128]{2,1,0:T(8,128)(2,1)}), bf16[16,64,128]{2,1,0:T(8,128)(2,1)S(1)}, u32[]{:S(2)}, u32[]{:S(2)}) %all-to-all-start.1) | async-done | bytes 262176 | tf_op jit(solution)/shard_map/all_to_all | solution.py:347
  36.0 1.1 %pick_outer.1 = bf16[8,128,128]{2,1,0:T(8,128)(2,1)} custom-call(s32[2,6]{1,0:T(2,128)S(1)} %copy-done.1, bf16[8,128,128]{2,1,0:T(8,128)(2,1)S(1)} %bitcast.5), custom_call_target="tpu_custom_call" | custom-call | tf_op jit(solution)/shard_map/pick_outer/pallas_call | solution.py:364
  37.1 8.8 %all-to-all-start.2 = ((bf16[8,128,128]{2,1,0:T(8,128)(2,1)}), bf16[8,128,128]{2,1,0:T(8,128)(2,1)S(1)}, u32[]{:S(2)}, u32[]{:S(2)}) async-start(bf16[8,128,128]{2,1,0:T(8,128)(2,1)} %pick_outer.1), calls=%async_computation.2 | async-start | bytes 524288 | tf_op jit(solution)/shard_map/all_to_all | solution.py:372
  45.9 0.0 collective-permute-done.far_ref
  45.9 3.0 %first.1 = (f32[1024,128]{1,0:T(8,128)S(1)}, bf16[128,128]{1,0:T(8,128)(2,1)S(1)}, bf16[16,128]{1,0:T(8,128)(2,1)S(1)}) custom-call(s32[2,6]{1,0:T(2,128)S(1)} %copy-done.1, bf16[4,384,128]{2,1,0:T(8,128)(2,1)S(1)} %all_to_all.20.blocks_ref.near_ref, bf16[4,192,128]{2,1,0:T(8,128)(2,1)S(1)} %collective-permute-done.far_ref), custom_call_target="tpu_custom_call" | custom-call | flops 6000000000 | bytes 2000000 | tf_op jit(solution)/shard_map/first/pallas_call | solution.py:350
  48.9 0.9 %middle.1 = (bf16[8,64,128]{2,1,0:T(8,128)(2,1)S(1)}, f32[128,128]{1,0:T(8,128)S(1)}) custom-call(s32[2,6]{1,0:T(2,128)S(1)} %copy-done.1, f32[1024,128]{1,0:T(8,128)S(1)} %get-tuple-element.13.state_ref, bf16[128,128]{1,0:T(8,128)(2,1)S(1)} %get-tuple-element.14.query_ref, bf16[1024,128]{1,0:T(8,128)(2,1)S(1)} %bitcast.6), custom_call_target="tpu_custom_call" | custom-call | flops 2000000000 | bytes 2000000 | tf_op jit(solution)/shard_map/middle/pallas_call | solution.py:373
  49.9 0.0 copy-start
  49.9 2.6 %all-to-all-done.2 = bf16[8,128,128]{2,1,0:T(8,128)(2,1)S(1)} async-done(((bf16[8,128,128]{2,1,0:T(8,128)(2,1)}), bf16[8,128,128]{2,1,0:T(8,128)(2,1)S(1)}, u32[]{:S(2)}, u32[]{:S(2)}) %all-to-all-start.2) | async-done | bytes 262176 | tf_op jit(solution)/shard_map/all_to_all | solution.py:372
  52.5 0.7 %outer.1 = bf16[8,64,128]{2,1,0:T(8,128)(2,1)S(1)} custom-call(s32[2,6]{1,0:T(2,128)S(1)} %copy-done.1, f32[128,128]{1,0:T(8,128)S(1)} %get-tuple-element.16.merged_ref, bf16[16,128]{1,0:T(8,128)(2,1)S(1)} %get-tuple-element.17.query_ref, bf16[1024,128]{1,0:T(8,128)(2,1)S(1)} %bitcast.4, ...), custom_call_target="tpu_custom_call", output_to_operand_aliasing={{}: (4, {})} | custom-call | tf_op jit(solution)/shard_map/outer/pallas_call | solution.py:382
  53.2 11.9 %all_to_all.21.blocks_ref = bf16[8,64,128]{2,1,0:T(8,128)(2,1)S(1)} all-to-all(bf16[8,64,128]{2,1,0:T(8,128)(2,1)S(1)} %outer.1), channel_id=1, replica_groups={{7,6,5,4,3,2,1,0},{15,14,13,12,11,10,9,8},{23,22,21,20,19,18,17,16},{31..., dimensions={0} | all-to-all | bytes 262144 | tf_op jit(solution)/shard_map/all_to_all | solution.py:389
  65.0 0.0 copy-done
  65.0 1.0 %project.1 = bf16[128,768]{1,0:T(8,128)(2,1)} custom-call(bf16[8,64,128]{2,1,0:T(8,128)(2,1)S(1)} %all_to_all.21.blocks_ref, bf16[384,768]{1,0:T(8,128)(2,1)S(1)} %copy-done), custom_call_target="tpu_custom_call" | custom-call | tf_op jit(solution)/shard_map/project/pallas_call | solution.py:391
Async XLA Ops:
  1.4 10.2 %copy-start.1 = (s32[2,6]{1,0:T(2,128)S(1)}, s32[2,6]{1,0:T(2,128)}, u32[]{:S(2)}) copy-start(s32[2,6]{1,0:T(2,128)} %offsets_ref.9) | copy-start | bytes 148
  12.5 23.5 %all-to-all-start.1 = ((bf16[16,64,128]{2,1,0:T(8,128)(2,1)}), bf16[16,64,128]{2,1,0:T(8,128)(2,1)S(1)}, u32[]{:S(2)}, u32[]{:S(2)}) async-start(bf16[16,64,128]{2,1,0:T(8,128)(2,1)} %get-tuple-element.15), calls=%async_computation.1 | async-start | bytes 524288 | tf_op jit(solution)/shard_map/all_to_all | solution.py:347
  30.8 15.1 %collective-permute-start = (bf16[4,192,128]{2,1,0:T(8,128)(2,1)S(1)}, bf16[4,192,128]{2,1,0:T(8,128)(2,1)S(1)}, u32[]{:S(2)}, u32[]{:S(2)}) collective-permute-start(bf16[4,192,128]{2,1,0:T(8,128)(2,1)S(1)} %get-tuple-element.12), channel_id=1, source_target_pairs={{0,4},{1,5},{2,6},{3,7},{4,0},{5,1},{6,2},{7,3},{8,12},{9,13},{10,... | collective-permute-start | bytes 589832 | tf_op jit(solution)/shard_map/ppermute | solution.py:349
  37.1 15.4 %all-to-all-start.2 = ((bf16[8,128,128]{2,1,0:T(8,128)(2,1)}), bf16[8,128,128]{2,1,0:T(8,128)(2,1)S(1)}, u32[]{:S(2)}, u32[]{:S(2)}) async-start(bf16[8,128,128]{2,1,0:T(8,128)(2,1)} %pick_outer.1), calls=%async_computation.2 | async-start | bytes 524288 | tf_op jit(solution)/shard_map/all_to_all | solution.py:372
  49.9 15.2 %copy-start = (bf16[384,768]{1,0:T(8,128)(2,1)S(1)}, bf16[384,768]{1,0:T(8,128)(2,1)}, u32[]{:S(2)}) copy-start(bf16[384,768]{1,0:T(8,128)(2,1)} %weight_ref.1) | copy-start | bytes 1769476

commit v13 on v12

--- a/solution.py
+++ b/solution.py
@@ -16,7 +16,7 @@
 NEAR_TURN = 3
 BLOCK_TURN = 4
 HALF_TURN = 1
-GROUP_ORDER = (6, 4, 2, 0, 7, 5, 3, 1)
+GROUP_ORDER = (6, 4, 7, 5, 2, 0, 3, 1)
 HOME_TURN = 7
 ROWS = 128
 FIRST_BLOCK = ROWS + ROWS // 2

time: 66.5 us -> 67.7 us (1.018)
  waiting for transfers between devices: 5.72 us -> 6.91 us
    all_to_all x1, waiting for transfers between devices: 2.6 us -> 3.79 us  [per_device(): swap(outer_send, 'grp', axis_index_groups=[list(GROUP_ORDER)])]
where the time goes in v13:
time: 67.7 us; the launch traced here: 67.2 us
  starting transfers between devices  29.1 us (43%)
  blocking collectives  22 us (32%)
  Pallas kernels  9.08 us (13%)
  waiting for transfers between devices  6.91 us (10%)
    all_to_all x1, starting transfers between devices, per_device(): swap(middle_send, ('blk', 'set'), axis_index_groups=middle_groups)  18.2 us
    all_to_all x1, blocking collectives, per_device(): swap(combined, 'set', axis_index_groups=[[s ^ HOME_TURN for s in range(PE...  11.9 us
    all_to_all x1, blocking collectives, per_device(): near = swap(packed, 'set', axis_index_groups=near_groups)  10.1 us
    all_to_all x1, starting transfers between devices, per_device(): swap(outer_send, 'grp', axis_index_groups=[list(GROUP_ORDER)])  8.78 us
    all_to_all x1, waiting for transfers between devices, per_device(): swap(outer_send, 'grp', axis_index_groups=[list(GROUP_ORDER)])  3.79 us
    all_to_all x1, waiting for transfers between devices, per_device(): swap(middle_send, ('blk', 'set'), axis_index_groups=middle_groups)  3.12 us
    pallas_call x1, Pallas kernels, per_device(): call(first_kernel, 'first', (shaped(PEERS * ROWS, 2 * HD, dtype=F32), sha...  3.04 us
    ppermute x1, starting transfers between devices, per_device(): lax.ppermute(cross, 'set', [(i, (i + NEAR) % PEERS) for i in range(PEERS)])  2.13 us
  transfers between devices with their start and end apart: 3, of which 2 were waited for; matrix products, arithmetic and copies ran while one was open for 0% of the time, Pallas kernels for 8%

profile of v13, /device:TPU:1, one launch (start us, length us, event | category | flops | bytes accessed | tf_op | source)
XLA Modules:
  0.0 67.2 jit_solution(156181201495074493)
XLA Ops:
  0.0 1.4 %pack.1 = bf16[4,384,128]{2,1,0:T(8,128)(2,1)S(1)} custom-call(bf16[128,384]{1,0:T(8,128)(2,1)} %query_hbm.1, bf16[128,384]{1,0:T(8,128)(2,1)} %key_hbm.1, bf16[128,384]{1,0:T(8,128)(2,1)} %value_hbm.1, s32[1,128]{1,0:T(1,128)} %bitcast.7), custom_call_target="tpu_custom_call" | custom-call | tf_op jit(solution)/shard_map/pack/pallas_call | solution.py:324
  1.4 0.0 copy-start.1
  1.4 10.1 %all_to_all.20.blocks_ref.near_ref = bf16[4,384,128]{2,1,0:T(8,128)(2,1)S(1)} all-to-all(bf16[4,384,128]{2,1,0:T(8,128)(2,1)S(1)} %pack.1), channel_id=1, replica_groups={{3,2,1,0},{7,6,5,4},{11,10,9,8},{15,14,13,12},{19,18,17,16},{23,22,21,2..., dimensions={0} | all-to-all | bytes 786432 | tf_op jit(solution)/shard_map/all_to_all | solution.py:332
  11.5 0.0 copy-done.1
  11.5 1.0 %pick_middle.1 = (bf16[16,64,128]{2,1,0:T(8,128)(2,1)}, bf16[4,192,128]{2,1,0:T(8,128)(2,1)S(1)}) custom-call(s32[2,6]{1,0:T(2,128)S(1)} %copy-done.1, bf16[4,384,128]{2,1,0:T(8,128)(2,1)S(1)} %all_to_all.20.blocks_ref.near_ref), custom_call_target="tpu_custom_call" | custom-call | tf_op jit(solution)/shard_map/pick_middle/pallas_call | solution.py:333
  12.5 18.2 %all-to-all-start.1 = ((bf16[16,64,128]{2,1,0:T(8,128)(2,1)}), bf16[16,64,128]{2,1,0:T(8,128)(2,1)S(1)}, u32[]{:S(2)}, u32[]{:S(2)}) async-start(bf16[16,64,128]{2,1,0:T(8,128)(2,1)} %get-tuple-element.15), calls=%async_computation.1 | async-start | bytes 524288 | tf_op jit(solution)/shard_map/all_to_all | solution.py:347
  30.8 2.1 %collective-permute-start = (bf16[4,192,128]{2,1,0:T(8,128)(2,1)S(1)}, bf16[4,192,128]{2,1,0:T(8,128)(2,1)S(1)}, u32[]{:S(2)}, u32[]{:S(2)}) collective-permute-start(bf16[4,192,128]{2,1,0:T(8,128)(2,1)S(1)} %get-tuple-element.12), channel_id=1, source_target_pairs={{0,4},{1,5},{2,6},{3,7},{4,0},{5,1},{6,2},{7,3},{8,12},{9,13},{10,... | collective-permute-start | bytes 589832 | tf_op jit(solution)/shard_map/ppermute | solution.py:349
  32.9 3.1 %all-to-all-done.1 = bf16[16,64,128]{2,1,0:T(8,128)(2,1)S(1)} async-done(((bf16[16,64,128]{2,1,0:T(8,128)(2,1)}), bf16[16,64,128]{2,1,0:T(8,128)(2,1)S(1)}, u32[]{:S(2)}, u32[]{:S(2)}) %all-to-all-start.1) | async-done | bytes 262176 | tf_op jit(solution)/shard_map/all_to_all | solution.py:347
  36.0 1.1 %pick_outer.1 = bf16[8,128,128]{2,1,0:T(8,128)(2,1)} custom-call(s32[2,6]{1,0:T(2,128)S(1)} %copy-done.1, bf16[8,128,128]{2,1,0:T(8,128)(2,1)S(1)} %bitcast.5), custom_call_target="tpu_custom_call" | custom-call | tf_op jit(solution)/shard_map/pick_outer/pallas_call | solution.py:364
  37.1 8.8 %all-to-all-start.2 = ((bf16[8,128,128]{2,1,0:T(8,128)(2,1)}), bf16[8,128,128]{2,1,0:T(8,128)(2,1)S(1)}, u32[]{:S(2)}, u32[]{:S(2)}) async-start(bf16[8,128,128]{2,1,0:T(8,128)(2,1)} %pick_outer.1), calls=%async_computation.2 | async-start | bytes 524288 | tf_op jit(solution)/shard_map/all_to_all | solution.py:372
  45.9 0.0 collective-permute-done.far_ref
  45.9 3.0 %first.1 = (f32[1024,128]{1,0:T(8,128)S(1)}, bf16[128,128]{1,0:T(8,128)(2,1)S(1)}, bf16[16,128]{1,0:T(8,128)(2,1)S(1)}) custom-call(s32[2,6]{1,0:T(2,128)S(1)} %copy-done.1, bf16[4,384,128]{2,1,0:T(8,128)(2,1)S(1)} %all_to_all.20.blocks_ref.near_ref, bf16[4,192,128]{2,1,0:T(8,128)(2,1)S(1)} %collective-permute-done.far_ref), custom_call_target="tpu_custom_call" | custom-call | flops 6000000000 | bytes 2000000 | tf_op jit(solution)/shard_map/first/pallas_call | solution.py:350
  48.9 0.9 %middle.1 = (bf16[8,64,128]{2,1,0:T(8,128)(2,1)S(1)}, f32[128,128]{1,0:T(8,128)S(1)}) custom-call(s32[2,6]{1,0:T(2,128)S(1)} %copy-done.1, f32[1024,128]{1,0:T(8,128)S(1)} %get-tuple-element.13.state_ref, bf16[128,128]{1,0:T(8,128)(2,1)S(1)} %get-tuple-element.14.query_ref, bf16[1024,128]{1,0:T(8,128)(2,1)S(1)} %bitcast.6), custom_call_target="tpu_custom_call" | custom-call | flops 2000000000 | bytes 2000000 | tf_op jit(solution)/shard_map/middle/pallas_call | solution.py:373
  49.9 0.0 copy-start
  49.9 3.8 %all-to-all-done.2 = bf16[8,128,128]{2,1,0:T(8,128)(2,1)S(1)} async-done(((bf16[8,128,128]{2,1,0:T(8,128)(2,1)}), bf16[8,128,128]{2,1,0:T(8,128)(2,1)S(1)}, u32[]{:S(2)}, u32[]{:S(2)}) %all-to-all-start.2) | async-done | bytes 262176 | tf_op jit(solution)/shard_map/all_to_all | solution.py:372
  53.7 0.7 outer.1
  54.4 11.9 %all_to_all.21.blocks_ref = bf16[8,64,128]{2,1,0:T(8,128)(2,1)S(1)} all-to-all(bf16[8,64,128]{2,1,0:T(8,128)(2,1)S(1)} %outer.1), channel_id=1, replica_groups={{7,6,5,4,3,2,1,0},{15,14,13,12,11,10,9,8},{23,22,21,20,19,18,17,16},{31..., dimensions={0} | all-to-all | bytes 262144 | tf_op jit(solution)/shard_map/all_to_all | solution.py:389
  66.2 0.0 copy-done
  66.3 1.0 %project.1 = bf16[128,768]{1,0:T(8,128)(2,1)} custom-call(bf16[8,64,128]{2,1,0:T(8,128)(2,1)S(1)} %all_to_all.21.blocks_ref, bf16[384,768]{1,0:T(8,128)(2,1)S(1)} %copy-done), custom_call_target="tpu_custom_call" | custom-call | tf_op jit(solution)/shard_map/project/pallas_call | solution.py:391
Async XLA Ops:
  1.4 10.2 %copy-start.1 = (s32[2,6]{1,0:T(2,128)S(1)}, s32[2,6]{1,0:T(2,128)}, u32[]{:S(2)}) copy-start(s32[2,6]{1,0:T(2,128)} %offsets_ref.9) | copy-start | bytes 148
  12.5 23.5 %all-to-all-start.1 = ((bf16[16,64,128]{2,1,0:T(8,128)(2,1)}), bf16[16,64,128]{2,1,0:T(8,128)(2,1)S(1)}, u32[]{:S(2)}, u32[]{:S(2)}) async-start(bf16[16,64,128]{2,1,0:T(8,128)(2,1)} %get-tuple-element.15), calls=%async_computation.1 | async-start | bytes 524288 | tf_op jit(solution)/shard_map/all_to_all | solution.py:347
  30.8 15.1 %collective-permute-start = (bf16[4,192,128]{2,1,0:T(8,128)(2,1)S(1)}, bf16[4,192,128]{2,1,0:T(8,128)(2,1)S(1)}, u32[]{:S(2)}, u32[]{:S(2)}) collective-permute-start(bf16[4,192,128]{2,1,0:T(8,128)(2,1)S(1)} %get-tuple-element.12), channel_id=1, source_target_pairs={{0,4},{1,5},{2,6},{3,7},{4,0},{5,1},{6,2},{7,3},{8,12},{9,13},{10,... | collective-permute-start | bytes 589832 | tf_op jit(solution)/shard_map/ppermute | solution.py:349
  37.1 16.6 %all-to-all-start.2 = ((bf16[8,128,128]{2,1,0:T(8,128)(2,1)}), bf16[8,128,128]{2,1,0:T(8,128)(2,1)S(1)}, u32[]{:S(2)}, u32[]{:S(2)}) async-start(bf16[8,128,128]{2,1,0:T(8,128)(2,1)} %pick_outer.1), calls=%async_computation.2 | async-start | bytes 524288 | tf_op jit(solution)/shard_map/all_to_all | solution.py:372
  49.9 16.4 %copy-start = (bf16[384,768]{1,0:T(8,128)(2,1)S(1)}, bf16[384,768]{1,0:T(8,128)(2,1)}, u32[]{:S(2)}) copy-start(bf16[384,768]{1,0:T(8,128)(2,1)} %weight_ref.1) | copy-start | bytes 1769476

commit v14 on v13

--- a/solution.py
+++ b/solution.py
@@ -16,7 +16,7 @@
 NEAR_TURN = 3
 BLOCK_TURN = 4
 HALF_TURN = 1
-GROUP_ORDER = (6, 4, 7, 5, 2, 0, 3, 1)
+GROUP_ORDER = (6, 0, 2, 4, 7, 1, 3, 5)
 HOME_TURN = 7
 ROWS = 128
 FIRST_BLOCK = ROWS + ROWS // 2

time: 67.7 us -> 67.7 us (level)
  no operation moved by 1% of the time
where the time goes in v14:
time: 67.7 us; the launch traced here: 67.2 us
  starting transfers between devices  29.1 us (43%)
  blocking collectives  22 us (32%)
  Pallas kernels  9.09 us (13%)
  waiting for transfers between devices  6.92 us (10%)
    all_to_all x1, starting transfers between devices, per_device(): swap(middle_send, ('blk', 'set'), axis_index_groups=middle_groups)  18.2 us
    all_to_all x1, blocking collectives, per_device(): swap(combined, 'set', axis_index_groups=[[s ^ HOME_TURN for s in range(PE...  11.9 us
    all_to_all x1, blocking collectives, per_device(): near = swap(packed, 'set', axis_index_groups=near_groups)  10.1 us
    all_to_all x1, starting transfers between devices, per_device(): swap(outer_send, 'grp', axis_index_groups=[list(GROUP_ORDER)])  8.76 us
    all_to_all x1, waiting for transfers between devices, per_device(): swap(outer_send, 'grp', axis_index_groups=[list(GROUP_ORDER)])  3.8 us
    all_to_all x1, waiting for transfers between devices, per_device(): swap(middle_send, ('blk', 'set'), axis_index_groups=middle_groups)  3.12 us
    pallas_call x1, Pallas kernels, per_device(): call(first_kernel, 'first', (shaped(PEERS * ROWS, 2 * HD, dtype=F32), sha...  3.05 us
    ppermute x1, starting transfers between devices, per_device(): lax.ppermute(cross, 'set', [(i, (i + NEAR) % PEERS) for i in range(PEERS)])  2.13 us
  transfers between devices with their start and end apart: 3, of which 2 were waited for; matrix products, arithmetic and copies ran while one was open for 0% of the time, Pallas kernels for 8%

profile of v14, /device:TPU:1, one launch (start us, length us, event | category | flops | bytes accessed | tf_op | source)
XLA Modules:
  0.0 67.2 jit_solution(15506419874000326808)
XLA Ops:
  0.0 1.4 %pack.1 = bf16[4,384,128]{2,1,0:T(8,128)(2,1)S(1)} custom-call(bf16[128,384]{1,0:T(8,128)(2,1)} %query_hbm.1, bf16[128,384]{1,0:T(8,128)(2,1)} %key_hbm.1, bf16[128,384]{1,0:T(8,128)(2,1)} %value_hbm.1, s32[1,128]{1,0:T(1,128)} %bitcast.7), custom_call_target="tpu_custom_call" | custom-call | tf_op jit(solution)/shard_map/pack/pallas_call | solution.py:324
  1.4 0.0 copy-start.1
  1.4 10.1 %all_to_all.20.blocks_ref.near_ref = bf16[4,384,128]{2,1,0:T(8,128)(2,1)S(1)} all-to-all(bf16[4,384,128]{2,1,0:T(8,128)(2,1)S(1)} %pack.1), channel_id=1, replica_groups={{3,2,1,0},{7,6,5,4},{11,10,9,8},{15,14,13,12},{19,18,17,16},{23,22,21,2..., dimensions={0} | all-to-all | bytes 786432 | tf_op jit(solution)/shard_map/all_to_all | solution.py:332
  11.5 0.0 copy-done.1
  11.5 1.0 %pick_middle.1 = (bf16[16,64,128]{2,1,0:T(8,128)(2,1)}, bf16[4,192,128]{2,1,0:T(8,128)(2,1)S(1)}) custom-call(s32[2,6]{1,0:T(2,128)S(1)} %copy-done.1, bf16[4,384,128]{2,1,0:T(8,128)(2,1)S(1)} %all_to_all.20.blocks_ref.near_ref), custom_call_target="tpu_custom_call" | custom-call | tf_op jit(solution)/shard_map/pick_middle/pallas_call | solution.py:333
  12.5 18.2 %all-to-all-start.1 = ((bf16[16,64,128]{2,1,0:T(8,128)(2,1)}), bf16[16,64,128]{2,1,0:T(8,128)(2,1)S(1)}, u32[]{:S(2)}, u32[]{:S(2)}) async-start(bf16[16,64,128]{2,1,0:T(8,128)(2,1)} %get-tuple-element.15), calls=%async_computation.1 | async-start | bytes 524288 | tf_op jit(solution)/shard_map/all_to_all | solution.py:347
  30.8 2.1 %collective-permute-start = (bf16[4,192,128]{2,1,0:T(8,128)(2,1)S(1)}, bf16[4,192,128]{2,1,0:T(8,128)(2,1)S(1)}, u32[]{:S(2)}, u32[]{:S(2)}) collective-permute-start(bf16[4,192,128]{2,1,0:T(8,128)(2,1)S(1)} %get-tuple-element.12), channel_id=1, source_target_pairs={{0,4},{1,5},{2,6},{3,7},{4,0},{5,1},{6,2},{7,3},{8,12},{9,13},{10,... | collective-permute-start | bytes 589832 | tf_op jit(solution)/shard_map/ppermute | solution.py:349
  32.9 3.1 %all-to-all-done.1 = bf16[16,64,128]{2,1,0:T(8,128)(2,1)S(1)} async-done(((bf16[16,64,128]{2,1,0:T(8,128)(2,1)}), bf16[16,64,128]{2,1,0:T(8,128)(2,1)S(1)}, u32[]{:S(2)}, u32[]{:S(2)}) %all-to-all-start.1) | async-done | bytes 262176 | tf_op jit(solution)/shard_map/all_to_all | solution.py:347
  36.0 1.1 %pick_outer.1 = bf16[8,128,128]{2,1,0:T(8,128)(2,1)} custom-call(s32[2,6]{1,0:T(2,128)S(1)} %copy-done.1, bf16[8,128,128]{2,1,0:T(8,128)(2,1)S(1)} %bitcast.5), custom_call_target="tpu_custom_call" | custom-call | tf_op jit(solution)/shard_map/pick_outer/pallas_call | solution.py:364
  37.1 8.8 %all-to-all-start.2 = ((bf16[8,128,128]{2,1,0:T(8,128)(2,1)}), bf16[8,128,128]{2,1,0:T(8,128)(2,1)S(1)}, u32[]{:S(2)}, u32[]{:S(2)}) async-start(bf16[8,128,128]{2,1,0:T(8,128)(2,1)} %pick_outer.1), calls=%async_computation.2 | async-start | bytes 524288 | tf_op jit(solution)/shard_map/all_to_all | solution.py:372
  45.9 0.0 collective-permute-done.far_ref
  45.9 3.0 %first.1 = (f32[1024,128]{1,0:T(8,128)S(1)}, bf16[128,128]{1,0:T(8,128)(2,1)S(1)}, bf16[16,128]{1,0:T(8,128)(2,1)S(1)}) custom-call(s32[2,6]{1,0:T(2,128)S(1)} %copy-done.1, bf16[4,384,128]{2,1,0:T(8,128)(2,1)S(1)} %all_to_all.20.blocks_ref.near_ref, bf16[4,192,128]{2,1,0:T(8,128)(2,1)S(1)} %collective-permute-done.far_ref), custom_call_target="tpu_custom_call" | custom-call | flops 6000000000 | bytes 2000000 | tf_op jit(solution)/shard_map/first/pallas_call | solution.py:350
  48.9 0.9 %middle.1 = (bf16[8,64,128]{2,1,0:T(8,128)(2,1)S(1)}, f32[128,128]{1,0:T(8,128)S(1)}) custom-call(s32[2,6]{1,0:T(2,128)S(1)} %copy-done.1, f32[1024,128]{1,0:T(8,128)S(1)} %get-tuple-element.13.state_ref, bf16[128,128]{1,0:T(8,128)(2,1)S(1)} %get-tuple-element.14.query_ref, bf16[1024,128]{1,0:T(8,128)(2,1)S(1)} %bitcast.6), custom_call_target="tpu_custom_call" | custom-call | flops 2000000000 | bytes 2000000 | tf_op jit(solution)/shard_map/middle/pallas_call | solution.py:373
  49.9 0.0 copy-start
  49.9 3.8 %all-to-all-done.2 = bf16[8,128,128]{2,1,0:T(8,128)(2,1)S(1)} async-done(((bf16[8,128,128]{2,1,0:T(8,128)(2,1)}), bf16[8,128,128]{2,1,0:T(8,128)(2,1)S(1)}, u32[]{:S(2)}, u32[]{:S(2)}) %all-to-all-start.2) | async-done | bytes 262176 | tf_op jit(solution)/shard_map/all_to_all | solution.py:372
  53.7 0.7 %outer.1 = bf16[8,64,128]{2,1,0:T(8,128)(2,1)S(1)} custom-call(s32[2,6]{1,0:T(2,128)S(1)} %copy-done.1, f32[128,128]{1,0:T(8,128)S(1)} %get-tuple-element.16.merged_ref, bf16[16,128]{1,0:T(8,128)(2,1)S(1)} %get-tuple-element.17.query_ref, bf16[1024,128]{1,0:T(8,128)(2,1)S(1)} %bitcast.4, ...), custom_call_target="tpu_custom_call", output_to_operand_aliasing={{}: (4, {})} | custom-call | tf_op jit(solution)/shard_map/outer/pallas_call | solution.py:382
  54.4 11.9 %all_to_all.21.blocks_ref = bf16[8,64,128]{2,1,0:T(8,128)(2,1)S(1)} all-to-all(bf16[8,64,128]{2,1,0:T(8,128)(2,1)S(1)} %outer.1), channel_id=1, replica_groups={{7,6,5,4,3,2,1,0},{15,14,13,12,11,10,9,8},{23,22,21,20,19,18,17,16},{31..., dimensions={0} | all-to-all | bytes 262144 | tf_op jit(solution)/shard_map/all_to_all | solution.py:389
  66.2 0.0 copy-done
  66.3 1.0 %project.1 = bf16[128,768]{1,0:T(8,128)(2,1)} custom-call(bf16[8,64,128]{2,1,0:T(8,128)(2,1)S(1)} %all_to_all.21.blocks_ref, bf16[384,768]{1,0:T(8,128)(2,1)S(1)} %copy-done), custom_call_target="tpu_custom_call" | custom-call | tf_op jit(solution)/shard_map/project/pallas_call | solution.py:391
Async XLA Ops:
  1.4 10.2 %copy-start.1 = (s32[2,6]{1,0:T(2,128)S(1)}, s32[2,6]{1,0:T(2,128)}, u32[]{:S(2)}) copy-start(s32[2,6]{1,0:T(2,128)} %offsets_ref.9) | copy-start | bytes 148
  12.5 23.5 %all-to-all-start.1 = ((bf16[16,64,128]{2,1,0:T(8,128)(2,1)}), bf16[16,64,128]{2,1,0:T(8,128)(2,1)S(1)}, u32[]{:S(2)}, u32[]{:S(2)}) async-start(bf16[16,64,128]{2,1,0:T(8,128)(2,1)} %get-tuple-element.15), calls=%async_computation.1 | async-start | bytes 524288 | tf_op jit(solution)/shard_map/all_to_all | solution.py:347
  30.8 15.1 %collective-permute-start = (bf16[4,192,128]{2,1,0:T(8,128)(2,1)S(1)}, bf16[4,192,128]{2,1,0:T(8,128)(2,1)S(1)}, u32[]{:S(2)}, u32[]{:S(2)}) collective-permute-start(bf16[4,192,128]{2,1,0:T(8,128)(2,1)S(1)} %get-tuple-element.12), channel_id=1, source_target_pairs={{0,4},{1,5},{2,6},{3,7},{4,0},{5,1},{6,2},{7,3},{8,12},{9,13},{10,... | collective-permute-start | bytes 589832 | tf_op jit(solution)/shard_map/ppermute | solution.py:349
  37.1 16.6 %all-to-all-start.2 = ((bf16[8,128,128]{2,1,0:T(8,128)(2,1)}), bf16[8,128,128]{2,1,0:T(8,128)(2,1)S(1)}, u32[]{:S(2)}, u32[]{:S(2)}) async-start(bf16[8,128,128]{2,1,0:T(8,128)(2,1)} %pick_outer.1), calls=%async_computation.2 | async-start | bytes 524288 | tf_op jit(solution)/shard_map/all_to_all | solution.py:372
  49.9 16.4 %copy-start = (bf16[384,768]{1,0:T(8,128)(2,1)S(1)}, bf16[384,768]{1,0:T(8,128)(2,1)}, u32[]{:S(2)}) copy-start(bf16[384,768]{1,0:T(8,128)(2,1)} %weight_ref.1) | copy-start | bytes 1769476

commit v15 on v12

--- a/solution.py
+++ b/solution.py
@@ -13,7 +13,7 @@
 PEERS = 8
 NEAR = 4
 HALF_HEADS = HEADS // 2
-NEAR_TURN = 3
+NEAR_TURN = 2
 BLOCK_TURN = 4
 HALF_TURN = 1
 GROUP_ORDER = (6, 4, 2, 0, 7, 5, 3, 1)

time: 66.5 us -> 66.2 us (level)
  waiting for transfers between devices: 5.72 us -> 6.98 us
  starting transfers between devices: 29.1 us -> 28.3 us
    all_to_all x1, starting transfers between devices: 8.77 us -> 7.47 us  [per_device(): swap(outer_send, 'grp', axis_index_groups=[list(GROUP_ORDER)])]
    all_to_all x1, waiting for transfers between devices: 3.12 us -> 4.42 us  [per_device(): swap(middle_send, ('blk', 'set'), axis_index_groups=middle_groups)]
where the time goes in v15:
time: 66.2 us; the launch traced here: 65.8 us
  starting transfers between devices  28.3 us (43%)
  blocking collectives  21.4 us (32%)
  Pallas kernels  9.08 us (14%)
  waiting for transfers between devices  6.98 us (11%)
    all_to_all x1, starting transfers between devices, per_device(): swap(middle_send, ('blk', 'set'), axis_index_groups=middle_groups)  18.7 us
    all_to_all x1, blocking collectives, per_device(): swap(combined, 'set', axis_index_groups=[[s ^ HOME_TURN for s in range(PE...  11.9 us
    all_to_all x1, blocking collectives, per_device(): near = swap(packed, 'set', axis_index_groups=near_groups)  9.51 us
    all_to_all x1, starting transfers between devices, per_device(): swap(outer_send, 'grp', axis_index_groups=[list(GROUP_ORDER)])  7.47 us
    all_to_all x1, waiting for transfers between devices, per_device(): swap(middle_send, ('blk', 'set'), axis_index_groups=middle_groups)  4.42 us
    pallas_call x1, Pallas kernels, per_device(): call(first_kernel, 'first', (shaped(PEERS * ROWS, 2 * HD, dtype=F32), sha...  3.04 us
    all_to_all x1, waiting for transfers between devices, per_device(): swap(outer_send, 'grp', axis_index_groups=[list(GROUP_ORDER)])  2.56 us
    ppermute x1, starting transfers between devices, per_device(): lax.ppermute(cross, 'set', [(i, (i + NEAR) % PEERS) for i in range(PEERS)])  2.13 us
  transfers between devices with their start and end apart: 3, of which 2 were waited for; matrix products, arithmetic and copies ran while one was open for 0% of the time, Pallas kernels for 8%

profile of v15, /device:TPU:1, one launch (start us, length us, event | category | flops | bytes accessed | tf_op | source)
XLA Modules:
  0.0 65.8 jit_solution(13272808687812407972)
XLA Ops:
  0.0 1.4 %pack.1 = bf16[4,384,128]{2,1,0:T(8,128)(2,1)S(1)} custom-call(bf16[128,384]{1,0:T(8,128)(2,1)} %query_hbm.1, bf16[128,384]{1,0:T(8,128)(2,1)} %key_hbm.1, bf16[128,384]{1,0:T(8,128)(2,1)} %value_hbm.1, s32[1,128]{1,0:T(1,128)} %bitcast.7), custom_call_target="tpu_custom_call" | custom-call | tf_op jit(solution)/shard_map/pack/pallas_call | solution.py:324
  1.4 0.0 copy-start.1
  1.4 9.5 %all_to_all.20.blocks_ref.near_ref = bf16[4,384,128]{2,1,0:T(8,128)(2,1)S(1)} all-to-all(bf16[4,384,128]{2,1,0:T(8,128)(2,1)S(1)} %pack.1), channel_id=1, replica_groups={{2,3,0,1},{6,7,4,5},{10,11,8,9},{14,15,12,13},{18,19,16,17},{22,23,20,2..., dimensions={0} | all-to-all | bytes 786432 | tf_op jit(solution)/shard_map/all_to_all | solution.py:332
  10.9 0.0 copy-done.1
  10.9 1.0 %pick_middle.1 = (bf16[16,64,128]{2,1,0:T(8,128)(2,1)}, bf16[4,192,128]{2,1,0:T(8,128)(2,1)S(1)}) custom-call(s32[2,6]{1,0:T(2,128)S(1)} %copy-done.1, bf16[4,384,128]{2,1,0:T(8,128)(2,1)S(1)} %all_to_all.20.blocks_ref.near_ref), custom_call_target="tpu_custom_call" | custom-call | tf_op jit(solution)/shard_map/pick_middle/pallas_call | solution.py:333
  11.9 18.7 %all-to-all-start.1 = ((bf16[16,64,128]{2,1,0:T(8,128)(2,1)}), bf16[16,64,128]{2,1,0:T(8,128)(2,1)S(1)}, u32[]{:S(2)}, u32[]{:S(2)}) async-start(bf16[16,64,128]{2,1,0:T(8,128)(2,1)} %get-tuple-element.15), calls=%async_computation.1 | async-start | bytes 524288 | tf_op jit(solution)/shard_map/all_to_all | solution.py:347
  30.6 2.1 %collective-permute-start = (bf16[4,192,128]{2,1,0:T(8,128)(2,1)S(1)}, bf16[4,192,128]{2,1,0:T(8,128)(2,1)S(1)}, u32[]{:S(2)}, u32[]{:S(2)}) collective-permute-start(bf16[4,192,128]{2,1,0:T(8,128)(2,1)S(1)} %get-tuple-element.12), channel_id=1, source_target_pairs={{0,4},{1,5},{2,6},{3,7},{4,0},{5,1},{6,2},{7,3},{8,12},{9,13},{10,... | collective-permute-start | bytes 589832 | tf_op jit(solution)/shard_map/ppermute | solution.py:349
  32.7 4.4 %all-to-all-done.1 = bf16[16,64,128]{2,1,0:T(8,128)(2,1)S(1)} async-done(((bf16[16,64,128]{2,1,0:T(8,128)(2,1)}), bf16[16,64,128]{2,1,0:T(8,128)(2,1)S(1)}, u32[]{:S(2)}, u32[]{:S(2)}) %all-to-all-start.1) | async-done | bytes 262176 | tf_op jit(solution)/shard_map/all_to_all | solution.py:347
  37.1 1.1 %pick_outer.1 = bf16[8,128,128]{2,1,0:T(8,128)(2,1)} custom-call(s32[2,6]{1,0:T(2,128)S(1)} %copy-done.1, bf16[8,128,128]{2,1,0:T(8,128)(2,1)S(1)} %bitcast.5), custom_call_target="tpu_custom_call" | custom-call | tf_op jit(solution)/shard_map/pick_outer/pallas_call | solution.py:364
  38.2 7.5 %all-to-all-start.2 = ((bf16[8,128,128]{2,1,0:T(8,128)(2,1)}), bf16[8,128,128]{2,1,0:T(8,128)(2,1)S(1)}, u32[]{:S(2)}, u32[]{:S(2)}) async-start(bf16[8,128,128]{2,1,0:T(8,128)(2,1)} %pick_outer.1), calls=%async_computation.2 | async-start | bytes 524288 | tf_op jit(solution)/shard_map/all_to_all | solution.py:372
  45.7 0.0 collective-permute-done.far_ref
  45.7 3.0 %first.1 = (f32[1024,128]{1,0:T(8,128)S(1)}, bf16[128,128]{1,0:T(8,128)(2,1)S(1)}, bf16[16,128]{1,0:T(8,128)(2,1)S(1)}) custom-call(s32[2,6]{1,0:T(2,128)S(1)} %copy-done.1, bf16[4,384,128]{2,1,0:T(8,128)(2,1)S(1)} %all_to_all.20.blocks_ref.near_ref, bf16[4,192,128]{2,1,0:T(8,128)(2,1)S(1)} %collective-permute-done.far_ref), custom_call_target="tpu_custom_call" | custom-call | flops 6000000000 | bytes 2000000 | tf_op jit(solution)/shard_map/first/pallas_call | solution.py:350
  48.7 0.9 %middle.1 = (bf16[8,64,128]{2,1,0:T(8,128)(2,1)S(1)}, f32[128,128]{1,0:T(8,128)S(1)}) custom-call(s32[2,6]{1,0:T(2,128)S(1)} %copy-done.1, f32[1024,128]{1,0:T(8,128)S(1)} %get-tuple-element.13.state_ref, bf16[128,128]{1,0:T(8,128)(2,1)S(1)} %get-tuple-element.14.query_ref, bf16[1024,128]{1,0:T(8,128)(2,1)S(1)} %bitcast.6), custom_call_target="tpu_custom_call" | custom-call | flops 2000000000 | bytes 2000000 | tf_op jit(solution)/shard_map/middle/pallas_call | solution.py:373
  49.7 0.0 copy-start
  49.7 2.6 %all-to-all-done.2 = bf16[8,128,128]{2,1,0:T(8,128)(2,1)S(1)} async-done(((bf16[8,128,128]{2,1,0:T(8,128)(2,1)}), bf16[8,128,128]{2,1,0:T(8,128)(2,1)S(1)}, u32[]{:S(2)}, u32[]{:S(2)}) %all-to-all-start.2) | async-done | bytes 262176 | tf_op jit(solution)/shard_map/all_to_all | solution.py:372
  52.3 0.7 %outer.1 = bf16[8,64,128]{2,1,0:T(8,128)(2,1)S(1)} custom-call(s32[2,6]{1,0:T(2,128)S(1)} %copy-done.1, f32[128,128]{1,0:T(8,128)S(1)} %get-tuple-element.16.merged_ref, bf16[16,128]{1,0:T(8,128)(2,1)S(1)} %get-tuple-element.17.query_ref, bf16[1024,128]{1,0:T(8,128)(2,1)S(1)} %bitcast.4, ...), custom_call_target="tpu_custom_call", output_to_operand_aliasing={{}: (4, {})} | custom-call | tf_op jit(solution)/shard_map/outer/pallas_call | solution.py:382
  52.9 11.9 %all_to_all.21.blocks_ref = bf16[8,64,128]{2,1,0:T(8,128)(2,1)S(1)} all-to-all(bf16[8,64,128]{2,1,0:T(8,128)(2,1)S(1)} %outer.1), channel_id=1, replica_groups={{7,6,5,4,3,2,1,0},{15,14,13,12,11,10,9,8},{23,22,21,20,19,18,17,16},{31..., dimensions={0} | all-to-all | bytes 262144 | tf_op jit(solution)/shard_map/all_to_all | solution.py:389
  64.8 0.0 copy-done
  64.8 1.0 %project.1 = bf16[128,768]{1,0:T(8,128)(2,1)} custom-call(bf16[8,64,128]{2,1,0:T(8,128)(2,1)S(1)} %all_to_all.21.blocks_ref, bf16[384,768]{1,0:T(8,128)(2,1)S(1)} %copy-done), custom_call_target="tpu_custom_call" | custom-call | tf_op jit(solution)/shard_map/project/pallas_call | solution.py:391
Async XLA Ops:
  1.4 9.5 %copy-start.1 = (s32[2,6]{1,0:T(2,128)S(1)}, s32[2,6]{1,0:T(2,128)}, u32[]{:S(2)}) copy-start(s32[2,6]{1,0:T(2,128)} %offsets_ref.9) | copy-start | bytes 148
  11.9 25.2 %all-to-all-start.1 = ((bf16[16,64,128]{2,1,0:T(8,128)(2,1)}), bf16[16,64,128]{2,1,0:T(8,128)(2,1)S(1)}, u32[]{:S(2)}, u32[]{:S(2)}) async-start(bf16[16,64,128]{2,1,0:T(8,128)(2,1)} %get-tuple-element.15), calls=%async_computation.1 | async-start | bytes 524288 | tf_op jit(solution)/shard_map/all_to_all | solution.py:347
  30.6 15.1 %collective-permute-start = (bf16[4,192,128]{2,1,0:T(8,128)(2,1)S(1)}, bf16[4,192,128]{2,1,0:T(8,128)(2,1)S(1)}, u32[]{:S(2)}, u32[]{:S(2)}) collective-permute-start(bf16[4,192,128]{2,1,0:T(8,128)(2,1)S(1)} %get-tuple-element.12), channel_id=1, source_target_pairs={{0,4},{1,5},{2,6},{3,7},{4,0},{5,1},{6,2},{7,3},{8,12},{9,13},{10,... | collective-permute-start | bytes 589832 | tf_op jit(solution)/shard_map/ppermute | solution.py:349
  38.2 14.0 %all-to-all-start.2 = ((bf16[8,128,128]{2,1,0:T(8,128)(2,1)}), bf16[8,128,128]{2,1,0:T(8,128)(2,1)S(1)}, u32[]{:S(2)}, u32[]{:S(2)}) async-start(bf16[8,128,128]{2,1,0:T(8,128)(2,1)} %pick_outer.1), calls=%async_computation.2 | async-start | bytes 524288 | tf_op jit(solution)/shard_map/all_to_all | solution.py:372
  49.7 15.1 %copy-start = (bf16[384,768]{1,0:T(8,128)(2,1)S(1)}, bf16[384,768]{1,0:T(8,128)(2,1)}, u32[]{:S(2)}) copy-start(bf16[384,768]{1,0:T(8,128)(2,1)} %weight_ref.1) | copy-start | bytes 1769476
